TPU v7x, 32 devices: a whole 2x2x4 slice. The times are simulated.
32 devices in a mesh: seq: 16 (over z, y, x), dp: 2 (over core).
Axes of the slice: x: 2, y: 2, z: 4, core: 2. Of those that a mesh axis runs over, the one named last changes fastest.
Arguments:
- tokens: bfloat16 [2, 64, 384, 256], P('dp', 'seq'), may hold values from -6 to 6
- column_rows: int32 [2, 384], P('dp', 'seq'), may hold values from 16 to 32, as said below
- cotangent: bfloat16 [2, 64, 384, 256], P('dp', 'seq'), may hold values from -6 to 6
- flat_params: bfloat16 [788736], P(('seq', 'dp')), as said below
Outputs:
- layer_out: bfloat16 [2, 64, 384, 256], P('dp', 'seq')
- input_grad: float32 [2, 64, 384, 256], P('dp', 'seq')
- param_grad: float32 [788736], P(('seq', 'dp'))
Inputs may be any that keep to these rules, and one draw needn't show every extreme that they name: `column_rows`: each aligned block of 96 grid columns of a group holds one value: 32 (images of 32 rows and 96 columns) or 32 / 2 (images of 16 rows, two stacked per 32 rows); every group has blocks of both values. `flat_params`: the entries of the two gain segments lie between 0.6 and 1.4.
All inputs are finite; a program needn't handle non-finite values.
Results may differ from a plain program's by a relative error of at most 0.012.
Values may be sent and summed in bfloat16 or wider, within the bound.
No kernel may reach another device: no remote copies, remote signals or barrier semaphores. Data moves between devices by JAX's collectives and lax.ppermute only.
A program may use at most 128 MiB of HBM per device.

v0:
```python
import jax
import jax.numpy as jnp
from jax import lax
from jax.sharding import PartitionSpec as P

D = 256
FF = 1024
HEADS = 2
TALL = 32


EPSILON = 1e-05


def unpack(flat_params, model_width, hidden_width):
    amounts = [
        model_width,
        model_width,
        model_width * 3 * model_width,
        model_width * model_width,
        model_width,
        model_width,
        model_width * hidden_width,
        hidden_width,
        hidden_width * model_width,
        model_width,
    ]
    pieces = []
    offset = 0
    for amount in amounts:
        pieces.append(flat_params[offset : offset + amount])
        offset = offset + amount
    return (
        pieces[0],
        pieces[1],
        pieces[2].reshape(model_width, 3 * model_width),
        pieces[3].reshape(model_width, model_width),
        pieces[4],
        pieces[5],
        pieces[6].reshape(model_width, hidden_width),
        pieces[7],
        pieces[8].reshape(hidden_width, model_width),
        pieces[9],
    )


def normalize(inputs, gain_vec, shift_vec):
    center = inputs - jnp.mean(inputs, axis=-1, keepdims=True)
    spread = jnp.mean(center * center, axis=-1, keepdims=True)
    return center * lax.rsqrt(spread + EPSILON) * gain_vec + shift_vec


def contract_rows(left, right):
    return lax.dot_general(
        left, right, (((0,), (0,)), ((), ())), preferred_element_type=jnp.float32
    )


def contract_last(left, right):
    return lax.dot_general(
        left, right, (((1,), (1,)), ((), ())), preferred_element_type=jnp.float32
    )


def allowed_pairs(column_span):
    later_rows = jnp.arange(TALL, dtype=jnp.int32)[None, :, None]
    earlier_rows = jnp.arange(TALL, dtype=jnp.int32)[None, None, :]
    span_wide = column_span[:, None, None]
    same_image = later_rows // span_wide == earlier_rows // span_wide
    return (later_rows >= earlier_rows) & same_image


def column_scores(packed, scale_factor):
    rows_all, grid_cols = (packed.shape[1], packed.shape[2])
    grouped = packed.reshape(rows_all // TALL, TALL, grid_cols, 3, HEADS, D // HEADS)
    queries = grouped[:, :, :, 0]
    key_rows = grouped[:, :, :, 1]
    values = grouped[:, :, :, 2]
    scores = (
        jnp.einsum("qichd,qjchd->qchij", queries, key_rows, preferred_element_type=jnp.float32)
        * scale_factor
    )
    return (scores, queries, key_rows, values)


def attend(packed, pair_mask, scale_factor):
    rows_all, grid_cols = (packed.shape[1], packed.shape[2])
    scores, queries, key_rows, values = column_scores(packed, scale_factor)
    masked = jnp.where(pair_mask, scores, -1e30)
    row_peak = jnp.max(masked, axis=-1, keepdims=True)
    exp_terms = jnp.where(pair_mask, jnp.exp(masked - row_peak), 0.0)
    row_total = jnp.sum(exp_terms, axis=-1, keepdims=True)
    probabilities = (exp_terms / row_total).astype(jnp.bfloat16)
    logsum = row_peak + jnp.log(row_total)
    result = jnp.einsum(
        "qchij,qjchd->qichd", probabilities, values, preferred_element_type=jnp.float32
    )
    return (result.astype(jnp.bfloat16).reshape(1, rows_all, grid_cols, D), logsum)


def attend_back(packed, pair_mask, logsum, grad_cols, scale_factor):
    rows_all, grid_cols = (packed.shape[1], packed.shape[2])
    scores, queries, key_rows, values = column_scores(packed, scale_factor)
    probs_wide = jnp.where(pair_mask, jnp.exp(scores - logsum), 0.0)
    grad_grouped = grad_cols.reshape(rows_all // TALL, TALL, grid_cols, HEADS, D // HEADS)
    grad_probs = jnp.einsum(
        "qichd,qjchd->qchij", grad_grouped, values, preferred_element_type=jnp.float32
    )
    grad_scores = probs_wide * (
        grad_probs - jnp.sum(probs_wide * grad_probs, axis=-1, keepdims=True)
    )
    grad_scores = grad_scores.astype(jnp.bfloat16)
    grad_queries = (
        jnp.einsum("qchij,qjchd->qichd", grad_scores, key_rows, preferred_element_type=jnp.float32)
        * scale_factor
    )
    grad_keys = (
        jnp.einsum("qchij,qichd->qjchd", grad_scores, queries, preferred_element_type=jnp.float32)
        * scale_factor
    )
    grad_values = jnp.einsum(
        "qchij,qichd->qjchd",
        probs_wide.astype(jnp.bfloat16),
        grad_grouped,
        preferred_element_type=jnp.float32,
    )
    stacked = jnp.stack([grad_queries, grad_keys, grad_values], axis=3).astype(jnp.bfloat16)
    return stacked.reshape(1, rows_all, grid_cols, 3 * D)


def local(tokens, column_rows, cotangent, flat_params):
    gathered = lax.all_gather(flat_params, ("seq", "dp"), axis=0, tiled=True)
    gain_one, shift_one, w_qkv, w_out, gain_two, shift_two, w_in, bias_in, w_back, bias_back = (
        unpack(gathered, D, FF)
    )
    local_rows, local_cols = (tokens.shape[1], tokens.shape[2])
    scale_factor = (D // HEADS) ** (-0.5)
    rows_flat = tokens.reshape(-1, D).astype(jnp.float32)
    normed, norm_one_back = jax.vjp(
        normalize, rows_flat, gain_one.astype(jnp.float32), shift_one.astype(jnp.float32)
    )
    normed_low = normed.astype(jnp.bfloat16)
    pair_mask = allowed_pairs(column_rows[0])[None, :, None]
    packed_rows = jnp.dot(normed_low, w_qkv, preferred_element_type=jnp.float32).astype(
        jnp.bfloat16
    )
    packed = lax.all_to_all(
        packed_rows.reshape(1, local_rows, local_cols, 3 * D),
        "seq",
        split_axis=2,
        concat_axis=1,
        tiled=True,
    )
    attended_cols, logsum = attend(packed, pair_mask, scale_factor)
    attended = lax.all_to_all(
        attended_cols, "seq", split_axis=1, concat_axis=2, tiled=True
    ).reshape(-1, D)
    branch = jnp.dot(attended, w_out, preferred_element_type=jnp.float32)
    middle = rows_flat + branch
    normed_two, norm_two_back = jax.vjp(
        normalize, middle, gain_two.astype(jnp.float32), shift_two.astype(jnp.float32)
    )
    normed_two_low = normed_two.astype(jnp.bfloat16)
    inner = jnp.dot(normed_two_low, w_in, preferred_element_type=jnp.float32) + bias_in.astype(
        jnp.float32
    )
    activated, gelu_back = jax.vjp(jax.nn.gelu, inner)
    activated_low = activated.astype(jnp.bfloat16)
    second = jnp.dot(activated_low, w_back, preferred_element_type=jnp.float32) + bias_back.astype(
        jnp.float32
    )
    layer_out = (middle + second).astype(jnp.bfloat16).reshape(tokens.shape)
    grad_output = cotangent.reshape(-1, D).astype(jnp.float32)
    grad_second = grad_output.astype(jnp.bfloat16)
    grad_w_back = contract_rows(activated_low, grad_second)
    grad_bias_back = jnp.sum(grad_second.astype(jnp.float32), axis=0)
    grad_activated = contract_last(grad_second, w_back)
    grad_inner = gelu_back(grad_activated)[0].astype(jnp.bfloat16)
    grad_w_in = contract_rows(normed_two_low, grad_inner)
    grad_bias_in = jnp.sum(grad_inner.astype(jnp.float32), axis=0)
    grad_normed_two = contract_last(grad_inner, w_in)
    grad_middle_norm, grad_gain_two, grad_shift_two = norm_two_back(grad_normed_two)
    grad_middle = grad_output + grad_middle_norm
    grad_branch = grad_middle.astype(jnp.bfloat16)
    grad_w_out = contract_rows(attended, grad_branch)
    grad_attended = (
        contract_last(grad_branch, w_out).astype(jnp.bfloat16).reshape(1, local_rows, local_cols, D)
    )
    grad_att_cols = lax.all_to_all(grad_attended, "seq", split_axis=2, concat_axis=1, tiled=True)
    grad_packed = attend_back(packed, pair_mask, logsum, grad_att_cols, scale_factor)
    grad_rows = lax.all_to_all(grad_packed, "seq", split_axis=1, concat_axis=2, tiled=True).reshape(
        -1, 3 * D
    )
    grad_w_qkv = contract_rows(normed_low, grad_rows)
    grad_normed = contract_last(grad_rows, w_qkv)
    grad_input_norm, grad_gain_one, grad_shift_one = norm_one_back(grad_normed)
    input_grad = (grad_middle + grad_input_norm).reshape(tokens.shape)
    flat_grad = jnp.concatenate(
        [
            grad_gain_one,
            grad_shift_one,
            grad_w_qkv.reshape(-1),
            grad_w_out.reshape(-1),
            grad_gain_two,
            grad_shift_two,
            grad_w_in.reshape(-1),
            grad_bias_in,
            grad_w_back.reshape(-1),
            grad_bias_back,
        ]
    )
    param_grad = lax.psum_scatter(flat_grad, ("seq", "dp"), scatter_dimension=0, tiled=True)
    return (layer_out, input_grad, param_grad)


def solution(mesh):
    placed = (
        P("dp", "seq", None, None),
        P("dp", "seq"),
        P("dp", "seq", None, None),
        P(("seq", "dp")),
    )
    return jax.shard_map(
        local,
        mesh=mesh,
        in_specs=placed,
        out_specs=(P("dp", "seq", None, None), P("dp", "seq", None, None), P(("seq", "dp"))),
        check_vma=False,
    )
```

profile of v0, /device:TPU:0, one launch (start us, length us, event | category | flops | bytes accessed | tf_op | source)
XLA Modules:
  0.0 530.8 jit_solution(10192410891543049322)
XLA Ops:
  11.1 136.4 %all-reduce.5.cloned.1.call-done = bf16[788736]{0:T(1024)(128)(2,1)} async-done(((bf16[788736]{0:T(1024)(128)(2,1)}), bf16[788736]{0:T(1024)(128)(2,1)}) %all-reduce.5.cloned.1.call-update) | async-done | bytes 1577488
  151.8 3.2 copy.54
  155.0 5.7 %all-to-all-start = ((bf16[1,4,384,768]{3,1,0,2:T(4,128)(2,1)}), bf16[1,4,384,768]{3,1,0,2:T(4,128)(2,1)S(1)}, u32[]{:S(2)}, u32[]{:S(2)}) async-start(bf16[1,4,384,768]{3,1,0,2:T(4,128)(2,1)} %copy.54), calls=%async_computation | async-start | bytes 4718592 | tf_op jit(solution)/shard_map/all_to_all | solution.py:147
  161.2 46.3 %all-to-all-done = bf16[1,4,384,768]{3,1,0,2:T(4,128)(2,1)S(1)} async-done(((bf16[1,4,384,768]{3,1,0,2:T(4,128)(2,1)}), bf16[1,4,384,768]{3,1,0,2:T(4,128)(2,1)S(1)}, u32[]{:S(2)}, u32[]{:S(2)}) %all-to-all-start) | async-done | bytes 2359328 | tf_op jit(solution)/shard_map/all_to_all | solution.py:147
  209.5 4.6 reshape.443
  220.3 10.8 %all-to-all-start.1 = ((bf16[1,64,24,256]{3,2,0,1:T(8,128)(2,1)}), bf16[1,64,24,256]{3,2,0,1:T(8,128)(2,1)S(1)}, u32[]{:S(2)}, u32[]{:S(2)}) async-start(bf16[1,64,24,256]{3,2,0,1:T(8,128)(2,1)} %bitcast.135), calls=%async_computation.1 | async-start | bytes 1572864 | tf_op jit(solution)/shard_map/all_to_all | solution.py:155
  231.1 2.2 fusion.42
  234.4 2.1 reshape.446
  236.4 2.0 slice.75
  239.2 10.9 %all-to-all-done.1 = bf16[1,64,24,256]{3,2,0,1:T(8,128)(2,1)S(1)} async-done(((bf16[1,64,24,256]{3,2,0,1:T(8,128)(2,1)}), bf16[1,64,24,256]{3,2,0,1:T(8,128)(2,1)S(1)}, u32[]{:S(2)}, u32[]{:S(2)}) %all-to-all-start.1) | async-done | bytes 786464 | tf_op jit(solution)/shard_map/all_to_all | solution.py:155
  252.5 4.2 multiply_convert_fusion
  256.7 5.2 convert_reduce_fusion
  268.4 4.9 all-to-all-start.2
  273.4 18.6 %all-to-all-done.2 = bf16[1,4,384,256]{3,1,0,2:T(4,128)(2,1)S(1)} async-done(((bf16[1,4,384,256]{3,1,0,2:T(4,128)(2,1)}), bf16[1,4,384,256]{3,1,0,2:T(4,128)(2,1)S(1)}, u32[]{:S(2)}, u32[]{:S(2)}) %all-to-all-start.2) | async-done | bytes 786464 | tf_op jit(solution)/shard_map/all_to_all | solution.py:189
  302.3 2.5 convert_element_type.119
  304.8 5.1 all-to-all-start.3
  310.5 3.5 convolution_bitcast_fusion.1
  318.9 37.7 %all-to-all-done.3 = bf16[1,64,24,768]{3,2,0,1:T(8,128)(2,1)} async-done(((bf16[1,64,24,768]{3,2,0,1:T(8,128)(2,1)}), bf16[1,64,24,768]{3,2,0,1:T(8,128)(2,1)}, u32[]{:S(2)}, u32[]{:S(2)}) %all-to-all-start.3) | async-done | bytes 2359328 | tf_op jit(solution)/shard_map/all_to_all | solution.py:191
  362.2 2.1 reshape.453
  364.3 2.5 multiply_reduce_fusion.1
  369.5 2.1 constant_dynamic-update-slice_fusion.7
  380.0 4.0 fusion.11
  384.0 2.2 add_add_fusion.2
  386.2 136.1 %all-reduce.7.cloned.1.call-done = f32[788736]{0:T(1024)} async-done(((f32[788736]{0:T(1024)}), f32[788736]{0:T(1024)}) %all-reduce.7.cloned.1.call-update) | async-done | bytes 3154960
  (160 shorter events, 60.9 us)
Async XLA Ops:
  7.2 140.4 %all-reduce.5.cloned.1.call-start = ((), (), s32[]{:S(2)}) async-start(), calls=%async_computation.4 | async-start | bytes 3158016
  7.2 2.5 copy-start
  10.0 140.8 %copy-start.29 = (f32[4,384]{1,0:T(4,128)}, f32[4,384]{1,0:T(4,128)S(1)}, u32[]{:S(2)}) copy-start(f32[4,384]{1,0:T(4,128)S(1)} %broadcast_multiply_fusion.1) | copy-start | bytes 18436
  149.0 2.6 copy-start.23
  155.0 5.7 %copy-start.38 = (s32[1,24]{1,0:T(1,128)S(1)}, s32[1,24]{1,0:T(1,128)}, u32[]{:S(2)}) copy-start(s32[1,24]{1,0:T(1,128)} %param.5) | copy-start | bytes 292
  155.0 52.5 %all-to-all-start = ((bf16[1,4,384,768]{3,1,0,2:T(4,128)(2,1)}), bf16[1,4,384,768]{3,1,0,2:T(4,128)(2,1)S(1)}, u32[]{:S(2)}, u32[]{:S(2)}) async-start(bf16[1,4,384,768]{3,1,0,2:T(4,128)(2,1)} %copy.54), calls=%async_computation | async-start | bytes 4718592 | tf_op jit(solution)/shard_map/all_to_all | solution.py:147
  220.3 29.8 %all-to-all-start.1 = ((bf16[1,64,24,256]{3,2,0,1:T(8,128)(2,1)}), bf16[1,64,24,256]{3,2,0,1:T(8,128)(2,1)S(1)}, u32[]{:S(2)}, u32[]{:S(2)}) async-start(bf16[1,64,24,256]{3,2,0,1:T(8,128)(2,1)} %bitcast.135), calls=%async_computation.1 | async-start | bytes 1572864 | tf_op jit(solution)/shard_map/all_to_all | solution.py:155
  251.0 12.6 %copy-start.1 = (f32[1536,256]{1,0:T(8,128)}, f32[1536,256]{1,0:T(8,128)S(1)}, u32[]{:S(2)}) copy-start(f32[1536,256]{1,0:T(8,128)S(1)} %get-tuple-element.29) | copy-start | bytes 4718596
  252.4 4.3 copy-start.5
  252.4 4.3 copy-start.25
  266.9 6.4 %copy-start.28 = (f32[2,24,2,32]{3,2,1,0:T(2,128)S(1)}, f32[2,24,2,32]{3,2,1,0:T(2,128)}, u32[]{:S(2)}) copy-start(f32[2,24,2,32]{3,2,1,0:T(2,128)} %copy-done.27) | copy-start | bytes 36868
  268.4 23.5 %all-to-all-start.2 = ((bf16[1,4,384,256]{3,1,0,2:T(4,128)(2,1)}), bf16[1,4,384,256]{3,1,0,2:T(4,128)(2,1)S(1)}, u32[]{:S(2)}, u32[]{:S(2)}) async-start(bf16[1,4,384,256]{3,1,0,2:T(4,128)(2,1)} %copy.65), calls=%async_computation.2 | async-start | bytes 1572864 | tf_op jit(solution)/shard_map/all_to_all | solution.py:189
  304.8 5.4 %copy-start.30 = (f32[4,384]{1,0:T(4,128)S(1)}, f32[4,384]{1,0:T(4,128)}, u32[]{:S(2)}) copy-start(f32[4,384]{1,0:T(4,128)} %copy-done.29) | copy-start | bytes 18436
  304.8 5.4 %copy-start.32 = (f32[4,384]{1,0:T(4,128)S(1)}, f32[4,384]{1,0:T(4,128)}, u32[]{:S(2)}) copy-start(f32[4,384]{1,0:T(4,128)} %get-tuple-element.24) | copy-start | bytes 18436
  304.8 5.5 %copy-start.6 = (bf16[1,4,384,256]{3,2,1,0:T(8,128)(2,1)S(1)}, bf16[1,4,384,256]{3,2,1,0:T(8,128)(2,1)}, u32[]{:S(2)}) copy-start(bf16[1,4,384,256]{3,2,1,0:T(8,128)(2,1)} %param.6) | copy-start | bytes 2359300
  304.8 5.7 %copy-start.2 = (f32[1536,256]{1,0:T(8,128)S(1)}, f32[1536,256]{1,0:T(8,128)}, u32[]{:S(2)}) copy-start(f32[1536,256]{1,0:T(8,128)} %copy-done.1) | copy-start | bytes 4718596
  304.8 51.7 %all-to-all-start.3 = ((bf16[1,64,24,768]{3,2,0,1:T(8,128)(2,1)}), bf16[1,64,24,768]{3,2,0,1:T(8,128)(2,1)}, u32[]{:S(2)}, u32[]{:S(2)}) async-start(bf16[1,64,24,768]{3,2,0,1:T(8,128)(2,1)} %bitcast.125), calls=%async_computation.3 | async-start | bytes 4718592 | tf_op jit(solution)/shard_map/all_to_all | solution.py:191
  309.9 212.4 %all-reduce.7.cloned.1.call-start = ((), (), s32[]{:S(2)}) async-start(), calls=%async_computation.5 | async-start | bytes 6316032
  310.5 5.8 %copy-start.40 = (bf16[1536,1024]{1,0:T(8,128)(2,1)S(1)}, bf16[1536,1024]{1,0:T(8,128)(2,1)}, u32[]{:S(2)}) copy-start(bf16[1536,1024]{1,0:T(8,128)(2,1)} %get-tuple-element.30) | copy-start | bytes 9437188
  364.3 5.2 copy-start.18
  366.8 9.2 %copy-start.9 = (f32[32,8,8,128]{3,1,2,0:T(8,128)S(1)}, f32[32,8,8,128]{3,1,2,0:T(8,128)}, u32[]{:S(2)}) copy-start(f32[32,8,8,128]{3,1,2,0:T(8,128)} %copy.81) | copy-start | bytes 3145732
  371.6 6.0 %copy-start.10 = (f32[128,2,8,128]{3,1,2,0:T(2,128)S(1)}, f32[128,2,8,128]{3,1,2,0:T(2,128)}, u32[]{:S(2)}) copy-start(f32[128,2,8,128]{3,1,2,0:T(2,128)} %copy.82) | copy-start | bytes 3145732
  379.9 4.0 copy-start.4
  379.9 4.0 copy-start.8
  (23 other events, 28.7 us)
Sparse Core Ops, SparseCore 0:
  13.4 134.1 all-reduce.4
  379.4 142.8 all-reduce.6
where the time goes:
time: 532 us; the launch traced here: 531 us
  waiting for transfers between devices  386 us (73%)
  local copies, waits for them, and re-layouts  60.4 us (11%)
  matrix products  29.9 us (6%)
  starting transfers between devices  26.8 us (5%)
  between operations  14.7 us (3%)
  other arithmetic  12.7 us (2%)
    unnamed x4, waiting for transfers between devices  273 us
    all_to_all x1, waiting for transfers between devices, local(): lax.all_to_all(packed_rows.reshape(1, local_rows, local_cols, 3 * D), 'se...  46.3 us
    all_to_all x1, waiting for transfers between devices, local(): lax.all_to_all(grad_packed, 'seq', split_axis=1, concat_axis=2, tiled=True)  37.7 us
    unnamed x97, local copies, waits for them, and re-layouts  24.6 us
    all_to_all x1, waiting for transfers between devices, local(): lax.all_to_all(grad_attended, 'seq', split_axis=2, concat_axis=1, tiled=T...  18.6 us
    all_to_all x1, waiting for transfers between devices, local(): lax.all_to_all(attended_cols, 'seq', split_axis=1, concat_axis=2, tiled=T...  10.9 us
    all_to_all x1, starting transfers between devices, local(): lax.all_to_all(attended_cols, 'seq', split_axis=1, concat_axis=2, tiled=T...  10.8 us
  transfers between devices with their start and end apart: 6, of which 6 were waited for; matrix products, arithmetic and copies ran while one was open for 5% of the time, Pallas kernels for 0%

commit v1 on v0

v1 whole, which is shorter than its diff:
```python
import jax
import jax.numpy as jnp
from jax import lax
from jax.experimental import pallas as pl
from jax.experimental.pallas import tpu as pltpu
from jax.sharding import PartitionSpec as P

D = 256
FF = 1024
HEADS = 2
HEAD = D // HEADS
TALL = 32
STRIDE = 96
EPSILON = 1e-05
LANES = 128
PLANE = 4
CORES = 2
BLOCK = 16
HALF = 8
TOKENS = TALL * BLOCK
TILE = TALL * HALF
VMEM_BYTES = 50 * 1024 * 1024

ROW_GAIN_ONE = 0
ROW_SHIFT_ONE = 2
ROW_QKV = 4
ROW_OUT = ROW_QKV + 6 * D
ROW_GAIN_TWO = ROW_OUT + 2 * D
ROW_SHIFT_TWO = ROW_GAIN_TWO + 2
ROW_IN = ROW_SHIFT_TWO + 2
ROW_BIAS_IN = ROW_IN + 8 * D
ROW_BACK = ROW_BIAS_IN + 8
ROW_BIAS_BACK = ROW_BACK + 2 * FF
ROWS = ROW_BIAS_BACK + 2

F32 = jnp.float32
BF16 = jnp.bfloat16


def nn(left, right):
    return lax.dot_general(left, right, (((1,), (0,)), ((), ())), preferred_element_type=F32)


def nt(left, right):
    return lax.dot_general(left, right, (((1,), (1,)), ((), ())), preferred_element_type=F32)


def tn(left, right):
    return lax.dot_general(left, right, (((0,), (0,)), ((), ())), preferred_element_type=F32)


def to_tokens(block):
    width = block.shape[-1]
    return jnp.concatenate(
        [block[:, :HALF].reshape(TILE, width), block[:, HALF:].reshape(TILE, width)], axis=0
    )


def from_tokens(flat):
    width = flat.shape[-1]
    return jnp.concatenate(
        [flat[:TILE].reshape(TALL, HALF, width), flat[TILE:].reshape(TALL, HALF, width)], axis=1
    )


def center(value):
    offset = value - jnp.mean(value, axis=-1, keepdims=True)
    inverse = lax.rsqrt(jnp.mean(offset * offset, axis=-1, keepdims=True) + EPSILON)
    return offset * inverse, inverse


def center_back(grad_hat, hat, inverse):
    mean_one = jnp.mean(grad_hat, axis=-1, keepdims=True)
    mean_two = jnp.mean(grad_hat * hat, axis=-1, keepdims=True)
    return inverse * (grad_hat - mean_one - hat * mean_two)


def allowed(span):
    key = lax.broadcasted_iota(jnp.int32, (TILE, TILE), 0)
    query = lax.broadcasted_iota(jnp.int32, (TILE, TILE), 1)
    same_column = (key % HALF) == (query % HALF)
    half_tile = TILE // 2
    same_image = (key // half_tile == query // half_tile) | (span >= TALL)
    return same_column & (key <= query) & same_image


class Plan:
    def __init__(self, seq, shard):
        self.shard = shard
        self.deep = seq // PLANE
        self.count = seq * CORES
        self.pairwise = self.deep == 4
        rows = (shard + LANES - 2) // LANES + 1
        self.rows = -(-rows // 16) * 16
        self.lead = -(-(ROW_OUT * LANES) // (PLANE * CORES * shard))

    def first_row(self, device):
        return self.shard * device // LANES


def prepare(plan):
    def kernel(place_ref, *refs):
        sources, rest = refs[: CORES * PLANE], refs[CORES * PLANE :]
        w_qkv, w_out, w_in, w_back, vectors, bias_in, held, flat, sems = rest
        deep_at, plane_at, core_at = place_ref[0], place_ref[1], place_ref[2]
        copies = []
        for core in range(CORES):
            for plane in range(PLANE):
                source = sources[core * PLANE + plane]
                for deep in range(plan.deep):
                    slot = deep ^ deep_at if plan.pairwise else deep
                    copies.append(
                        pltpu.make_async_copy(
                            source.at[deep],
                            held.at[slot, plane ^ plane_at, core ^ core_at],
                            sems.at[len(copies)],
                        )
                    )
        for copy in copies:
            copy.start()
        for copy in copies:
            copy.wait()
        for device in range(plan.count):
            row = plan.first_row(device)
            value = held[device // 8, device // 2 % PLANE, device % CORES].astype(F32)
            if plan.shard * device % LANES:
                before = flat[row : row + 1]
                flat[row : row + plan.rows] = value
                flat[row : row + 1] = flat[row : row + 1] + before
            else:
                flat[row : row + plan.rows] = value
        for ref, row, wide in (
            (w_qkv, ROW_QKV, 6),
            (w_out, ROW_OUT, 2),
            (w_in, ROW_IN, 8),
            (w_back, ROW_BACK, 2),
        ):
            for part in range(wide):
                ref[:, part * LANES : (part + 1) * LANES] = flat[
                    pl.ds(row + part, ref.shape[0], stride=wide)
                ].astype(BF16)
        for index, row in enumerate(
            (ROW_GAIN_ONE, ROW_SHIFT_ONE, ROW_GAIN_TWO, ROW_SHIFT_TWO, ROW_BIAS_BACK)
        ):
            for part in range(2):
                vectors[index : index + 1, part * LANES : (part + 1) * LANES] = flat[
                    row + part : row + part + 1
                ]
        for part in range(8):
            bias_in[0:1, part * LANES : (part + 1) * LANES] = flat[
                ROW_BIAS_IN + part : ROW_BIAS_IN + part + 1
            ]

    shapes = [((D, 3 * D), BF16), ((D, D), BF16), ((D, FF), BF16), ((FF, D), BF16)]
    shapes += [((8, D), F32), ((8, FF), F32)]
    return pl.pallas_call(
        kernel,
        out_shape=[jax.ShapeDtypeStruct(shape, kind) for shape, kind in shapes],
        in_specs=[pl.BlockSpec(memory_space=pltpu.SMEM)]
        + [pl.BlockSpec(memory_space=pl.ANY)] * (CORES * PLANE),
        out_specs=[pl.BlockSpec(memory_space=pltpu.VMEM)] * len(shapes),
        scratch_shapes=[
            pltpu.VMEM((plan.deep, PLANE, CORES, plan.rows, LANES), BF16),
            pltpu.VMEM((ROWS + plan.rows + 8, LANES), F32),
            pltpu.SemaphoreType.DMA((plan.count,)),
        ],
        compiler_params=pltpu.CompilerParams(vmem_limit_bytes=VMEM_BYTES),
        name="prepare",
    )


def forward_kernel(
    span_ref, x_ref, w_qkv, w_out, vectors, packed_ref, attended_ref, middle_ref, logsum_ref
):
    x = to_tokens(x_ref[...].astype(F32))
    hat, _ = center(x)
    normed = (hat * vectors[0:1] + vectors[1:2]).astype(BF16)
    packed = nn(normed, w_qkv[...]).astype(BF16)
    packed_ref[...] = packed
    mask = allowed(span_ref[0, 0])
    scale = HEAD**-0.5
    tiles = []
    for half in range(2):
        rows = packed[half * TILE : (half + 1) * TILE]
        heads = []
        for head in range(HEADS):
            query = rows[:, head * HEAD : (head + 1) * HEAD]
            key = rows[:, D + head * HEAD : D + (head + 1) * HEAD]
            value = rows[:, 2 * D + head * HEAD : 2 * D + (head + 1) * HEAD]
            scores = jnp.where(mask, nt(key, query) * scale, -1e30)
            peak = jnp.max(scores, axis=0, keepdims=True)
            terms = jnp.exp(scores - peak)
            total = jnp.sum(terms, axis=0, keepdims=True)
            probs = (terms * (1.0 / total)).astype(BF16)
            heads.append(tn(probs, value).astype(BF16))
            slot = half * HEADS + head
            logsum_ref[0, slot : slot + 1] = peak + jnp.log(total)
        tiles.append(jnp.concatenate(heads, axis=1))
    attended = jnp.concatenate(tiles, axis=0)
    attended_ref[...] = attended
    middle_ref[...] = x + nn(attended, w_out[...])


def flatten(flat, base, matrix, row, wide):
    for part in range(wide):
        flat[pl.ds(row - base + part, matrix.shape[0], stride=wide)] = matrix[
            :, part * LANES : (part + 1) * LANES
        ]


def feed_kernel(plan):
    base = ROW_OUT - 4

    def kernel(
        place_ref,
        middle_ref,
        attended_ref,
        cot_ref,
        w_out,
        w_in,
        w_back,
        vectors,
        bias_in,
        out_ref,
        grad_att_ref,
        grad_mid_ref,
        parts_ref,
        first_ref,
        acc_in,
        acc_back,
        acc_out,
        acc_vec,
        acc_bias,
        flat,
    ):
        step = pl.program_id(0)

        @pl.when(step == 0)
        def _():
            for ref in (acc_in, acc_back, acc_out, acc_vec, acc_bias):
                ref[...] = jnp.zeros_like(ref)

        middle = middle_ref[...]
        hat, inverse = center(middle)
        normed = (hat * vectors[2:3] + vectors[3:4]).astype(BF16)
        cot_wide = to_tokens(cot_ref[...].astype(F32))
        cot = cot_wide.astype(BF16)
        out = middle + vectors[4:5]
        grad_normed = jnp.zeros((TOKENS, D), F32)
        rate = (2.0 / jnp.pi) ** 0.5
        for part in range(FF // D):
            cut = slice(part * D, (part + 1) * D)
            inner = nn(normed, w_in[:, cut]) + bias_in[0:1, cut]
            square = inner * inner
            bend = jnp.tanh(inner * (rate + (rate * 0.044715) * square))
            half = 0.5 * inner
            activated = (half + half * bend).astype(BF16)
            slope = (0.5 + 0.5 * bend) + half * (1.0 - bend * bend) * (
                rate + (3.0 * rate * 0.044715) * square
            )
            grad_inner_wide = nt(cot, w_back[cut, :]) * slope
            grad_inner = grad_inner_wide.astype(BF16)
            acc_bias[0:1, cut] += jnp.sum(grad_inner.astype(F32), axis=0, keepdims=True)
            out = out + nn(activated, w_back[cut, :])
            grad_normed = grad_normed + nt(grad_inner, w_in[:, cut])
            acc_back[:, cut] += tn(cot, activated)
            acc_in[:, cut] += tn(normed, grad_inner)
        out_ref[...] = from_tokens(out).astype(BF16)
        acc_vec[0:1] += jnp.sum(grad_normed * hat, axis=0, keepdims=True)
        acc_vec[1:2] += jnp.sum(grad_normed, axis=0, keepdims=True)
        acc_vec[2:3] += jnp.sum(cot_wide, axis=0, keepdims=True)
        grad_mid = cot_wide + center_back(grad_normed * vectors[2:3], hat, inverse)
        grad_mid_ref[...] = grad_mid
        grad_branch = grad_mid.astype(BF16)
        acc_out[...] += tn(attended_ref[...], grad_branch)
        grad_att_ref[...] = nt(grad_branch, w_out[...]).astype(BF16)

        @pl.when(step == pl.num_programs(0) - 1)
        def _():
            flatten(flat, base, acc_out[...], ROW_OUT, 2)
            flatten(flat, base, acc_in[...], ROW_IN, 8)
            flatten(flat, base, acc_back[...].T, ROW_BACK, 2)
            for index, row in ((0, ROW_GAIN_TWO), (1, ROW_SHIFT_TWO), (2, ROW_BIAS_BACK)):
                for part in range(2):
                    flat[row - base + part : row - base + part + 1] = acc_vec[
                        index : index + 1, part * LANES : (part + 1) * LANES
                    ]
            for part in range(8):
                flat[ROW_BIAS_IN - base + part : ROW_BIAS_IN - base + part + 1] = acc_bias[
                    0:1, part * LANES : (part + 1) * LANES
                ]
            first_ref[...] = flat[ROW_OUT - base : ROW_OUT - base + 8]
            send_rows(plan, place_ref, flat, base, parts_ref, plan.lead, plan.deep)

    return kernel


def send_rows(plan, place_ref, flat, base, parts_ref, low, high):
    plane_at, core_at = place_ref[1], place_ref[2]
    for device in range(low * PLANE * CORES, high * PLANE * CORES):
        row = plan.first_row(device) - base
        parts_ref[
            (device % CORES) ^ core_at, (device // CORES % PLANE) ^ plane_at, device // 8 - low
        ] = flat[row : row + plan.rows].astype(BF16)


def back_kernel(plan):
    def kernel(
        place_ref,
        span_ref,
        x_ref,
        packed_ref,
        logsum_ref,
        grad_att_ref,
        grad_mid_ref,
        first_ref,
        w_qkv,
        vectors,
        grad_x_ref,
        parts_ref,
        acc_qkv,
        acc_vec,
        flat,
    ):
        step = pl.program_id(0)

        @pl.when(step == 0)
        def _():
            for ref in (acc_qkv, acc_vec):
                ref[...] = jnp.zeros_like(ref)

        mask = allowed(span_ref[0, 0])
        scale = HEAD**-0.5
        tiles = []
        for half in range(2):
            rows = packed_ref[half * TILE : (half + 1) * TILE]
            grads = grad_att_ref[half * TILE : (half + 1) * TILE]
            pieces = [[], [], []]
            for head in range(HEADS):
                query = rows[:, head * HEAD : (head + 1) * HEAD]
                key = rows[:, D + head * HEAD : D + (head + 1) * HEAD]
                value = rows[:, 2 * D + head * HEAD : 2 * D + (head + 1) * HEAD]
                grad = grads[:, head * HEAD : (head + 1) * HEAD]
                slot = half * HEADS + head
                scores = nt(key, query) * scale - logsum_ref[0, slot : slot + 1]
                probs = jnp.exp(jnp.where(mask, scores, -1e30))
                grad_probs = nt(value, grad)
                weighted = probs * grad_probs
                total = jnp.sum(weighted, axis=0, keepdims=True)
                grad_scores = (weighted - probs * total).astype(BF16)
                pieces[0].append((tn(grad_scores, key) * scale).astype(BF16))
                pieces[1].append((nn(grad_scores, query) * scale).astype(BF16))
                pieces[2].append(nn(probs.astype(BF16), grad).astype(BF16))
            tiles.append(jnp.concatenate(pieces[0] + pieces[1] + pieces[2], axis=1))
        grad_packed = jnp.concatenate(tiles, axis=0)
        hat, inverse = center(to_tokens(x_ref[...].astype(F32)))
        normed = (hat * vectors[0:1] + vectors[1:2]).astype(BF16)
        acc_qkv[...] += tn(normed, grad_packed)
        grad_normed = nt(grad_packed, w_qkv[...])
        acc_vec[0:1] += jnp.sum(grad_normed * hat, axis=0, keepdims=True)
        acc_vec[1:2] += jnp.sum(grad_normed, axis=0, keepdims=True)
        grad_x = grad_mid_ref[...] + center_back(grad_normed * vectors[0:1], hat, inverse)
        grad_x_ref[...] = from_tokens(grad_x).astype(BF16)

        @pl.when(step == pl.num_programs(0) - 1)
        def _():
            flatten(flat, 0, acc_qkv[...], ROW_QKV, 6)
            for index, row in ((0, ROW_GAIN_ONE), (1, ROW_SHIFT_ONE)):
                for part in range(2):
                    flat[row + part : row + part + 1] = acc_vec[
                        index : index + 1, part * LANES : (part + 1) * LANES
                    ]
            flat[ROW_OUT : ROW_OUT + 8] = first_ref[...]
            send_rows(plan, place_ref, flat, 0, parts_ref, 0, plan.lead)

    return kernel


def whole(shape):
    return pl.BlockSpec(shape, lambda step: (0,) * len(shape))


def local(mesh_shape, tokens, column_rows, cotangent, flat_params):
    seq = mesh_shape["seq"]
    local_rows, columns = tokens.shape[1], tokens.shape[2]
    group = TALL // local_rows
    owned = columns // group
    steps = owned // BLOCK
    plan = Plan(seq, flat_params.shape[0])
    seq_at = lax.axis_index("seq")
    core_at = lax.axis_index("dp")
    deep_at, plane_at = seq_at // PLANE, seq_at % PLANE
    place = jnp.stack([deep_at, plane_at, core_at]).astype(jnp.int32)
    shift = plan.shard * (seq_at * CORES + core_at) % LANES
    smem = pl.BlockSpec(memory_space=pltpu.SMEM)
    params = pltpu.CompilerParams(
        vmem_limit_bytes=VMEM_BYTES, dimension_semantics=("arbitrary",)
    )

    groups = [[group * g + i for i in range(group)] for g in range(seq // group)]
    deep_groups = [[PLANE * z + q for z in range(plan.deep)] for q in range(PLANE)]

    def to_columns(rows):
        cut = rows.reshape(local_rows, group, owned, D).transpose(1, 0, 2, 3)
        moved = lax.all_to_all(cut, "seq", 0, 0, axis_index_groups=groups, tiled=True)
        return moved.reshape(TALL, owned, D)

    def to_rows(cols):
        moved = lax.all_to_all(
            cols.reshape(group, local_rows, owned, D),
            "seq",
            0,
            0,
            axis_index_groups=groups,
            tiled=True,
        )
        return moved.transpose(1, 0, 2, 3).reshape(tokens.shape)

    def swap_seq(value, distance):
        return lax.ppermute(value, "seq", [(i, i ^ distance) for i in range(seq)])

    def swap_core(value):
        return lax.ppermute(value, "dp", [(0, 1), (1, 0)])

    per_block = STRIDE // owned
    holders = seq * STRIDE // columns
    routes = []
    for target in range(seq):
        index, place_in = target // group, target % group
        source = place_in // per_block * holders + index * per_block + place_in % per_block
        routes.append((source, target))
    span = lax.ppermute(column_rows[:1, :1], "seq", routes)

    own = lax.dynamic_update_slice(
        jnp.zeros((plan.rows * LANES,), BF16), flat_params, (shift,)
    ).reshape(plan.rows, LANES)
    if plan.pairwise:
        deep = jnp.stack([own] + [swap_seq(own, PLANE * k) for k in range(1, plan.deep)])
    else:
        deep = lax.all_gather(own, "seq", axis=0, axis_index_groups=deep_groups)
    plane = [deep] + [swap_seq(deep, k) for k in range(1, PLANE)]
    pieces = plane + [swap_core(piece) for piece in plane]
    x = to_columns(tokens)
    cot = to_columns(cotangent)

    w_qkv, w_out, w_in, w_back, vectors, bias_in = prepare(plan)(place, *pieces)

    count = TALL * owned
    token_spec = lambda width: pl.BlockSpec((TOKENS, width), lambda step: (step, 0))
    grid_spec = pl.BlockSpec((TALL, BLOCK, D), lambda step: (0, step, 0))
    logsum_spec = pl.BlockSpec((1, 8, TILE), lambda step: (step, 0, 0))
    shape = jax.ShapeDtypeStruct
    packed, attended, middle, logsum = pl.pallas_call(
        forward_kernel,
        grid=(steps,),
        in_specs=[smem, grid_spec, whole((D, 3 * D)), whole((D, D)), whole((8, D))],
        out_specs=[token_spec(3 * D), token_spec(D), token_spec(D), logsum_spec],
        out_shape=[
            shape((count, 3 * D), BF16),
            shape((count, D), BF16),
            shape((count, D), F32),
            shape((steps, 8, TILE), F32),
        ],
        compiler_params=params,
        cost_estimate=pl.CostEstimate(
            flops=10**9, bytes_accessed=7 * 10**6, transcendentals=10**6
        ),
        name="forward",
    )(span, x, w_qkv, w_out, vectors)

    feed_rows = ROWS - (ROW_OUT - 4) + plan.rows
    out, grad_att, grad_mid, parts, first = pl.pallas_call(
        feed_kernel(plan),
        grid=(steps,),
        in_specs=[
            smem,
            token_spec(D),
            token_spec(D),
            grid_spec,
            whole((D, D)),
            whole((D, FF)),
            whole((FF, D)),
            whole((8, D)),
            whole((8, FF)),
        ],
        out_specs=[
            grid_spec,
            token_spec(D),
            token_spec(D),
            whole((CORES, PLANE, plan.deep - plan.lead, plan.rows, LANES)),
            whole((8, LANES)),
        ],
        out_shape=[
            shape((TALL, owned, D), BF16),
            shape((count, D), BF16),
            shape((count, D), F32),
            shape((CORES, PLANE, plan.deep - plan.lead, plan.rows, LANES), BF16),
            shape((8, LANES), F32),
        ],
        scratch_shapes=[
            pltpu.VMEM((D, FF), F32),
            pltpu.VMEM((D, FF), F32),
            pltpu.VMEM((D, D), F32),
            pltpu.VMEM((8, D), F32),
            pltpu.VMEM((8, FF), F32),
            pltpu.VMEM((feed_rows, LANES), F32),
        ],
        compiler_params=params,
        cost_estimate=pl.CostEstimate(
            flops=5 * 10**9, bytes_accessed=10**7, transcendentals=2 * 10**6
        ),
        name="feed",
    )(place, middle, attended, cot, w_out, w_in, w_back, vectors, bias_in)

    layer_out = to_rows(out)

    def stages(value):
        value = value[0].astype(F32) + swap_core(value[1]).astype(F32)
        total = value[0]
        sent = value.astype(BF16)
        for k in range(1, PLANE):
            total = total + swap_seq(sent[k], k).astype(F32)
        return total

    later = stages(parts)

    grad_x, lead_parts = pl.pallas_call(
        back_kernel(plan),
        grid=(steps,),
        in_specs=[
            smem,
            smem,
            grid_spec,
            token_spec(3 * D),
            logsum_spec,
            token_spec(D),
            token_spec(D),
            whole((8, LANES)),
            whole((D, 3 * D)),
            whole((8, D)),
        ],
        out_specs=[grid_spec, whole((CORES, PLANE, plan.lead, plan.rows, LANES))],
        out_shape=[
            shape((TALL, owned, D), BF16),
            shape((CORES, PLANE, plan.lead, plan.rows, LANES), BF16),
        ],
        scratch_shapes=[
            pltpu.VMEM((D, 3 * D), F32),
            pltpu.VMEM((8, D), F32),
            pltpu.VMEM((ROW_OUT + plan.rows + 8, LANES), F32),
        ],
        compiler_params=params,
        cost_estimate=pl.CostEstimate(
            flops=3 * 10**9, bytes_accessed=8 * 10**6, transcendentals=10**6
        ),
        name="back",
    )(place, span, x, packed, logsum, grad_att, grad_mid, first, w_qkv, vectors)

    input_grad = to_rows(grad_x).astype(F32)
    total = jnp.concatenate([stages(lead_parts), later], axis=0)
    if plan.pairwise:
        sent = total.astype(BF16)
        result = lax.dynamic_index_in_dim(total, deep_at, 0, keepdims=False)
        for k in range(1, plan.deep):
            piece = lax.dynamic_index_in_dim(sent, deep_at ^ k, 0, keepdims=False)
            result = result + swap_seq(piece, PLANE * k).astype(F32)
    else:
        moved = lax.all_to_all(
            total.astype(BF16), "seq", 0, 0, axis_index_groups=deep_groups, tiled=True
        )
        result = jnp.sum(moved.astype(F32), axis=0)
    param_grad = lax.dynamic_slice(result.reshape(-1), (shift,), (plan.shard,))
    return layer_out, input_grad, param_grad


def solution(mesh):
    shape = dict(mesh.shape)
    rows = P("dp", "seq", None, None)
    flat = P(("seq", "dp"))
    return jax.shard_map(
        lambda *args: local(shape, *args),
        mesh=mesh,
        in_specs=(rows, P("dp", "seq"), rows, flat),
        out_specs=(rows, rows, flat),
        check_vma=False,
    )
```

time: 532 us -> 141 us (0.27)
  waiting for transfers between devices: 386 us -> 50.4 us
  local copies, waits for them, and re-layouts: 60.4 us -> 12.4 us
  Pallas kernels: 0 us -> 32.6 us
  matrix products: 29.9 us -> 0 us
  starting transfers between devices: 26.8 us -> 43.7 us
  between operations: 14.7 us -> 0.87 us
  other arithmetic: 12.7 us -> 0.7 us
    unnamed x4 -> x0, waiting for transfers between devices: 273 us -> none
    all_to_all x4, waiting for transfers between devices: 114 us -> 10.7 us  [the longest x2 10.7 us: to_columns(): lax.all_to_all(cut, 'seq', 0, 0, axis_index_groups=groups, tiled=True)]
    ppermute x0 -> x22, waiting for transfers between devices: none -> 39.6 us  [the longest x15 39.4 us: swap_seq(): return lax.ppermute(value, 'seq', [(i, i ^ distance) for i in range(seq)])]
    pallas_call x0 -> x4, Pallas kernels: none -> 32.6 us  [the longest x1 12.9 us: local(): pl.pallas_call(feed_kernel(plan), grid=(steps,), in_specs=[smem, token_sp...]
    dot_general x18 -> x0, matrix products: 29.9 us -> none  [the longest x4 9.07 us: contract_last(): lax.dot_general(left, right, (((1,), (1,)), ((), ())), preferred_element_...]
    ppermute x0 -> x22, starting transfers between devices: none -> 24.1 us  [the longest x15 22.1 us: swap_seq(): return lax.ppermute(value, 'seq', [(i, i ^ distance) for i in range(seq)])]
    unnamed x97 -> x24, local copies, waits for them, and re-layouts: 24.6 us -> 4.1 us
    reshape x8 -> x2, local copies, waits for them, and re-layouts: 17.3 us -> 3.09 us  [to_columns(): cut = rows.reshape(local_rows, group, owned, D).transpose(1, 0, 2, 3)]
  transfers between devices with their start and end apart: 6 -> 26, of which waited for: 6 -> 12; matrix products, arithmetic and copies ran while one was open for 5% -> 4% of each run, Pallas kernels for 0% -> 6%
where the time goes in v1:
time: 141 us
  waiting for transfers between devices  50.4 us (36%)
  starting transfers between devices  43.7 us (31%)
  Pallas kernels  32.6 us (23%)
  local copies, waits for them, and re-layouts  12.4 us (9%)
    ppermute x15, waiting for transfers between devices, swap_seq(): return lax.ppermute(value, 'seq', [(i, i ^ distance) for i in range(seq)])  39.4 us
    ppermute x15, starting transfers between devices, swap_seq(): return lax.ppermute(value, 'seq', [(i, i ^ distance) for i in range(seq)])  22.1 us
    pallas_call x1, Pallas kernels, local(): pl.pallas_call(feed_kernel(plan), grid=(steps,), in_specs=[smem, token_sp...  12.9 us
    all_to_all x2, waiting for transfers between devices, to_columns(): lax.all_to_all(cut, 'seq', 0, 0, axis_index_groups=groups, tiled=True)  10.7 us
    pallas_call x1, Pallas kernels, local(): pl.pallas_call(back_kernel(plan), grid=(steps,), in_specs=[smem, smem, gr...  10.6 us
    all_to_all x2, starting transfers between devices, to_columns(): lax.all_to_all(cut, 'seq', 0, 0, axis_index_groups=groups, tiled=True)  10.4 us
    all_to_all x2, starting transfers between devices, to_rows(): lax.all_to_all(cols.reshape(group, local_rows, owned, D), 'seq', 0, 0, ax...  9.26 us
    pallas_call x1, Pallas kernels, local(): pl.pallas_call(forward_kernel, grid=(steps,), in_specs=[smem, grid_spec,...  5.32 us
  transfers between devices with their start and end apart: 26, of which 12 were waited for; matrix products, arithmetic and copies ran while one was open for 4% of the time, Pallas kernels for 6%

profile of v1, /device:TPU:0, one launch (start us, length us, event | category | flops | bytes accessed | tf_op | source)
XLA Modules:
  0.0 140.6 jit_solution(3888623355223621940)
XLA Ops:
  0.6 2.2 %copy.18 = bf16[4,8,48,256]{3,2,0,1:T(8,128)(2,1)} copy(bf16[4,8,48,256]{3,2,1,0:T(8,128)(2,1)} %bitcast.97) | data formatting | bytes 1572864 | tf_op jit(solution)/shard_map/reshape | solution.py:404
  2.8 6.2 %all-to-all-start = ((bf16[8,4,48,256]{3,2,1,0:T(8,128)(2,1)}), bf16[8,4,48,256]{3,2,1,0:T(8,128)(2,1)S(1)}, u32[]{:S(2)}, u32[]{:S(2)}) async-start(bf16[8,4,48,256]{3,2,1,0:T(8,128)(2,1)} %bitcast.90), calls=%async_computation | async-start | bytes 1572864 | tf_op jit(solution)/shard_map/all_to_all | solution.py:405
  9.9 10.7 %all-to-all-done = bf16[8,4,48,256]{3,2,1,0:T(8,128)(2,1)S(1)} async-done(((bf16[8,4,48,256]{3,2,1,0:T(8,128)(2,1)}), bf16[8,4,48,256]{3,2,1,0:T(8,128)(2,1)S(1)}, u32[]{:S(2)}, u32[]{:S(2)}) %all-to-all-start) | async-done | bytes 786464 | tf_op jit(solution)/shard_map/all_to_all | solution.py:405
  20.7 4.2 %all-to-all-start.1 = ((bf16[8,4,48,256]{3,2,1,0:T(8,128)(2,1)}), bf16[8,4,48,256]{3,2,1,0:T(8,128)(2,1)}, u32[]{:S(2)}, u32[]{:S(2)}) async-start(bf16[8,4,48,256]{3,2,1,0:T(8,128)(2,1)} %bitcast.89), calls=%async_computation.1 | async-start | bytes 1572864 | tf_op jit(solution)/shard_map/all_to_all | solution.py:405
  25.5 4.0 %collective-permute-start.3 = (bf16[208,128]{1,0:T(8,128)(2,1)S(1)}, bf16[208,128]{1,0:T(8,128)(2,1)S(1)}, u32[]{:S(2)}, u32[]{:S(2)}) collective-permute-start(bf16[208,128]{1,0:T(8,128)(2,1)S(1)} %bitcast.101), channel_id=1, source_target_pairs={{0,24},{2,26},{4,28},{6,30},{8,16},{10,18},{12,20},{14,22},{16,8},... | collective-permute-start | bytes 159752 | tf_op jit(solution)/shard_map/ppermute | solution.py:420
  30.2 9.8 %collective-permute-done.3 = bf16[208,128]{1,0:T(8,128)(2,1)S(1)} collective-permute-done((bf16[208,128]{1,0:T(8,128)(2,1)S(1)}, bf16[208,128]{1,0:T(8,128)(2,1)S(1)}, u32[]{:S(2)}, u32[]{:S(2)}) %collective-permute-start.3) | collective-permute-done | bytes 53280 | tf_op jit(solution)/shard_map/ppermute | solution.py:420
  41.9 1.6 %collective-permute-start.5 = (bf16[4,208,128]{2,1,0:T(8,128)(2,1)S(1)}, bf16[4,208,128]{2,1,0:T(8,128)(2,1)S(1)}, u32[]{:S(2)}, u32[]{:S(2)}) collective-permute-start(bf16[4,208,128]{2,1,0:T(8,128)(2,1)S(1)} %pad_maximum_fusion.1.refs_0_), channel_id=1, source_target_pairs={{0,4},{2,6},{4,0},{6,2},{8,12},{10,14},{12,8},{14,10},{16,20},{18,... | collective-permute-start | bytes 638984 | tf_op jit(solution)/shard_map/ppermute | solution.py:420
  43.6 4.4 %collective-permute-done.6.refs_3_ = bf16[4,208,128]{2,1,0:T(8,128)(2,1)S(1)} collective-permute-done((bf16[4,208,128]{2,1,0:T(8,128)(2,1)S(1)}, bf16[4,208,128]{2,1,0:T(8,128)(2,1)S(1)}, u32[]{:S(2)}, u32[]{:S(2)}) %collective-permute-start.6) | collective-permute-done | bytes 213024 | tf_op jit(solution)/shard_map/ppermute | solution.py:420
  51.6 3.8 %prepare.1 = (bf16[256,768]{1,0:T(8,128)(2,1)S(1)}, bf16[256,256]{1,0:T(8,128)(2,1)S(1)}, bf16[256,1024]{1,0:T(8,128)(2,1)S(1)}, bf16[1024,256]{1,0:T(8,128)(2,1...) custom-call(s32[3]{0:T(128)S(1)} %pad_add_fusion.place_ref, bf16[4,208,128]{2,1,0:T(8,128)(2,1)S(1)} %pad_maximum_fusion.1.refs_0_, ...), custom_call_target="tpu_custom_call" | custom-call | tf_op jit(solution)/shard_map/prepare/pallas_call | solution.py:446
  56.0 5.3 %forward.1 = (bf16[1536,768]{1,0:T(8,128)(2,1)}, bf16[1536,256]{1,0:T(8,128)(2,1)S(1)}, f32[1536,256]{1,0:T(8,128)S(1)}, f32[3,8,256]{2,1,0:T(8,128)S(1)}) custom-call(s32[1,1]{1,0:T(1,128)} %collective-permute-done.span_ref, bf16[32,48,256]{2,1,0:T(8,128)(2,1)S(1)} %bitcast.92, bf16[256,768]{1,0:T(8,128)(2,1)S(1)} %get-tuple-element.20.w_qkv, ...), custom_call_target="tpu_custom_call" | custom-call | flops 1000000000 | bytes 7000000 | tf_op jit(solution)/shard_map/forward/pallas_call | solution.py:453
  64.8 12.9 %feed.1 = (bf16[32,48,256]{2,1,0:T(8,128)(2,1)}, bf16[1536,256]{1,0:T(8,128)(2,1)S(1)}, f32[1536,256]{1,0:T(8,128)}, bf16[2,4,3,208,128]{4,3,2,1,0:T(8,128)(2,1)}, f32[8,128]{1,0:T(8,128)S(1)}) custom-call(s32[3]{0:T(128)S(1)} %pad_add_fusion.place_ref, f32[1536,256]{1,0:T(8,128)} %copy-done.6, bf16[1536,256]{1,0:T(8,128)(2,1)S(1)} %get-tuple-element.24.attended_ref, ...), custom_call_target="tpu_custom_call" | custom-call | flops 5000000000 | bytes 10000000 | tf_op jit(solution)/shard_map/feed/pallas_call | solution.py:472
  77.7 10.6 %back.1 = (bf16[32,48,256]{2,1,0:T(8,128)(2,1)}, bf16[2,4,1,208,128]{4,3,2,1,0:T(8,128)(2,1)S(1)}) custom-call(s32[3]{0:T(128)S(1)} %pad_add_fusion.place_ref, s32[1,1]{1,0:T(1,128)} %collective-permute-done.span_ref, bf16[32,48,256]{2,1,0:T(8,128)(2,1)S(1)} %bitcast.93, bf16[1536,768]{1,0:T(8,128)(2,1)} %get-tuple-element.29.packed_ref, ...), custom_call_target="tpu_custom_call" | custom-call | flops 3000000000 | bytes 8000000 | tf_op jit(solution)/shard_map/back/pallas_call | solution.py:527
  90.4 5.7 %all-to-all-start.3 = ((bf16[8,4,48,256]{3,2,1,0:T(8,128)(2,1)}), bf16[8,4,48,256]{3,2,1,0:T(8,128)(2,1)S(1)}, u32[]{:S(2)}, u32[]{:S(2)}) async-start(bf16[8,4,48,256]{3,2,1,0:T(8,128)(2,1)} %bitcast.17), calls=%async_computation.3 | async-start | bytes 1572864 | tf_op jit(solution)/shard_map/all_to_all | solution.py:409
  96.1 2.1 %collective-permute-start.12 = (bf16[1,208,128]{2,1,0:T(8,128)(2,1)S(1)}, bf16[1,208,128]{2,1,0:T(8,128)(2,1)S(1)}, u32[]{:S(2)}, u32[]{:S(2)}) collective-permute-start(bf16[1,208,128]{2,1,0:T(8,128)(2,1)S(1)} %get-tuple-element.47), channel_id=1, source_target_pairs={{0,2},{2,0},{4,6},{6,4},{8,10},{10,8},{12,14},{14,12},{16,18},{18,... | collective-permute-start | bytes 159752 | tf_op jit(solution)/shard_map/ppermute | solution.py:420
  100.0 2.0 %collective-permute-start.16 = (bf16[3,208,128]{2,1,0:T(8,128)(2,1)S(1)}, bf16[3,208,128]{2,1,0:T(8,128)(2,1)S(1)}, u32[]{:S(2)}, u32[]{:S(2)}) collective-permute-start(bf16[3,208,128]{2,1,0:T(8,128)(2,1)S(1)} %get-tuple-element.41), channel_id=1, source_target_pairs={{0,2},{2,0},{4,6},{6,4},{8,10},{10,8},{12,14},{14,12},{16,18},{18,... | collective-permute-start | bytes 479240 | tf_op jit(solution)/shard_map/ppermute | solution.py:420
  103.5 5.7 %collective-permute-done.12 = bf16[1,208,128]{2,1,0:T(8,128)(2,1)S(1)} collective-permute-done((bf16[1,208,128]{2,1,0:T(8,128)(2,1)S(1)}, bf16[1,208,128]{2,1,0:T(8,128)(2,1)S(1)}, u32[]{:S(2)}, u32[]{:S(2)}) %collective-permute-start.12) | collective-permute-done | bytes 53280 | tf_op jit(solution)/shard_map/ppermute | solution.py:420
  109.2 1.8 %collective-permute-start.18 = (bf16[3,208,128]{2,1,0:T(8,128)(2,1)S(1)}, bf16[3,208,128]{2,1,0:T(8,128)(2,1)S(1)}, u32[]{:S(2)}, u32[]{:S(2)}) collective-permute-start(bf16[3,208,128]{2,1,0:T(8,128)(2,1)S(1)} %get-tuple-element.42), channel_id=1, source_target_pairs={{0,6},{2,4},{4,2},{6,0},{8,14},{10,12},{12,10},{14,8},{16,22},{18,... | collective-permute-start | bytes 479240 | tf_op jit(solution)/shard_map/ppermute | solution.py:420
  111.2 2.5 %collective-permute-done.16 = bf16[3,208,128]{2,1,0:T(8,128)(2,1)S(1)} collective-permute-done((bf16[3,208,128]{2,1,0:T(8,128)(2,1)S(1)}, bf16[3,208,128]{2,1,0:T(8,128)(2,1)S(1)}, u32[]{:S(2)}, u32[]{:S(2)}) %collective-permute-start.16) | collective-permute-done | bytes 159776 | tf_op jit(solution)/shard_map/ppermute | solution.py:420
  113.7 3.3 %collective-permute-done.18 = bf16[3,208,128]{2,1,0:T(8,128)(2,1)S(1)} collective-permute-done((bf16[3,208,128]{2,1,0:T(8,128)(2,1)S(1)}, bf16[3,208,128]{2,1,0:T(8,128)(2,1)S(1)}, u32[]{:S(2)}, u32[]{:S(2)}) %collective-permute-start.18) | collective-permute-done | bytes 159776 | tf_op jit(solution)/shard_map/ppermute | solution.py:420
  117.1 3.6 %all-to-all-start.2 = ((bf16[8,4,48,256]{3,2,1,0:T(8,128)(2,1)}), bf16[8,4,48,256]{3,2,1,0:T(8,128)(2,1)S(1)}, u32[]{:S(2)}, u32[]{:S(2)}) async-start(bf16[8,4,48,256]{3,2,1,0:T(8,128)(2,1)} %bitcast.14), calls=%async_computation.2 | async-start | bytes 1572864 | tf_op jit(solution)/shard_map/all_to_all | solution.py:409
  120.8 2.0 %collective-permute-start.19 = (bf16[208,128]{1,0:T(8,128)(2,1)S(1)}, bf16[208,128]{1,0:T(8,128)(2,1)S(1)}, u32[]{:S(2)}, u32[]{:S(2)}) collective-permute-start(bf16[208,128]{1,0:T(8,128)(2,1)S(1)} %get-tuple-element.44), channel_id=1, source_target_pairs={{0,8},{2,10},{4,12},{6,14},{8,0},{10,2},{12,4},{14,6},{16,24},{18,... | collective-permute-start | bytes 159752 | tf_op jit(solution)/shard_map/ppermute | solution.py:420
  122.8 3.0 %collective-permute-start.20 = (bf16[208,128]{1,0:T(8,128)(2,1)S(1)}, bf16[208,128]{1,0:T(8,128)(2,1)S(1)}, u32[]{:S(2)}, u32[]{:S(2)}) collective-permute-start(bf16[208,128]{1,0:T(8,128)(2,1)S(1)} %get-tuple-element.46), channel_id=1, source_target_pairs={{0,16},{2,18},{4,20},{6,22},{8,24},{10,26},{12,28},{14,30},{16,0},... | collective-permute-start | bytes 159752 | tf_op jit(solution)/shard_map/ppermute | solution.py:420
  125.8 8.0 %collective-permute-done.19 = bf16[208,128]{1,0:T(8,128)(2,1)S(1)} collective-permute-done((bf16[208,128]{1,0:T(8,128)(2,1)S(1)}, bf16[208,128]{1,0:T(8,128)(2,1)S(1)}, u32[]{:S(2)}, u32[]{:S(2)}) %collective-permute-start.19) | collective-permute-done | bytes 53280 | tf_op jit(solution)/shard_map/ppermute | solution.py:420
  133.8 3.6 %collective-permute-done.21 = bf16[208,128]{1,0:T(8,128)(2,1)S(1)} collective-permute-done((bf16[208,128]{1,0:T(8,128)(2,1)S(1)}, bf16[208,128]{1,0:T(8,128)(2,1)S(1)}, u32[]{:S(2)}, u32[]{:S(2)}) %collective-permute-start.21) | collective-permute-done | bytes 53280 | tf_op jit(solution)/shard_map/ppermute | solution.py:420
  (78 shorter events, 20.8 us)
Async XLA Ops:
  2.8 17.9 %all-to-all-start = ((bf16[8,4,48,256]{3,2,1,0:T(8,128)(2,1)}), bf16[8,4,48,256]{3,2,1,0:T(8,128)(2,1)S(1)}, u32[]{:S(2)}, u32[]{:S(2)}) async-start(bf16[8,4,48,256]{3,2,1,0:T(8,128)(2,1)} %bitcast.90), calls=%async_computation | async-start | bytes 1572864 | tf_op jit(solution)/shard_map/all_to_all | solution.py:405
  20.7 43.2 %all-to-all-start.1 = ((bf16[8,4,48,256]{3,2,1,0:T(8,128)(2,1)}), bf16[8,4,48,256]{3,2,1,0:T(8,128)(2,1)}, u32[]{:S(2)}, u32[]{:S(2)}) async-start(bf16[8,4,48,256]{3,2,1,0:T(8,128)(2,1)} %bitcast.89), calls=%async_computation.1 | async-start | bytes 1572864 | tf_op jit(solution)/shard_map/all_to_all | solution.py:405
  25.5 14.4 %collective-permute-start.3 = (bf16[208,128]{1,0:T(8,128)(2,1)S(1)}, bf16[208,128]{1,0:T(8,128)(2,1)S(1)}, u32[]{:S(2)}, u32[]{:S(2)}) collective-permute-start(bf16[208,128]{1,0:T(8,128)(2,1)S(1)} %bitcast.101), channel_id=1, source_target_pairs={{0,24},{2,26},{4,28},{6,30},{8,16},{10,18},{12,20},{14,22},{16,8},... | collective-permute-start | bytes 159752 | tf_op jit(solution)/shard_map/ppermute | solution.py:420
  29.5 10.5 %collective-permute-start.1 = (bf16[208,128]{1,0:T(8,128)(2,1)S(1)}, bf16[208,128]{1,0:T(8,128)(2,1)S(1)}, u32[]{:S(2)}, u32[]{:S(2)}) collective-permute-start(bf16[208,128]{1,0:T(8,128)(2,1)S(1)} %bitcast.102), channel_id=1, source_target_pairs={{0,8},{2,10},{4,12},{6,14},{8,0},{10,2},{12,4},{14,6},{16,24},{18,... | collective-permute-start | bytes 159752 | tf_op jit(solution)/shard_map/ppermute | solution.py:420
  29.5 10.5 %collective-permute-start.2 = (bf16[208,128]{1,0:T(8,128)(2,1)S(1)}, bf16[208,128]{1,0:T(8,128)(2,1)S(1)}, u32[]{:S(2)}, u32[]{:S(2)}) collective-permute-start(bf16[208,128]{1,0:T(8,128)(2,1)S(1)} %bitcast.103), channel_id=1, source_target_pairs={{0,16},{2,18},{4,20},{6,22},{8,24},{10,26},{12,28},{14,30},{16,0},... | collective-permute-start | bytes 159752 | tf_op jit(solution)/shard_map/ppermute | solution.py:420
  40.0 8.0 %collective-permute-start.6 = (bf16[4,208,128]{2,1,0:T(8,128)(2,1)S(1)}, bf16[4,208,128]{2,1,0:T(8,128)(2,1)S(1)}, u32[]{:S(2)}, u32[]{:S(2)}) collective-permute-start(bf16[4,208,128]{2,1,0:T(8,128)(2,1)S(1)} %pad_maximum_fusion.1.refs_0_), channel_id=1, source_target_pairs={{0,6},{2,4},{4,2},{6,0},{8,14},{10,12},{12,10},{14,8},{16,22},{18,... | collective-permute-start | bytes 638984 | tf_op jit(solution)/shard_map/ppermute | solution.py:420
  41.5 6.8 %collective-permute-start.4 = (bf16[4,208,128]{2,1,0:T(8,128)(2,1)S(1)}, bf16[4,208,128]{2,1,0:T(8,128)(2,1)S(1)}, u32[]{:S(2)}, u32[]{:S(2)}) collective-permute-start(bf16[4,208,128]{2,1,0:T(8,128)(2,1)S(1)} %pad_maximum_fusion.1.refs_0_), channel_id=1, source_target_pairs={{0,2},{2,0},{4,6},{6,4},{8,10},{10,8},{12,14},{14,12},{16,18},{18,... | collective-permute-start | bytes 638984 | tf_op jit(solution)/shard_map/ppermute | solution.py:420
  41.9 8.2 %collective-permute-start.5 = (bf16[4,208,128]{2,1,0:T(8,128)(2,1)S(1)}, bf16[4,208,128]{2,1,0:T(8,128)(2,1)S(1)}, u32[]{:S(2)}, u32[]{:S(2)}) collective-permute-start(bf16[4,208,128]{2,1,0:T(8,128)(2,1)S(1)} %pad_maximum_fusion.1.refs_0_), channel_id=1, source_target_pairs={{0,4},{2,6},{4,0},{6,2},{8,12},{10,14},{12,8},{14,10},{16,20},{18,... | collective-permute-start | bytes 638984 | tf_op jit(solution)/shard_map/ppermute | solution.py:420
  43.6 7.8 %collective-permute-start.7 = (bf16[4,208,128]{2,1,0:T(8,128)(2,1)S(1)}, bf16[4,208,128]{2,1,0:T(8,128)(2,1)S(1)}, u32[]{:S(2)}, u32[]{:S(2)}) collective-permute-start(bf16[4,208,128]{2,1,0:T(8,128)(2,1)S(1)} %pad_maximum_fusion.1.refs_0_), channel_id=1, source_target_pairs={{0,1},{1,0},{2,3},{3,2},{4,5},{5,4},{6,7},{7,6},{8,9},{9,8},{10,11... | collective-permute-start | bytes 638984 | tf_op jit(solution)/shard_map/ppermute | solution.py:423
  48.0 3.4 %collective-permute-start.10 = (bf16[4,208,128]{2,1,0:T(8,128)(2,1)S(1)}, bf16[4,208,128]{2,1,0:T(8,128)(2,1)S(1)}, u32[]{:S(2)}, u32[]{:S(2)}) collective-permute-start(bf16[4,208,128]{2,1,0:T(8,128)(2,1)S(1)} %collective-permute-done.6.refs_3_), channel_id=1, source_target_pairs={{0,1},{1,0},{2,3},{3,2},{4,5},{5,4},{6,7},{7,6},{8,9},{9,8},{10,11... | collective-permute-start | bytes 638984 | tf_op jit(solution)/shard_map/ppermute | solution.py:423
  50.1 5.9 %collective-permute-start = (s32[1,1]{1,0:T(1,128)S(1)}, s32[1,1]{1,0:T(1,128)}, u32[]{:S(2)}, u32[]{:S(2)}) collective-permute-start(s32[1,1]{1,0:T(1,128)S(1)} %bitcast.108), channel_id=1, source_target_pairs={{0,0},{2,2},{8,4},{10,6},{16,8},{18,10},{24,12},{26,14},{4,16},{6,... | collective-permute-start | bytes 20 | tf_op jit(solution)/shard_map/ppermute | solution.py:432
  88.9 7.1 %collective-permute-start.11 = (bf16[4,1,208,128]{3,2,0,1:T(8,128)(2,1)}, bf16[4,1,208,128]{3,2,0,1:T(8,128)(2,1)S(1)}, u32[]{:S(2)}, u32[]{:S(2)}) collective-permute-start(bf16[4,1,208,128]{3,2,0,1:T(8,128)(2,1)} %slice_bitcast_fusion.3), channel_id=1, source_target_pairs={{0,1},{1,0},{2,3},{3,2},{4,5},{5,4},{6,7},{7,6},{8,9},{9,8},{10,11... | collective-permute-start | bytes 638984 | tf_op jit(solution)/shard_map/ppermute | solution.py:423
  90.2 9.6 %collective-permute-start.15 = (bf16[4,3,208,128]{3,2,1,0:T(8,128)(2,1)}, bf16[4,3,208,128]{3,2,1,0:T(8,128)(2,1)S(1)}, u32[]{:S(2)}, u32[]{:S(2)}) collective-permute-start(bf16[4,3,208,128]{3,2,1,0:T(8,128)(2,1)} %slice_bitcast_fusion), channel_id=1, source_target_pairs={{0,1},{1,0},{2,3},{3,2},{4,5},{5,4},{6,7},{7,6},{8,9},{9,8},{10,11... | collective-permute-start | bytes 1916936 | tf_op jit(solution)/shard_map/ppermute | solution.py:423
  90.4 26.8 %all-to-all-start.3 = ((bf16[8,4,48,256]{3,2,1,0:T(8,128)(2,1)}), bf16[8,4,48,256]{3,2,1,0:T(8,128)(2,1)S(1)}, u32[]{:S(2)}, u32[]{:S(2)}) async-start(bf16[8,4,48,256]{3,2,1,0:T(8,128)(2,1)} %bitcast.17), calls=%async_computation.3 | async-start | bytes 1572864 | tf_op jit(solution)/shard_map/all_to_all | solution.py:409
  96.1 13.0 %collective-permute-start.12 = (bf16[1,208,128]{2,1,0:T(8,128)(2,1)S(1)}, bf16[1,208,128]{2,1,0:T(8,128)(2,1)S(1)}, u32[]{:S(2)}, u32[]{:S(2)}) collective-permute-start(bf16[1,208,128]{2,1,0:T(8,128)(2,1)S(1)} %get-tuple-element.47), channel_id=1, source_target_pairs={{0,2},{2,0},{4,6},{6,4},{8,10},{10,8},{12,14},{14,12},{16,18},{18,... | collective-permute-start | bytes 159752 | tf_op jit(solution)/shard_map/ppermute | solution.py:420
  98.2 12.8 %collective-permute-start.13 = (bf16[1,208,128]{2,1,0:T(8,128)(2,1)S(1)}, bf16[1,208,128]{2,1,0:T(8,128)(2,1)S(1)}, u32[]{:S(2)}, u32[]{:S(2)}) collective-permute-start(bf16[1,208,128]{2,1,0:T(8,128)(2,1)S(1)} %get-tuple-element.48), channel_id=1, source_target_pairs={{0,4},{2,6},{4,0},{6,2},{8,12},{10,14},{12,8},{14,10},{16,20},{18,... | collective-permute-start | bytes 159752 | tf_op jit(solution)/shard_map/ppermute | solution.py:420
  99.7 11.5 %collective-permute-start.14 = (bf16[1,208,128]{2,1,0:T(8,128)(2,1)S(1)}, bf16[1,208,128]{2,1,0:T(8,128)(2,1)S(1)}, u32[]{:S(2)}, u32[]{:S(2)}) collective-permute-start(bf16[1,208,128]{2,1,0:T(8,128)(2,1)S(1)} %slice_bitcast_fusion.8), channel_id=1, source_target_pairs={{0,6},{2,4},{4,2},{6,0},{8,14},{10,12},{12,10},{14,8},{16,22},{18,... | collective-permute-start | bytes 159752 | tf_op jit(solution)/shard_map/ppermute | solution.py:420
  100.0 13.7 %collective-permute-start.16 = (bf16[3,208,128]{2,1,0:T(8,128)(2,1)S(1)}, bf16[3,208,128]{2,1,0:T(8,128)(2,1)S(1)}, u32[]{:S(2)}, u32[]{:S(2)}) collective-permute-start(bf16[3,208,128]{2,1,0:T(8,128)(2,1)S(1)} %get-tuple-element.41), channel_id=1, source_target_pairs={{0,2},{2,0},{4,6},{6,4},{8,10},{10,8},{12,14},{14,12},{16,18},{18,... | collective-permute-start | bytes 479240 | tf_op jit(solution)/shard_map/ppermute | solution.py:420
  102.0 11.7 %collective-permute-start.17 = (bf16[3,208,128]{2,1,0:T(8,128)(2,1)S(1)}, bf16[3,208,128]{2,1,0:T(8,128)(2,1)S(1)}, u32[]{:S(2)}, u32[]{:S(2)}) collective-permute-start(bf16[3,208,128]{2,1,0:T(8,128)(2,1)S(1)} %get-tuple-element.43), channel_id=1, source_target_pairs={{0,4},{2,6},{4,0},{6,2},{8,12},{10,14},{12,8},{14,10},{16,20},{18,... | collective-permute-start | bytes 479240 | tf_op jit(solution)/shard_map/ppermute | solution.py:420
  109.2 7.9 %collective-permute-start.18 = (bf16[3,208,128]{2,1,0:T(8,128)(2,1)S(1)}, bf16[3,208,128]{2,1,0:T(8,128)(2,1)S(1)}, u32[]{:S(2)}, u32[]{:S(2)}) collective-permute-start(bf16[3,208,128]{2,1,0:T(8,128)(2,1)S(1)} %get-tuple-element.42), channel_id=1, source_target_pairs={{0,6},{2,4},{4,2},{6,0},{8,14},{10,12},{12,10},{14,8},{16,22},{18,... | collective-permute-start | bytes 479240 | tf_op jit(solution)/shard_map/ppermute | solution.py:420
  117.1 22.6 %all-to-all-start.2 = ((bf16[8,4,48,256]{3,2,1,0:T(8,128)(2,1)}), bf16[8,4,48,256]{3,2,1,0:T(8,128)(2,1)S(1)}, u32[]{:S(2)}, u32[]{:S(2)}) async-start(bf16[8,4,48,256]{3,2,1,0:T(8,128)(2,1)} %bitcast.14), calls=%async_computation.2 | async-start | bytes 1572864 | tf_op jit(solution)/shard_map/all_to_all | solution.py:409
  120.8 13.0 %collective-permute-start.19 = (bf16[208,128]{1,0:T(8,128)(2,1)S(1)}, bf16[208,128]{1,0:T(8,128)(2,1)S(1)}, u32[]{:S(2)}, u32[]{:S(2)}) collective-permute-start(bf16[208,128]{1,0:T(8,128)(2,1)S(1)} %get-tuple-element.44), channel_id=1, source_target_pairs={{0,8},{2,10},{4,12},{6,14},{8,0},{10,2},{12,4},{14,6},{16,24},{18,... | collective-permute-start | bytes 159752 | tf_op jit(solution)/shard_map/ppermute | solution.py:420
  122.8 11.0 %collective-permute-start.20 = (bf16[208,128]{1,0:T(8,128)(2,1)S(1)}, bf16[208,128]{1,0:T(8,128)(2,1)S(1)}, u32[]{:S(2)}, u32[]{:S(2)}) collective-permute-start(bf16[208,128]{1,0:T(8,128)(2,1)S(1)} %get-tuple-element.46), channel_id=1, source_target_pairs={{0,16},{2,18},{4,20},{6,22},{8,24},{10,26},{12,28},{14,30},{16,0},... | collective-permute-start | bytes 159752 | tf_op jit(solution)/shard_map/ppermute | solution.py:420
  125.8 11.7 %collective-permute-start.21 = (bf16[208,128]{1,0:T(8,128)(2,1)S(1)}, bf16[208,128]{1,0:T(8,128)(2,1)S(1)}, u32[]{:S(2)}, u32[]{:S(2)}) collective-permute-start(bf16[208,128]{1,0:T(8,128)(2,1)S(1)} %get-tuple-element.45), channel_id=1, source_target_pairs={{0,24},{2,26},{4,28},{6,30},{8,16},{10,18},{12,20},{14,22},{16,8},... | collective-permute-start | bytes 159752 | tf_op jit(solution)/shard_map/ppermute | solution.py:420
  (14 other events, 115.0 us)

commit v2 on v1

--- a/solution.py
+++ b/solution.py
@@ -19,7 +19,7 @@
 HALF = 8
 TOKENS = TALL * BLOCK
 TILE = TALL * HALF
-VMEM_BYTES = 50 * 1024 * 1024
+VMEM_BYTES = 60 * 1024 * 1024
 
 ROW_GAIN_ONE = 0
 ROW_SHIFT_ONE = 2
@@ -33,6 +33,8 @@
 ROW_BIAS_BACK = ROW_BACK + 2 * FF
 ROWS = ROW_BIAS_BACK + 2
 
+SPAN = 5
+
 F32 = jnp.float32
 BF16 = jnp.bfloat16
 
@@ -90,7 +92,7 @@
         self.deep = seq // PLANE
         self.count = seq * CORES
         self.pairwise = self.deep == 4
-        rows = (shard + LANES - 2) // LANES + 1
+        rows = (shard + LANES - 2) // LANES + 2
         self.rows = -(-rows // 16) * 16
         self.lead = -(-(ROW_OUT * LANES) // (PLANE * CORES * shard))
 
@@ -146,6 +148,10 @@
                 vectors[index : index + 1, part * LANES : (part + 1) * LANES] = flat[
                     row + part : row + part + 1
                 ]
+        holder = place_ref[3]
+        vectors[SPAN : SPAN + 1, :LANES] = held[holder // PLANE, holder % PLANE, core_at][
+            plan.rows - 1 :
+        ].astype(F32)
         for part in range(8):
             bias_in[0:1, part * LANES : (part + 1) * LANES] = flat[
                 ROW_BIAS_IN + part : ROW_BIAS_IN + part + 1
@@ -170,14 +176,14 @@
 
 
 def forward_kernel(
-    span_ref, x_ref, w_qkv, w_out, vectors, packed_ref, attended_ref, middle_ref, logsum_ref
+    x_ref, w_qkv, w_out, vectors, packed_ref, attended_ref, middle_ref, logsum_ref
 ):
     x = to_tokens(x_ref[...].astype(F32))
     hat, _ = center(x)
     normed = (hat * vectors[0:1] + vectors[1:2]).astype(BF16)
     packed = nn(normed, w_qkv[...]).astype(BF16)
     packed_ref[...] = packed
-    mask = allowed(span_ref[0, 0])
+    mask = allowed(vectors[SPAN : SPAN + 1, 0:1])
     scale = HEAD**-0.5
     tiles = []
     for half in range(2):
@@ -208,31 +214,13 @@
         ]
 
 
-def feed_kernel(plan):
+def feed_kernel(plan, group):
     base = ROW_OUT - 4
 
-    def kernel(
-        place_ref,
-        middle_ref,
-        attended_ref,
-        cot_ref,
-        w_out,
-        w_in,
-        w_back,
-        vectors,
-        bias_in,
-        out_ref,
-        grad_att_ref,
-        grad_mid_ref,
-        parts_ref,
-        first_ref,
-        acc_in,
-        acc_back,
-        acc_out,
-        acc_vec,
-        acc_bias,
-        flat,
-    ):
+    def kernel(place_ref, middle_ref, attended_ref, cot_ref, *refs):
+        w_out, w_in, w_back, vectors, bias_in = refs[:5]
+        out_ref, grad_att_ref, grad_mid_ref, keep_ref, send_ref, first_ref = refs[5:11]
+        acc_in, acc_back, acc_out, acc_vec, acc_bias, flat = refs[11:]
         step = pl.program_id(0)
 
         @pl.when(step == 0)
@@ -290,24 +278,29 @@
                     0:1, part * LANES : (part + 1) * LANES
                 ]
             first_ref[...] = flat[ROW_OUT - base : ROW_OUT - base + 8]
-            send_rows(plan, place_ref, flat, base, parts_ref, plan.lead, plan.deep)
+            send_rows(plan, place_ref, flat, base, (keep_ref, send_ref), plan.lead, plan.deep)
 
     return kernel
 
 
-def send_rows(plan, place_ref, flat, base, parts_ref, low, high):
+def send_rows(plan, place_ref, flat, base, refs, low, high):
     plane_at, core_at = place_ref[1], place_ref[2]
-    for device in range(low * PLANE * CORES, high * PLANE * CORES):
-        row = plan.first_row(device) - base
-        parts_ref[
-            (device % CORES) ^ core_at, (device // CORES % PLANE) ^ plane_at, device // 8 - low
-        ] = flat[row : row + plan.rows].astype(BF16)
-
-
-def back_kernel(plan):
+
+    def write(own_core):
+        for device in range(low * PLANE * CORES, high * PLANE * CORES):
+            row = plan.first_row(device) - base
+            ref = refs[(device % CORES) ^ own_core]
+            ref[(device // CORES % PLANE) ^ plane_at, device // (PLANE * CORES) - low] = flat[
+                row : row + plan.rows
+            ].astype(BF16)
+
+    for own_core in range(CORES):
+        pl.when(core_at == own_core)(lambda own_core=own_core: write(own_core))
+
+
+def attend_back_kernel(plan):
     def kernel(
         place_ref,
-        span_ref,
         x_ref,
         packed_ref,
         logsum_ref,
@@ -317,7 +310,8 @@
         w_qkv,
         vectors,
         grad_x_ref,
-        parts_ref,
+        keep_ref,
+        send_ref,
         acc_qkv,
         acc_vec,
         flat,
@@ -329,7 +323,7 @@
             for ref in (acc_qkv, acc_vec):
                 ref[...] = jnp.zeros_like(ref)
 
-        mask = allowed(span_ref[0, 0])
+        mask = allowed(vectors[SPAN : SPAN + 1, 0:1])
         scale = HEAD**-0.5
         tiles = []
         for half in range(2):
@@ -371,7 +365,24 @@
                         index : index + 1, part * LANES : (part + 1) * LANES
                     ]
             flat[ROW_OUT : ROW_OUT + 8] = first_ref[...]
-            send_rows(plan, place_ref, flat, 0, parts_ref, 0, plan.lead)
+            send_rows(plan, place_ref, flat, 0, (keep_ref, send_ref), 0, plan.lead)
+
+    return kernel
+
+
+def cut_rows_kernel(group, owned):
+    def kernel(rows_ref, out_ref):
+        for index in range(group):
+            out_ref[index] = rows_ref[:, index * owned : (index + 1) * owned]
+
+    return kernel
+
+
+def cut_pieces_kernel(group, owned):
+    def kernel(place_ref, rows_ref, *pieces):
+        for index, piece in enumerate(pieces):
+            column = pl.multiple_of((index ^ place_ref[3]) * owned, 16)
+            piece[...] = rows_ref[:, pl.ds(column, owned)]
 
     return kernel
 
@@ -390,7 +401,8 @@
     seq_at = lax.axis_index("seq")
     core_at = lax.axis_index("dp")
     deep_at, plane_at = seq_at // PLANE, seq_at % PLANE
-    place = jnp.stack([deep_at, plane_at, core_at]).astype(jnp.int32)
+    holder = seq_at % group * owned // STRIDE * (seq * STRIDE // columns)
+    place = jnp.stack([deep_at, plane_at, core_at, holder]).astype(jnp.int32)
     shift = plan.shard * (seq_at * CORES + core_at) % LANES
     smem = pl.BlockSpec(memory_space=pltpu.SMEM)
     params = pltpu.CompilerParams(
@@ -400,20 +412,11 @@
     groups = [[group * g + i for i in range(group)] for g in range(seq // group)]
     deep_groups = [[PLANE * z + q for z in range(plan.deep)] for q in range(PLANE)]
 
-    def to_columns(rows):
-        cut = rows.reshape(local_rows, group, owned, D).transpose(1, 0, 2, 3)
-        moved = lax.all_to_all(cut, "seq", 0, 0, axis_index_groups=groups, tiled=True)
-        return moved.reshape(TALL, owned, D)
+    def exchange(blocks):
+        return lax.all_to_all(blocks, "seq", 0, 0, axis_index_groups=groups, tiled=True)
 
     def to_rows(cols):
-        moved = lax.all_to_all(
-            cols.reshape(group, local_rows, owned, D),
-            "seq",
-            0,
-            0,
-            axis_index_groups=groups,
-            tiled=True,
-        )
+        moved = exchange(cols.reshape(group, local_rows, owned, D))
         return moved.transpose(1, 0, 2, 3).reshape(tokens.shape)
 
     def swap_seq(value, distance):
@@ -422,26 +425,36 @@
     def swap_core(value):
         return lax.ppermute(value, "dp", [(0, 1), (1, 0)])
 
-    per_block = STRIDE // owned
-    holders = seq * STRIDE // columns
-    routes = []
-    for target in range(seq):
-        index, place_in = target // group, target % group
-        source = place_in // per_block * holders + index * per_block + place_in % per_block
-        routes.append((source, target))
-    span = lax.ppermute(column_rows[:1, :1], "seq", routes)
-
-    own = lax.dynamic_update_slice(
-        jnp.zeros((plan.rows * LANES,), BF16), flat_params, (shift,)
-    ).reshape(plan.rows, LANES)
+    blank = jnp.zeros((plan.rows - 1) * LANES, BF16)
+    blank = jnp.concatenate([blank, jnp.broadcast_to(column_rows[0, 0].astype(BF16), (LANES,))])
+    own = lax.dynamic_update_slice(blank, flat_params, (shift,)).reshape(plan.rows, LANES)
     if plan.pairwise:
-        deep = jnp.stack([own] + [swap_seq(own, PLANE * k) for k in range(1, plan.deep)])
+        arrived = [swap_seq(own, PLANE * k) for k in range(1, plan.deep)]
+        deep = jnp.stack([own] + arrived)
     else:
+        arrived = [own]
         deep = lax.all_gather(own, "seq", axis=0, axis_index_groups=deep_groups)
+    vmem = pl.BlockSpec(memory_space=pltpu.VMEM)
+    x_cut = pl.pallas_call(
+        cut_rows_kernel(group, owned),
+        out_shape=jax.ShapeDtypeStruct((group, local_rows, owned, D), BF16),
+        in_specs=[vmem],
+        out_specs=vmem,
+        name="cut_tokens",
+    )(tokens.reshape(local_rows, columns, D))
+    x_cut, _ = lax.optimization_barrier((x_cut, arrived))
+    x = exchange(x_cut).reshape(TALL, owned, D)
     plane = [deep] + [swap_seq(deep, k) for k in range(1, PLANE)]
     pieces = plane + [swap_core(piece) for piece in plane]
-    x = to_columns(tokens)
-    cot = to_columns(cotangent)
+    cot_cut = pl.pallas_call(
+        cut_rows_kernel(group, owned),
+        out_shape=jax.ShapeDtypeStruct((group, local_rows, owned, D), BF16),
+        in_specs=[vmem],
+        out_specs=vmem,
+        name="cut_cotangent",
+    )(cotangent.reshape(local_rows, columns, D))
+    cot_cut, _ = lax.optimization_barrier((cot_cut, (x, plane[1:])))
+    cot = exchange(cot_cut).reshape(TALL, owned, D)
 
     w_qkv, w_out, w_in, w_back, vectors, bias_in = prepare(plan)(place, *pieces)
 
@@ -453,7 +466,7 @@
     packed, attended, middle, logsum = pl.pallas_call(
         forward_kernel,
         grid=(steps,),
-        in_specs=[smem, grid_spec, whole((D, 3 * D)), whole((D, D)), whole((8, D))],
+        in_specs=[grid_spec, whole((D, 3 * D)), whole((D, D)), whole((8, D))],
         out_specs=[token_spec(3 * D), token_spec(D), token_spec(D), logsum_spec],
         out_shape=[
             shape((count, 3 * D), BF16),
@@ -466,11 +479,12 @@
             flops=10**9, bytes_accessed=7 * 10**6, transcendentals=10**6
         ),
         name="forward",
-    )(span, x, w_qkv, w_out, vectors)
+    )(x, w_qkv, w_out, vectors)
 
     feed_rows = ROWS - (ROW_OUT - 4) + plan.rows
-    out, grad_att, grad_mid, parts, first = pl.pallas_call(
-        feed_kernel(plan),
+    parts_shape = lambda deep: (PLANE, deep, plan.rows, LANES)
+    out, grad_att, grad_mid, keep, send, first = pl.pallas_call(
+        feed_kernel(plan, group),
         grid=(steps,),
         in_specs=[
             smem,
@@ -487,14 +501,14 @@
             grid_spec,
             token_spec(D),
             token_spec(D),
-            whole((CORES, PLANE, plan.deep - plan.lead, plan.rows, LANES)),
+            *[whole(parts_shape(plan.deep - plan.lead))] * CORES,
             whole((8, LANES)),
         ],
         out_shape=[
             shape((TALL, owned, D), BF16),
             shape((count, D), BF16),
             shape((count, D), F32),
-            shape((CORES, PLANE, plan.deep - plan.lead, plan.rows, LANES), BF16),
+            *[shape(parts_shape(plan.deep - plan.lead), BF16)] * CORES,
             shape((8, LANES), F32),
         ],
         scratch_shapes=[
@@ -514,21 +528,22 @@
 
     layer_out = to_rows(out)
 
-    def stages(value):
-        value = value[0].astype(F32) + swap_core(value[1]).astype(F32)
+    def core_sum(keep, send):
+        return keep.astype(F32) + swap_core(send).astype(F32)
+
+    def plane_sum(value):
         total = value[0]
         sent = value.astype(BF16)
         for k in range(1, PLANE):
             total = total + swap_seq(sent[k], k).astype(F32)
         return total
 
-    later = stages(parts)
-
-    grad_x, lead_parts = pl.pallas_call(
-        back_kernel(plan),
+    later = plane_sum(core_sum(keep, send))
+
+    grad_x, lead_keep, lead_send = pl.pallas_call(
+        attend_back_kernel(plan),
         grid=(steps,),
         in_specs=[
-            smem,
             smem,
             grid_spec,
             token_spec(3 * D),
@@ -539,10 +554,10 @@
             whole((D, 3 * D)),
             whole((8, D)),
         ],
-        out_specs=[grid_spec, whole((CORES, PLANE, plan.lead, plan.rows, LANES))],
+        out_specs=[grid_spec, *[whole(parts_shape(plan.lead))] * CORES],
         out_shape=[
             shape((TALL, owned, D), BF16),
-            shape((CORES, PLANE, plan.lead, plan.rows, LANES), BF16),
+            *[shape(parts_shape(plan.lead), BF16)] * CORES,
         ],
         scratch_shapes=[
             pltpu.VMEM((D, 3 * D), F32),
@@ -551,13 +566,15 @@
         ],
         compiler_params=params,
         cost_estimate=pl.CostEstimate(
-            flops=3 * 10**9, bytes_accessed=8 * 10**6, transcendentals=10**6
+            flops=10 * 10**9, bytes_accessed=8 * 10**6, transcendentals=10**6
         ),
-        name="back",
-    )(place, span, x, packed, logsum, grad_att, grad_mid, first, w_qkv, vectors)
-
+        name="attend_back",
+    )(place, x, packed, logsum, grad_att, grad_mid, first, w_qkv, vectors)
+    (grad_x, lead_keep, lead_send), layer_out, later = lax.optimization_barrier(
+        ((grad_x, lead_keep, lead_send), layer_out, later)
+    )
+    total = jnp.concatenate([plane_sum(core_sum(lead_keep, lead_send)), later], axis=0)
     input_grad = to_rows(grad_x).astype(F32)
-    total = jnp.concatenate([stages(lead_parts), later], axis=0)
     if plan.pairwise:
         sent = total.astype(BF16)
         result = lax.dynamic_index_in_dim(total, deep_at, 0, keepdims=False)

time: 141 us -> 119 us (0.84)
  waiting for transfers between devices: 50.4 us -> 31.8 us
  starting transfers between devices: 43.7 us -> 38.1 us
  local copies, waits for them, and re-layouts: 12.4 us -> 7.03 us
  Pallas kernels: 32.6 us -> 37.5 us
  other arithmetic: 0.7 us -> 3.01 us
    all_to_all x4, waiting for transfers between devices: 10.7 us -> 0.01 us  [exchange(): lax.all_to_all(blocks, 'seq', 0, 0, axis_index_groups=groups, tiled=True)]
    ppermute x15, waiting for transfers between devices: 39.4 us -> 29.6 us  [swap_seq(): return lax.ppermute(value, 'seq', [(i, i ^ distance) for i in range(seq)])]
    pallas_call x3 -> x5, Pallas kernels: 28.8 us -> 33.7 us  [the longest x1 13.5 us: local(): pl.pallas_call(feed_kernel(plan, group), grid=(steps,), in_specs=[smem, t...]
    all_to_all x4, starting transfers between devices: 19.7 us -> 15.8 us  [exchange(): lax.all_to_all(blocks, 'seq', 0, 0, axis_index_groups=groups, tiled=True)]
    reshape x2 -> x0, local copies, waits for them, and re-layouts: 3.09 us -> none  [to_columns(): cut = rows.reshape(local_rows, group, owned, D).transpose(1, 0, 2, 3)]
    ppermute x6, waiting for transfers between devices: 0.19 us -> 2.17 us  [swap_core(): return lax.ppermute(value, 'dp', [(0, 1), (1, 0)])]
    squeeze x5 -> x2, local copies, waits for them, and re-layouts: 1.62 us -> 0.05 us  [plane_sum(): total = total + swap_seq(sent[k], k).astype(F32)]
    unnamed x24 -> x28, local copies, waits for them, and re-layouts: 4.1 us -> 2.79 us
  transfers between devices with their start and end apart: 26 -> 25, of which waited for: 12 -> 12; matrix products, arithmetic and copies ran while one was open for 4% -> 2% of each run, Pallas kernels for 6% -> 20%
where the time goes in v2:
time: 119 us; the launch traced here: 118 us
  starting transfers between devices  38.1 us (32%)
  Pallas kernels  37.5 us (32%)
  waiting for transfers between devices  31.8 us (27%)
  local copies, waits for them, and re-layouts  7.03 us (6%)
  other arithmetic  3.01 us (3%)
    ppermute x15, waiting for transfers between devices, swap_seq(): return lax.ppermute(value, 'seq', [(i, i ^ distance) for i in range(seq)])  29.6 us
    ppermute x15, starting transfers between devices, swap_seq(): return lax.ppermute(value, 'seq', [(i, i ^ distance) for i in range(seq)])  20.9 us
    all_to_all x4, starting transfers between devices, exchange(): lax.all_to_all(blocks, 'seq', 0, 0, axis_index_groups=groups, tiled=True)  15.8 us
    pallas_call x1, Pallas kernels, local(): pl.pallas_call(feed_kernel(plan, group), grid=(steps,), in_specs=[smem, t...  13.5 us
    pallas_call x1, Pallas kernels, local(): pl.pallas_call(attend_back_kernel(plan), grid=(steps,), in_specs=[smem, g...  10.2 us
    pallas_call x1, Pallas kernels, local(): pl.pallas_call(forward_kernel, grid=(steps,), in_specs=[grid_spec, whole(...  5.84 us
    pallas_call x2, Pallas kernels, local(): pl.pallas_call(cut_rows_kernel(group, owned), out_shape=jax.ShapeDtypeStr...  4.12 us
    pallas_call x1, Pallas kernels, local(): w_qkv, w_out, w_in, w_back, vectors, bias_in = prepare(plan)(place, *pieces)  3.84 us
  transfers between devices with their start and end apart: 25, of which 12 were waited for; matrix products, arithmetic and copies ran while one was open for 2% of the time, Pallas kernels for 20%

profile of v2, /device:TPU:0, one launch (start us, length us, event | category | flops | bytes accessed | tf_op | source)
XLA Modules:
  0.0 118.4 jit_solution(6892481718465389151)
XLA Ops:
  2.5 3.1 %collective-permute-start = (bf16[208,128]{1,0:T(8,128)(2,1)S(1)}, bf16[208,128]{1,0:T(8,128)(2,1)S(1)}, u32[]{:S(2)}, u32[]{:S(2)}) collective-permute-start(bf16[208,128]{1,0:T(8,128)(2,1)S(1)} %bitcast.77), channel_id=1, source_target_pairs={{0,8},{2,10},{4,12},{6,14},{8,0},{10,2},{12,4},{14,6},{16,24},{18,... | collective-permute-start | bytes 159752 | tf_op jit(solution)/shard_map/ppermute | solution.py:423
  5.6 2.6 %collective-permute-start.1 = (bf16[208,128]{1,0:T(8,128)(2,1)S(1)}, bf16[208,128]{1,0:T(8,128)(2,1)S(1)}, u32[]{:S(2)}, u32[]{:S(2)}) collective-permute-start(bf16[208,128]{1,0:T(8,128)(2,1)S(1)} %bitcast.78), channel_id=1, source_target_pairs={{0,16},{2,18},{4,20},{6,22},{8,24},{10,26},{12,28},{14,30},{16,0},... | collective-permute-start | bytes 159752 | tf_op jit(solution)/shard_map/ppermute | solution.py:423
  8.2 2.1 %cut_tokens.1 = bf16[8,4,48,256]{3,2,1,0:T(8,128)(2,1)} custom-call(bf16[4,384,256]{2,1,0:T(8,128)(2,1)} %bitcast.70), custom_call_target="tpu_custom_call" | custom-call | tf_op jit(solution)/shard_map/cut_tokens/pallas_call | solution.py:438
  10.3 1.4 %collective-permute-done.1 = bf16[208,128]{1,0:T(8,128)(2,1)S(1)} collective-permute-done((bf16[208,128]{1,0:T(8,128)(2,1)S(1)}, bf16[208,128]{1,0:T(8,128)(2,1)S(1)}, u32[]{:S(2)}, u32[]{:S(2)}) %collective-permute-start.1) | collective-permute-done | bytes 53280 | tf_op jit(solution)/shard_map/ppermute | solution.py:423
  11.7 2.5 %collective-permute-done.2 = bf16[208,128]{1,0:T(8,128)(2,1)S(1)} collective-permute-done((bf16[208,128]{1,0:T(8,128)(2,1)S(1)}, bf16[208,128]{1,0:T(8,128)(2,1)S(1)}, u32[]{:S(2)}, u32[]{:S(2)}) %collective-permute-start.2) | collective-permute-done | bytes 53280 | tf_op jit(solution)/shard_map/ppermute | solution.py:423
  14.1 3.7 %all-to-all-start = ((bf16[8,4,48,256]{3,2,1,0:T(8,128)(2,1)}), bf16[8,4,48,256]{3,2,1,0:T(8,128)(2,1)S(1)}, u32[]{:S(2)}, u32[]{:S(2)}) async-start(bf16[8,4,48,256]{3,2,1,0:T(8,128)(2,1)} %cut_tokens.1), calls=%async_computation | async-start | bytes 1572864 | tf_op jit(solution)/shard_map/all_to_all | solution.py:416
  17.9 2.1 %collective-permute-start.3 = (bf16[4,208,128]{2,1,0:T(8,128)(2,1)S(1)}, bf16[4,208,128]{2,1,0:T(8,128)(2,1)S(1)}, u32[]{:S(2)}, u32[]{:S(2)}) collective-permute-start(bf16[4,208,128]{2,1,0:T(8,128)(2,1)S(1)} %pad_maximum_fusion.1.refs_0_), channel_id=1, source_target_pairs={{0,2},{2,0},{4,6},{6,4},{8,10},{10,8},{12,14},{14,12},{16,18},{18,... | collective-permute-start | bytes 638984 | tf_op jit(solution)/shard_map/ppermute | solution.py:423
  20.0 1.5 %collective-permute-start.4 = (bf16[4,208,128]{2,1,0:T(8,128)(2,1)S(1)}, bf16[4,208,128]{2,1,0:T(8,128)(2,1)S(1)}, u32[]{:S(2)}, u32[]{:S(2)}) collective-permute-start(bf16[4,208,128]{2,1,0:T(8,128)(2,1)S(1)} %pad_maximum_fusion.1.refs_0_), channel_id=1, source_target_pairs={{0,4},{2,6},{4,0},{6,2},{8,12},{10,14},{12,8},{14,10},{16,20},{18,... | collective-permute-start | bytes 638984 | tf_op jit(solution)/shard_map/ppermute | solution.py:423
  21.5 2.1 %cut_cotangent.1 = bf16[8,4,48,256]{3,2,1,0:T(8,128)(2,1)} custom-call(bf16[4,384,256]{2,1,0:T(8,128)(2,1)} %bitcast.71), custom_call_target="tpu_custom_call" | custom-call | tf_op jit(solution)/shard_map/cut_cotangent/pallas_call | solution.py:449
  23.6 10.1 %collective-permute-done.3.refs_1_ = bf16[4,208,128]{2,1,0:T(8,128)(2,1)S(1)} collective-permute-done((bf16[4,208,128]{2,1,0:T(8,128)(2,1)S(1)}, bf16[4,208,128]{2,1,0:T(8,128)(2,1)S(1)}, u32[]{:S(2)}, u32[]{:S(2)}) %collective-permute-start.3) | collective-permute-done | bytes 213024 | tf_op jit(solution)/shard_map/ppermute | solution.py:423
  33.7 3.4 %collective-permute-done.5.refs_3_ = bf16[4,208,128]{2,1,0:T(8,128)(2,1)S(1)} collective-permute-done((bf16[4,208,128]{2,1,0:T(8,128)(2,1)S(1)}, bf16[4,208,128]{2,1,0:T(8,128)(2,1)S(1)}, u32[]{:S(2)}, u32[]{:S(2)}) %collective-permute-start.5) | collective-permute-done | bytes 213024 | tf_op jit(solution)/shard_map/ppermute | solution.py:423
  37.1 3.6 %all-to-all-start.1 = ((bf16[8,4,48,256]{3,2,1,0:T(8,128)(2,1)}), bf16[8,4,48,256]{3,2,1,0:T(8,128)(2,1)S(1)}, u32[]{:S(2)}, u32[]{:S(2)}) async-start(bf16[8,4,48,256]{3,2,1,0:T(8,128)(2,1)} %cut_cotangent.1), calls=%async_computation.1 | async-start | bytes 1572864 | tf_op jit(solution)/shard_map/all_to_all | solution.py:416
  44.2 3.8 %prepare.1 = (bf16[256,768]{1,0:T(8,128)(2,1)}, bf16[256,256]{1,0:T(8,128)(2,1)}, bf16[256,1024]{1,0:T(8,128)(2,1)}, bf16[1024,256]{1,0:T(8,128)(2,1)}, f32[8,256]{1,0:T(8,128)}, /*index=5*/f32[8,1024]{1,0:T(8,128)}) custom-call(s32[4]{0:T(128)} %pad_add_fusion.place_ref, bf16[4,208,128]{2,1,0:T(8,128)(2,1)} %copy-done, bf16[4,208,128]{2,1,0:T(8,128)(2,1)} %copy-done.5, ...), custom_call_target="tpu_custom_call" | custom-call | tf_op jit(solution)/shard_map/prepare/pallas_call | solution.py:459
  48.1 5.8 %forward.1 = (bf16[1536,768]{1,0:T(8,128)(2,1)}, bf16[1536,256]{1,0:T(8,128)(2,1)}, f32[1536,256]{1,0:T(8,128)}, f32[3,8,256]{2,1,0:T(8,128)}) custom-call(bf16[32,48,256]{2,1,0:T(8,128)(2,1)} %bitcast.72, bf16[256,768]{1,0:T(8,128)(2,1)} %get-tuple-element.30.w_qkv, bf16[256,256]{1,0:T(8,128)(2,1)} %get-tuple-element.31.w_out.refs_0_, ...), custom_call_target="tpu_custom_call" | custom-call | flops 1000000000 | bytes 7000000 | tf_op jit(solution)/shard_map/forward/pallas_call | solution.py:466
  54.8 13.5 %feed.1 = (bf16[32,48,256]{2,1,0:T(8,128)(2,1)}, bf16[1536,256]{1,0:T(8,128)(2,1)}, f32[1536,256]{1,0:T(8,128)}, bf16[4,3,208,128]{3,2,1,0:T(8,128)(2,1)}, bf16[...) custom-call(s32[4]{0:T(128)} %pad_add_fusion.place_ref, f32[1536,256]{1,0:T(8,128)} %get-tuple-element.35.middle_ref, ...), custom_call_target="tpu_custom_call" | custom-call | flops 5000000000 | bytes 10000000 | tf_op jit(solution)/shard_map/feed/pallas_call | solution.py:486
  68.6 5.0 %all-to-all-start.2 = ((bf16[8,4,48,256]{3,2,1,0:T(8,128)(2,1)}), bf16[8,4,48,256]{3,2,1,0:T(8,128)(2,1)S(1)}, u32[]{:S(2)}, u32[]{:S(2)}) async-start(bf16[8,4,48,256]{3,2,1,0:T(8,128)(2,1)} %bitcast.76), calls=%async_computation.2 | async-start | bytes 1572864 | tf_op jit(solution)/shard_map/all_to_all | solution.py:416
  75.7 3.0 %collective-permute-start.13 = (bf16[3,208,128]{2,1,0:T(8,128)(2,1)S(1)}, bf16[3,208,128]{2,1,0:T(8,128)(2,1)S(1)}, u32[]{:S(2)}, u32[]{:S(2)}) collective-permute-start(bf16[3,208,128]{2,1,0:T(8,128)(2,1)S(1)} %get-tuple-element.58), channel_id=1, source_target_pairs={{0,6},{2,4},{4,2},{6,0},{8,14},{10,12},{12,10},{14,8},{16,22},{18,... | collective-permute-start | bytes 479240 | tf_op jit(solution)/shard_map/ppermute | solution.py:423
  79.3 10.2 %attend_back.1 = (bf16[32,48,256]{2,1,0:T(8,128)(2,1)}, bf16[4,1,208,128]{3,2,1,0:T(8,128)(2,1)}, bf16[4,1,208,128]{3,2,1,0:T(8,128)(2,1)}) custom-call(s32[4]{0:T(128)} %pad_add_fusion.place_ref, bf16[32,48,256]{2,1,0:T(8,128)(2,1)} %bitcast.73, bf16[1536,768]{1,0:T(8,128)(2,1)} %get-tuple-element.33.packed_ref, f32[3,8,256]{2,1,0:T(8,128)} %get-tuple-element.34.logsum_ref, ...), custom_call_target="tpu_custom_call" | custom-call | flops 10000000000 | bytes 8000000 | tf_op jit(solution)/shard_map/attend_back/pallas_call | solution.py:543
  90.1 2.4 %collective-permute-done.12 = bf16[3,208,128]{2,1,0:T(8,128)(2,1)S(1)} collective-permute-done((bf16[3,208,128]{2,1,0:T(8,128)(2,1)S(1)}, bf16[3,208,128]{2,1,0:T(8,128)(2,1)S(1)}, u32[]{:S(2)}, u32[]{:S(2)}) %collective-permute-start.12) | collective-permute-done | bytes 159776 | tf_op jit(solution)/shard_map/ppermute | solution.py:423
  93.5 1.5 %collective-permute-done.14 = bf16[4,1,208,128]{3,2,1,0:T(8,128)(2,1)S(1)} collective-permute-done((bf16[4,1,208,128]{3,2,1,0:T(8,128)(2,1)S(1)}, bf16[4,1,208,128]{3,2,1,0:T(8,128)(2,1)S(1)}, u32[]{:S(2)}, u32[]{:S(2)}) %collective-permute-start.14) | collective-permute-done | bytes 213024 | tf_op jit(solution)/shard_map/ppermute | solution.py:426
  97.2 1.4 %collective-permute-start.15 = (bf16[1,208,128]{2,1,0:T(8,128)(2,1)S(1)}, bf16[1,208,128]{2,1,0:T(8,128)(2,1)S(1)}, u32[]{:S(2)}, u32[]{:S(2)}) collective-permute-start(bf16[1,208,128]{2,1,0:T(8,128)(2,1)S(1)} %get-tuple-element.65), channel_id=1, source_target_pairs={{0,2},{2,0},{4,6},{6,4},{8,10},{10,8},{12,14},{14,12},{16,18},{18,... | collective-permute-start | bytes 159752 | tf_op jit(solution)/shard_map/ppermute | solution.py:423
  98.6 3.5 %all-to-all-start.3 = ((bf16[8,4,48,256]{3,2,1,0:T(8,128)(2,1)}), bf16[8,4,48,256]{3,2,1,0:T(8,128)(2,1)S(1)}, u32[]{:S(2)}, u32[]{:S(2)}) async-start(bf16[8,4,48,256]{3,2,1,0:T(8,128)(2,1)} %bitcast.21), calls=%async_computation.3 | async-start | bytes 1572864 | tf_op jit(solution)/shard_map/all_to_all | solution.py:416
  102.3 2.3 %collective-permute-start.20 = (bf16[208,128]{1,0:T(8,128)(2,1)S(1)}, bf16[208,128]{1,0:T(8,128)(2,1)S(1)}, u32[]{:S(2)}, u32[]{:S(2)}) collective-permute-start(bf16[208,128]{1,0:T(8,128)(2,1)S(1)} %get-tuple-element.63), channel_id=1, source_target_pairs={{0,24},{2,26},{4,28},{6,30},{8,16},{10,18},{12,20},{14,22},{16,8},... | collective-permute-start | bytes 159752 | tf_op jit(solution)/shard_map/ppermute | solution.py:423
  106.8 8.7 %collective-permute-done.20 = bf16[208,128]{1,0:T(8,128)(2,1)S(1)} collective-permute-done((bf16[208,128]{1,0:T(8,128)(2,1)S(1)}, bf16[208,128]{1,0:T(8,128)(2,1)S(1)}, u32[]{:S(2)}, u32[]{:S(2)}) %collective-permute-start.20) | collective-permute-done | bytes 53280 | tf_op jit(solution)/shard_map/ppermute | solution.py:423
  (79 shorter events, 18.3 us)
Async XLA Ops:
  2.5 7.7 %collective-permute-start = (bf16[208,128]{1,0:T(8,128)(2,1)S(1)}, bf16[208,128]{1,0:T(8,128)(2,1)S(1)}, u32[]{:S(2)}, u32[]{:S(2)}) collective-permute-start(bf16[208,128]{1,0:T(8,128)(2,1)S(1)} %bitcast.77), channel_id=1, source_target_pairs={{0,8},{2,10},{4,12},{6,14},{8,0},{10,2},{12,4},{14,6},{16,24},{18,... | collective-permute-start | bytes 159752 | tf_op jit(solution)/shard_map/ppermute | solution.py:423
  5.6 6.1 %collective-permute-start.1 = (bf16[208,128]{1,0:T(8,128)(2,1)S(1)}, bf16[208,128]{1,0:T(8,128)(2,1)S(1)}, u32[]{:S(2)}, u32[]{:S(2)}) collective-permute-start(bf16[208,128]{1,0:T(8,128)(2,1)S(1)} %bitcast.78), channel_id=1, source_target_pairs={{0,16},{2,18},{4,20},{6,22},{8,24},{10,26},{12,28},{14,30},{16,0},... | collective-permute-start | bytes 159752 | tf_op jit(solution)/shard_map/ppermute | solution.py:423
  8.2 5.9 %collective-permute-start.2 = (bf16[208,128]{1,0:T(8,128)(2,1)S(1)}, bf16[208,128]{1,0:T(8,128)(2,1)S(1)}, u32[]{:S(2)}, u32[]{:S(2)}) collective-permute-start(bf16[208,128]{1,0:T(8,128)(2,1)S(1)} %bitcast.79), channel_id=1, source_target_pairs={{0,24},{2,26},{4,28},{6,30},{8,16},{10,18},{12,20},{14,22},{16,8},... | collective-permute-start | bytes 159752 | tf_op jit(solution)/shard_map/ppermute | solution.py:423
  14.1 23.0 %all-to-all-start = ((bf16[8,4,48,256]{3,2,1,0:T(8,128)(2,1)}), bf16[8,4,48,256]{3,2,1,0:T(8,128)(2,1)S(1)}, u32[]{:S(2)}, u32[]{:S(2)}) async-start(bf16[8,4,48,256]{3,2,1,0:T(8,128)(2,1)} %cut_tokens.1), calls=%async_computation | async-start | bytes 1572864 | tf_op jit(solution)/shard_map/all_to_all | solution.py:416
  17.9 15.8 %collective-permute-start.3 = (bf16[4,208,128]{2,1,0:T(8,128)(2,1)S(1)}, bf16[4,208,128]{2,1,0:T(8,128)(2,1)S(1)}, u32[]{:S(2)}, u32[]{:S(2)}) collective-permute-start(bf16[4,208,128]{2,1,0:T(8,128)(2,1)S(1)} %pad_maximum_fusion.1.refs_0_), channel_id=1, source_target_pairs={{0,2},{2,0},{4,6},{6,4},{8,10},{10,8},{12,14},{14,12},{16,18},{18,... | collective-permute-start | bytes 638984 | tf_op jit(solution)/shard_map/ppermute | solution.py:423
  20.0 13.7 %collective-permute-start.4 = (bf16[4,208,128]{2,1,0:T(8,128)(2,1)S(1)}, bf16[4,208,128]{2,1,0:T(8,128)(2,1)S(1)}, u32[]{:S(2)}, u32[]{:S(2)}) collective-permute-start(bf16[4,208,128]{2,1,0:T(8,128)(2,1)S(1)} %pad_maximum_fusion.1.refs_0_), channel_id=1, source_target_pairs={{0,4},{2,6},{4,0},{6,2},{8,12},{10,14},{12,8},{14,10},{16,20},{18,... | collective-permute-start | bytes 638984 | tf_op jit(solution)/shard_map/ppermute | solution.py:423
  21.5 15.6 %collective-permute-start.5 = (bf16[4,208,128]{2,1,0:T(8,128)(2,1)S(1)}, bf16[4,208,128]{2,1,0:T(8,128)(2,1)S(1)}, u32[]{:S(2)}, u32[]{:S(2)}) collective-permute-start(bf16[4,208,128]{2,1,0:T(8,128)(2,1)S(1)} %pad_maximum_fusion.1.refs_0_), channel_id=1, source_target_pairs={{0,6},{2,4},{4,2},{6,0},{8,14},{10,12},{12,10},{14,8},{16,22},{18,... | collective-permute-start | bytes 638984 | tf_op jit(solution)/shard_map/ppermute | solution.py:423
  37.1 16.8 %all-to-all-start.1 = ((bf16[8,4,48,256]{3,2,1,0:T(8,128)(2,1)}), bf16[8,4,48,256]{3,2,1,0:T(8,128)(2,1)S(1)}, u32[]{:S(2)}, u32[]{:S(2)}) async-start(bf16[8,4,48,256]{3,2,1,0:T(8,128)(2,1)} %cut_cotangent.1), calls=%async_computation.1 | async-start | bytes 1572864 | tf_op jit(solution)/shard_map/all_to_all | solution.py:416
  40.7 1.7 %collective-permute-start.6 = (bf16[4,208,128]{2,1,0:T(8,128)(2,1)S(1)}, bf16[4,208,128]{2,1,0:T(8,128)(2,1)S(1)}, u32[]{:S(2)}, u32[]{:S(2)}) collective-permute-start(bf16[4,208,128]{2,1,0:T(8,128)(2,1)S(1)} %pad_maximum_fusion.1.refs_0_), channel_id=1, source_target_pairs={{0,1},{1,0},{2,3},{3,2},{4,5},{5,4},{6,7},{7,6},{8,9},{9,8},{10,11... | collective-permute-start | bytes 638984 | tf_op jit(solution)/shard_map/ppermute | solution.py:426
  40.8 1.8 %collective-permute-start.7 = (bf16[4,208,128]{2,1,0:T(8,128)(2,1)S(1)}, bf16[4,208,128]{2,1,0:T(8,128)(2,1)S(1)}, u32[]{:S(2)}, u32[]{:S(2)}) collective-permute-start(bf16[4,208,128]{2,1,0:T(8,128)(2,1)S(1)} %collective-permute-done.3.refs_1_), channel_id=1, source_target_pairs={{0,1},{1,0},{2,3},{3,2},{4,5},{5,4},{6,7},{7,6},{8,9},{9,8},{10,11... | collective-permute-start | bytes 638984 | tf_op jit(solution)/shard_map/ppermute | solution.py:426
  41.3 1.6 %collective-permute-start.8 = (bf16[4,208,128]{2,1,0:T(8,128)(2,1)S(1)}, bf16[4,208,128]{2,1,0:T(8,128)(2,1)S(1)}, u32[]{:S(2)}, u32[]{:S(2)}) collective-permute-start(bf16[4,208,128]{2,1,0:T(8,128)(2,1)S(1)} %collective-permute-done.4.refs_2_), channel_id=1, source_target_pairs={{0,1},{1,0},{2,3},{3,2},{4,5},{5,4},{6,7},{7,6},{8,9},{9,8},{10,11... | collective-permute-start | bytes 638984 | tf_op jit(solution)/shard_map/ppermute | solution.py:426
  41.3 1.8 %collective-permute-start.9 = (bf16[4,208,128]{2,1,0:T(8,128)(2,1)S(1)}, bf16[4,208,128]{2,1,0:T(8,128)(2,1)S(1)}, u32[]{:S(2)}, u32[]{:S(2)}) collective-permute-start(bf16[4,208,128]{2,1,0:T(8,128)(2,1)S(1)} %collective-permute-done.5.refs_3_), channel_id=1, source_target_pairs={{0,1},{1,0},{2,3},{3,2},{4,5},{5,4},{6,7},{7,6},{8,9},{9,8},{10,11... | collective-permute-start | bytes 638984 | tf_op jit(solution)/shard_map/ppermute | solution.py:426
  68.3 5.2 %collective-permute-start.10 = (bf16[4,3,208,128]{3,2,1,0:T(8,128)(2,1)}, bf16[4,3,208,128]{3,2,1,0:T(8,128)(2,1)S(1)}, u32[]{:S(2)}, u32[]{:S(2)}) collective-permute-start(bf16[4,3,208,128]{3,2,1,0:T(8,128)(2,1)} %get-tuple-element.49), channel_id=1, source_target_pairs={{0,1},{1,0},{2,3},{3,2},{4,5},{5,4},{6,7},{7,6},{8,9},{9,8},{10,11... | collective-permute-start | bytes 1916936 | tf_op jit(solution)/shard_map/ppermute | solution.py:426
  68.6 24.0 %all-to-all-start.2 = ((bf16[8,4,48,256]{3,2,1,0:T(8,128)(2,1)}), bf16[8,4,48,256]{3,2,1,0:T(8,128)(2,1)S(1)}, u32[]{:S(2)}, u32[]{:S(2)}) async-start(bf16[8,4,48,256]{3,2,1,0:T(8,128)(2,1)} %bitcast.76), calls=%async_computation.2 | async-start | bytes 1572864 | tf_op jit(solution)/shard_map/all_to_all | solution.py:416
  75.7 14.4 %collective-permute-start.13 = (bf16[3,208,128]{2,1,0:T(8,128)(2,1)S(1)}, bf16[3,208,128]{2,1,0:T(8,128)(2,1)S(1)}, u32[]{:S(2)}, u32[]{:S(2)}) collective-permute-start(bf16[3,208,128]{2,1,0:T(8,128)(2,1)S(1)} %get-tuple-element.58), channel_id=1, source_target_pairs={{0,6},{2,4},{4,2},{6,0},{8,14},{10,12},{12,10},{14,8},{16,22},{18,... | collective-permute-start | bytes 479240 | tf_op jit(solution)/shard_map/ppermute | solution.py:423
  78.7 13.8 %collective-permute-start.12 = (bf16[3,208,128]{2,1,0:T(8,128)(2,1)S(1)}, bf16[3,208,128]{2,1,0:T(8,128)(2,1)S(1)}, u32[]{:S(2)}, u32[]{:S(2)}) collective-permute-start(bf16[3,208,128]{2,1,0:T(8,128)(2,1)S(1)} %get-tuple-element.59), channel_id=1, source_target_pairs={{0,4},{2,6},{4,0},{6,2},{8,12},{10,14},{12,8},{14,10},{16,20},{18,... | collective-permute-start | bytes 479240 | tf_op jit(solution)/shard_map/ppermute | solution.py:423
  79.2 13.2 %collective-permute-start.11 = (bf16[3,208,128]{2,1,0:T(8,128)(2,1)S(1)}, bf16[3,208,128]{2,1,0:T(8,128)(2,1)S(1)}, u32[]{:S(2)}, u32[]{:S(2)}) collective-permute-start(bf16[3,208,128]{2,1,0:T(8,128)(2,1)S(1)} %get-tuple-element.57), channel_id=1, source_target_pairs={{0,2},{2,0},{4,6},{6,4},{8,10},{10,8},{12,14},{14,12},{16,18},{18,... | collective-permute-start | bytes 479240 | tf_op jit(solution)/shard_map/ppermute | solution.py:423
  95.1 7.1 %collective-permute-start.17 = (bf16[1,208,128]{2,1,0:T(8,128)(2,1)S(1)}, bf16[1,208,128]{2,1,0:T(8,128)(2,1)S(1)}, u32[]{:S(2)}, u32[]{:S(2)}) collective-permute-start(bf16[1,208,128]{2,1,0:T(8,128)(2,1)S(1)} %get-tuple-element.66), channel_id=1, source_target_pairs={{0,6},{2,4},{4,2},{6,0},{8,14},{10,12},{12,10},{14,8},{16,22},{18,... | collective-permute-start | bytes 159752 | tf_op jit(solution)/shard_map/ppermute | solution.py:423
  95.9 6.3 %collective-permute-start.16 = (bf16[1,208,128]{2,1,0:T(8,128)(2,1)S(1)}, bf16[1,208,128]{2,1,0:T(8,128)(2,1)S(1)}, u32[]{:S(2)}, u32[]{:S(2)}) collective-permute-start(bf16[1,208,128]{2,1,0:T(8,128)(2,1)S(1)} %get-tuple-element.67), channel_id=1, source_target_pairs={{0,4},{2,6},{4,0},{6,2},{8,12},{10,14},{12,8},{14,10},{16,20},{18,... | collective-permute-start | bytes 159752 | tf_op jit(solution)/shard_map/ppermute | solution.py:423
  97.2 5.0 %collective-permute-start.15 = (bf16[1,208,128]{2,1,0:T(8,128)(2,1)S(1)}, bf16[1,208,128]{2,1,0:T(8,128)(2,1)S(1)}, u32[]{:S(2)}, u32[]{:S(2)}) collective-permute-start(bf16[1,208,128]{2,1,0:T(8,128)(2,1)S(1)} %get-tuple-element.65), channel_id=1, source_target_pairs={{0,2},{2,0},{4,6},{6,4},{8,10},{10,8},{12,14},{14,12},{16,18},{18,... | collective-permute-start | bytes 159752 | tf_op jit(solution)/shard_map/ppermute | solution.py:423
  98.6 18.3 %all-to-all-start.3 = ((bf16[8,4,48,256]{3,2,1,0:T(8,128)(2,1)}), bf16[8,4,48,256]{3,2,1,0:T(8,128)(2,1)S(1)}, u32[]{:S(2)}, u32[]{:S(2)}) async-start(bf16[8,4,48,256]{3,2,1,0:T(8,128)(2,1)} %bitcast.21), calls=%async_computation.3 | async-start | bytes 1572864 | tf_op jit(solution)/shard_map/all_to_all | solution.py:416
  102.3 13.1 %collective-permute-start.20 = (bf16[208,128]{1,0:T(8,128)(2,1)S(1)}, bf16[208,128]{1,0:T(8,128)(2,1)S(1)}, u32[]{:S(2)}, u32[]{:S(2)}) collective-permute-start(bf16[208,128]{1,0:T(8,128)(2,1)S(1)} %get-tuple-element.63), channel_id=1, source_target_pairs={{0,24},{2,26},{4,28},{6,30},{8,16},{10,18},{12,20},{14,22},{16,8},... | collective-permute-start | bytes 159752 | tf_op jit(solution)/shard_map/ppermute | solution.py:423
  104.6 10.8 %collective-permute-start.19 = (bf16[208,128]{1,0:T(8,128)(2,1)S(1)}, bf16[208,128]{1,0:T(8,128)(2,1)S(1)}, u32[]{:S(2)}, u32[]{:S(2)}) collective-permute-start(bf16[208,128]{1,0:T(8,128)(2,1)S(1)} %get-tuple-element.64), channel_id=1, source_target_pairs={{0,16},{2,18},{4,20},{6,22},{8,24},{10,26},{12,28},{14,30},{16,0},... | collective-permute-start | bytes 159752 | tf_op jit(solution)/shard_map/ppermute | solution.py:423
  105.8 10.3 %collective-permute-start.18 = (bf16[208,128]{1,0:T(8,128)(2,1)S(1)}, bf16[208,128]{1,0:T(8,128)(2,1)S(1)}, u32[]{:S(2)}, u32[]{:S(2)}) collective-permute-start(bf16[208,128]{1,0:T(8,128)(2,1)S(1)} %get-tuple-element.62), channel_id=1, source_target_pairs={{0,8},{2,10},{4,12},{6,14},{8,0},{10,2},{12,4},{14,6},{16,24},{18,... | collective-permute-start | bytes 159752 | tf_op jit(solution)/shard_map/ppermute | solution.py:423
  (15 other events, 80.1 us)

commit v3 on v2

--- a/solution.py
+++ b/solution.py
@@ -63,6 +63,10 @@
     return jnp.concatenate(
         [flat[:TILE].reshape(TALL, HALF, width), flat[TILE:].reshape(TALL, HALF, width)], axis=1
     )
+
+
+def read_block(ref):
+    return to_tokens(ref[...].reshape(TALL, BLOCK, D).astype(F32))
 
 
 def center(value):
@@ -171,6 +175,7 @@
             pltpu.SemaphoreType.DMA((plan.count,)),
         ],
         compiler_params=pltpu.CompilerParams(vmem_limit_bytes=VMEM_BYTES),
+        cost_estimate=pl.CostEstimate(flops=25500000000, bytes_accessed=4 * 10**6, transcendentals=0),
         name="prepare",
     )
 
@@ -178,7 +183,7 @@
 def forward_kernel(
     x_ref, w_qkv, w_out, vectors, packed_ref, attended_ref, middle_ref, logsum_ref
 ):
-    x = to_tokens(x_ref[...].astype(F32))
+    x = read_block(x_ref)
     hat, _ = center(x)
     normed = (hat * vectors[0:1] + vectors[1:2]).astype(BF16)
     packed = nn(normed, w_qkv[...]).astype(BF16)
@@ -231,7 +236,7 @@
         middle = middle_ref[...]
         hat, inverse = center(middle)
         normed = (hat * vectors[2:3] + vectors[3:4]).astype(BF16)
-        cot_wide = to_tokens(cot_ref[...].astype(F32))
+        cot_wide = read_block(cot_ref)
         cot = cot_wide.astype(BF16)
         out = middle + vectors[4:5]
         grad_normed = jnp.zeros((TOKENS, D), F32)
@@ -347,7 +352,7 @@
                 pieces[2].append(nn(probs.astype(BF16), grad).astype(BF16))
             tiles.append(jnp.concatenate(pieces[0] + pieces[1] + pieces[2], axis=1))
         grad_packed = jnp.concatenate(tiles, axis=0)
-        hat, inverse = center(to_tokens(x_ref[...].astype(F32)))
+        hat, inverse = center(read_block(x_ref))
         normed = (hat * vectors[0:1] + vectors[1:2]).astype(BF16)
         acc_qkv[...] += tn(normed, grad_packed)
         grad_normed = nt(grad_packed, w_qkv[...])
@@ -370,19 +375,13 @@
     return kernel
 
 
-def cut_rows_kernel(group, owned):
-    def kernel(rows_ref, out_ref):
-        for index in range(group):
-            out_ref[index] = rows_ref[:, index * owned : (index + 1) * owned]
-
-    return kernel
-
-
-def cut_pieces_kernel(group, owned):
-    def kernel(place_ref, rows_ref, *pieces):
-        for index, piece in enumerate(pieces):
-            column = pl.multiple_of((index ^ place_ref[3]) * owned, 16)
-            piece[...] = rows_ref[:, pl.ds(column, owned)]
+def cut_kernel(group, steps):
+    def kernel(rows_ref, cot_ref, out_ref):
+        for member in range(group):
+            for step in range(steps):
+                column = (member * steps + step) * BLOCK
+                for kind, ref in enumerate((rows_ref, cot_ref)):
+                    out_ref[member, step, kind] = ref[:, column : column + BLOCK]
 
     return kernel
 
@@ -435,38 +434,32 @@
         arrived = [own]
         deep = lax.all_gather(own, "seq", axis=0, axis_index_groups=deep_groups)
     vmem = pl.BlockSpec(memory_space=pltpu.VMEM)
-    x_cut = pl.pallas_call(
-        cut_rows_kernel(group, owned),
-        out_shape=jax.ShapeDtypeStruct((group, local_rows, owned, D), BF16),
-        in_specs=[vmem],
+    both = pl.pallas_call(
+        cut_kernel(group, steps),
+        out_shape=jax.ShapeDtypeStruct((group, steps, 2, local_rows, BLOCK, D), BF16),
+        in_specs=[vmem, vmem],
         out_specs=vmem,
-        name="cut_tokens",
-    )(tokens.reshape(local_rows, columns, D))
-    x_cut, _ = lax.optimization_barrier((x_cut, arrived))
-    x = exchange(x_cut).reshape(TALL, owned, D)
+        compiler_params=pltpu.CompilerParams(vmem_limit_bytes=VMEM_BYTES),
+        name="cut",
+    )(tokens.reshape(local_rows, columns, D), cotangent.reshape(local_rows, columns, D))
+    deep, both = lax.optimization_barrier((deep, both))
+    both = exchange(both)
     plane = [deep] + [swap_seq(deep, k) for k in range(1, PLANE)]
     pieces = plane + [swap_core(piece) for piece in plane]
-    cot_cut = pl.pallas_call(
-        cut_rows_kernel(group, owned),
-        out_shape=jax.ShapeDtypeStruct((group, local_rows, owned, D), BF16),
-        in_specs=[vmem],
-        out_specs=vmem,
-        name="cut_cotangent",
-    )(cotangent.reshape(local_rows, columns, D))
-    cot_cut, _ = lax.optimization_barrier((cot_cut, (x, plane[1:])))
-    cot = exchange(cot_cut).reshape(TALL, owned, D)
-
     w_qkv, w_out, w_in, w_back, vectors, bias_in = prepare(plan)(place, *pieces)
 
     count = TALL * owned
     token_spec = lambda width: pl.BlockSpec((TOKENS, width), lambda step: (step, 0))
     grid_spec = pl.BlockSpec((TALL, BLOCK, D), lambda step: (0, step, 0))
+    moved = (group, 1, 1, local_rows, BLOCK, D)
+    x_spec = pl.BlockSpec(moved, lambda step: (0, step, 0, 0, 0, 0))
+    cot_spec = pl.BlockSpec(moved, lambda step: (0, step, 1, 0, 0, 0))
     logsum_spec = pl.BlockSpec((1, 8, TILE), lambda step: (step, 0, 0))
     shape = jax.ShapeDtypeStruct
     packed, attended, middle, logsum = pl.pallas_call(
         forward_kernel,
         grid=(steps,),
-        in_specs=[grid_spec, whole((D, 3 * D)), whole((D, D)), whole((8, D))],
+        in_specs=[x_spec, whole((D, 3 * D)), whole((D, D)), whole((8, D))],
         out_specs=[token_spec(3 * D), token_spec(D), token_spec(D), logsum_spec],
         out_shape=[
             shape((count, 3 * D), BF16),
@@ -479,7 +472,7 @@
             flops=10**9, bytes_accessed=7 * 10**6, transcendentals=10**6
         ),
         name="forward",
-    )(x, w_qkv, w_out, vectors)
+    )(both, w_qkv, w_out, vectors)
 
     feed_rows = ROWS - (ROW_OUT - 4) + plan.rows
     parts_shape = lambda deep: (PLANE, deep, plan.rows, LANES)
@@ -490,7 +483,7 @@
             smem,
             token_spec(D),
             token_spec(D),
-            grid_spec,
+            cot_spec,
             whole((D, D)),
             whole((D, FF)),
             whole((FF, D)),
@@ -524,7 +517,7 @@
             flops=5 * 10**9, bytes_accessed=10**7, transcendentals=2 * 10**6
         ),
         name="feed",
-    )(place, middle, attended, cot, w_out, w_in, w_back, vectors, bias_in)
+    )(place, middle, attended, both, w_out, w_in, w_back, vectors, bias_in)
 
     layer_out = to_rows(out)
 
@@ -545,7 +538,7 @@
         grid=(steps,),
         in_specs=[
             smem,
-            grid_spec,
+            x_spec,
             token_spec(3 * D),
             logsum_spec,
             token_spec(D),
@@ -569,12 +562,14 @@
             flops=10 * 10**9, bytes_accessed=8 * 10**6, transcendentals=10**6
         ),
         name="attend_back",
-    )(place, x, packed, logsum, grad_att, grad_mid, first, w_qkv, vectors)
-    (grad_x, lead_keep, lead_send), layer_out, later = lax.optimization_barrier(
-        ((grad_x, lead_keep, lead_send), layer_out, later)
+    )(place, both, packed, logsum, grad_att, grad_mid, first, w_qkv, vectors)
+    (lead_keep, lead_send), layer_out, later = lax.optimization_barrier(
+        ((lead_keep, lead_send), layer_out, later)
     )
     total = jnp.concatenate([plane_sum(core_sum(lead_keep, lead_send)), later], axis=0)
-    input_grad = to_rows(grad_x).astype(F32)
+    moved_x = exchange(grad_x.reshape(group, local_rows, owned, D))
+    total, moved_x = lax.optimization_barrier((total, moved_x))
+    input_grad = moved_x.transpose(1, 0, 2, 3).reshape(tokens.shape).astype(F32)
     if plan.pairwise:
         sent = total.astype(BF16)
         result = lax.dynamic_index_in_dim(total, deep_at, 0, keepdims=False)

time: 119 us -> 111 us (0.933)
  waiting for transfers between devices: 31.8 us -> 27 us
  starting transfers between devices: 38.1 us -> 34.4 us
  Pallas kernels: 37.5 us -> 36.2 us
  local copies, waits for them, and re-layouts: 7.03 us -> 8.32 us
    ppermute x15, waiting for transfers between devices: 29.6 us -> 22.6 us  [swap_seq(): return lax.ppermute(value, 'seq', [(i, i ^ distance) for i in range(seq)])]
    all_to_all x4 -> x3, starting transfers between devices: 15.8 us -> 13.4 us  [exchange(): lax.all_to_all(blocks, 'seq', 0, 0, axis_index_groups=groups, tiled=True)]
    all_to_all x4 -> x3, waiting for transfers between devices: 0.01 us -> 2.15 us  [exchange(): lax.all_to_all(blocks, 'seq', 0, 0, axis_index_groups=groups, tiled=True)]
    pallas_call x4 -> x3, Pallas kernels: 20.2 us -> 18.8 us  [the longest x1 10.4 us: local(): pl.pallas_call(attend_back_kernel(plan), grid=(steps,), in_specs=[smem, x...]
    ppermute x6, starting transfers between devices: 1.35 us -> 0.15 us  [swap_core(): return lax.ppermute(value, 'dp', [(0, 1), (1, 0)])]
  transfers between devices with their start and end apart: 25 -> 24, of which waited for: 12 -> 11; matrix products, arithmetic and copies ran while one was open for 2% -> 6% of each run, Pallas kernels for 20% -> 15%
where the time goes in v3:
time: 111 us
  Pallas kernels  36.2 us (33%)
  starting transfers between devices  34.4 us (31%)
  waiting for transfers between devices  27 us (24%)
  local copies, waits for them, and re-layouts  8.32 us (7%)
  other arithmetic  3.9 us (4%)
    ppermute x15, waiting for transfers between devices, swap_seq(): return lax.ppermute(value, 'seq', [(i, i ^ distance) for i in range(seq)])  22.6 us
    ppermute x15, starting transfers between devices, swap_seq(): return lax.ppermute(value, 'seq', [(i, i ^ distance) for i in range(seq)])  20.9 us
    pallas_call x1, Pallas kernels, local(): pl.pallas_call(feed_kernel(plan, group), grid=(steps,), in_specs=[smem, t...  13.5 us
    all_to_all x3, starting transfers between devices, exchange(): lax.all_to_all(blocks, 'seq', 0, 0, axis_index_groups=groups, tiled=True)  13.4 us
    pallas_call x1, Pallas kernels, local(): pl.pallas_call(attend_back_kernel(plan), grid=(steps,), in_specs=[smem, x...  10.4 us
    pallas_call x1, Pallas kernels, local(): pl.pallas_call(forward_kernel, grid=(steps,), in_specs=[x_spec, whole((D,...  5.82 us
    pallas_call x1, Pallas kernels, local(): w_qkv, w_out, w_in, w_back, vectors, bias_in = prepare(plan)(place, *pieces)  3.84 us
    unnamed x28, local copies, waits for them, and re-layouts  3.37 us
  transfers between devices with their start and end apart: 24, of which 11 were waited for; matrix products, arithmetic and copies ran while one was open for 6% of the time, Pallas kernels for 15%

profile of v3, /device:TPU:0, one launch (start us, length us, event | category | flops | bytes accessed | tf_op | source)
XLA Modules:
  0.0 110.8 jit_solution(14277813691618350665)
XLA Ops:
  2.5 5.1 %collective-permute-start.2 = (bf16[208,128]{1,0:T(8,128)(2,1)S(1)}, bf16[208,128]{1,0:T(8,128)(2,1)S(1)}, u32[]{:S(2)}, u32[]{:S(2)}) collective-permute-start(bf16[208,128]{1,0:T(8,128)(2,1)S(1)} %bitcast.71), channel_id=1, source_target_pairs={{0,24},{2,26},{4,28},{6,30},{8,16},{10,18},{12,20},{14,22},{16,8},... | collective-permute-start | bytes 159752 | tf_op jit(solution)/shard_map/ppermute | solution.py:422
  8.3 2.6 %cut.1 = bf16[8,3,2,4,16,256]{5,4,3,2,1,0:T(8,128)(2,1)} custom-call(bf16[4,384,256]{2,1,0:T(8,128)(2,1)} %bitcast.69, bf16[4,384,256]{2,1,0:T(8,128)(2,1)} %bitcast.70), custom_call_target="tpu_custom_call" | custom-call | tf_op jit(solution)/shard_map/cut/pallas_call | solution.py:437
  10.9 1.8 %collective-permute-done.1 = bf16[208,128]{1,0:T(8,128)(2,1)S(1)} collective-permute-done((bf16[208,128]{1,0:T(8,128)(2,1)S(1)}, bf16[208,128]{1,0:T(8,128)(2,1)S(1)}, u32[]{:S(2)}, u32[]{:S(2)}) %collective-permute-start.1) | collective-permute-done | bytes 53280 | tf_op jit(solution)/shard_map/ppermute | solution.py:422
  12.7 1.6 %collective-permute-start.3 = (bf16[4,208,128]{2,1,0:T(8,128)(2,1)S(1)}, bf16[4,208,128]{2,1,0:T(8,128)(2,1)S(1)}, u32[]{:S(2)}, u32[]{:S(2)}) collective-permute-start(bf16[4,208,128]{2,1,0:T(8,128)(2,1)S(1)} %pad_maximum_fusion.1.refs_0_), channel_id=1, source_target_pairs={{0,2},{2,0},{4,6},{6,4},{8,10},{10,8},{12,14},{14,12},{16,18},{18,... | collective-permute-start | bytes 638984 | tf_op jit(solution)/shard_map/ppermute | solution.py:422
  14.3 1.5 %collective-permute-start.4 = (bf16[4,208,128]{2,1,0:T(8,128)(2,1)S(1)}, bf16[4,208,128]{2,1,0:T(8,128)(2,1)S(1)}, u32[]{:S(2)}, u32[]{:S(2)}) collective-permute-start(bf16[4,208,128]{2,1,0:T(8,128)(2,1)S(1)} %pad_maximum_fusion.1.refs_0_), channel_id=1, source_target_pairs={{0,4},{2,6},{4,0},{6,2},{8,12},{10,14},{12,8},{14,10},{16,20},{18,... | collective-permute-start | bytes 638984 | tf_op jit(solution)/shard_map/ppermute | solution.py:422
  16.3 4.0 %all-to-all-start = ((bf16[8,3,2,4,16,256]{5,4,3,2,1,0:T(8,128)(2,1)}), bf16[8,3,2,4,16,256]{5,4,3,2,1,0:T(8,128)(2,1)S(1)}, u32[]{:S(2)}, u32[]{:S(2)}) async-start(bf16[8,3,2,4,16,256]{5,4,3,2,1,0:T(8,128)(2,1)} %cut.1), calls=%async_computation | async-start | bytes 3145728 | tf_op jit(solution)/shard_map/all_to_all | solution.py:415
  21.0 6.2 %collective-permute-done.4.refs_2_ = bf16[4,208,128]{2,1,0:T(8,128)(2,1)S(1)} collective-permute-done((bf16[4,208,128]{2,1,0:T(8,128)(2,1)S(1)}, bf16[4,208,128]{2,1,0:T(8,128)(2,1)S(1)}, u32[]{:S(2)}, u32[]{:S(2)}) %collective-permute-start.4) | collective-permute-done | bytes 213024 | tf_op jit(solution)/shard_map/ppermute | solution.py:422
  27.2 6.1 %collective-permute-done.5.refs_3_ = bf16[4,208,128]{2,1,0:T(8,128)(2,1)S(1)} collective-permute-done((bf16[4,208,128]{2,1,0:T(8,128)(2,1)S(1)}, bf16[4,208,128]{2,1,0:T(8,128)(2,1)S(1)}, u32[]{:S(2)}, u32[]{:S(2)}) %collective-permute-start.5) | collective-permute-done | bytes 213024 | tf_op jit(solution)/shard_map/ppermute | solution.py:422
  35.6 3.8 %prepare.1 = (bf16[256,768]{1,0:T(8,128)(2,1)}, bf16[256,256]{1,0:T(8,128)(2,1)}, bf16[256,1024]{1,0:T(8,128)(2,1)}, bf16[1024,256]{1,0:T(8,128)(2,1)}, f32[8,256]{1,0:T(8,128)}, /*index=5*/f32[8,1024]{1,0:T(8,128)}) custom-call(s32[4]{0:T(128)} %pad_add_fusion.place_ref, bf16[4,208,128]{2,1,0:T(8,128)(2,1)} %copy-done.3, bf16[4,208,128]{2,1,0:T(8,128)(2,1)} %copy-done.6, ...), custom_call_target="tpu_custom_call" | custom-call | flops 25500000256 | bytes 4000000 | tf_op jit(solution)/shard_map/prepare/pallas_call | solution.py:449
  39.4 2.1 %all-to-all-done.x_ref.cot_ref = bf16[8,3,2,4,16,256]{5,4,3,2,1,0:T(8,128)(2,1)S(1)} async-done(((bf16[8,3,2,4,16,256]{5,4,3,2,1,0:T(8,128)(2,1)}), bf16[8,3,2,4,16,256]{5,4,3,2,1,0:T(8,128)(2,1)S(1)}, u32[]{:S(2)}, u32[]{:S(2)}) %all-to-all-start) | async-done | bytes 1572896 | tf_op jit(solution)/shard_map/all_to_all | solution.py:415
  42.7 5.8 %forward.1 = (bf16[1536,768]{1,0:T(8,128)(2,1)}, bf16[1536,256]{1,0:T(8,128)(2,1)}, f32[1536,256]{1,0:T(8,128)}, f32[3,8,256]{2,1,0:T(8,128)}) custom-call(bf16[8,3,2,4,16,256]{5,4,3,2,1,0:T(8,128)(2,1)} %copy-done, bf16[256,768]{1,0:T(8,128)(2,1)} %get-tuple-element.32.w_qkv, bf16[256,256]{1,0:T(8,128)(2,1)} %get-tuple-element.33.w_out.refs_0_, ...), custom_call_target="tpu_custom_call" | custom-call | flops 1000000000 | bytes 7000000 | tf_op jit(solution)/shard_map/forward/pallas_call | solution.py:459
  48.5 13.5 %feed.1 = (bf16[32,48,256]{2,1,0:T(8,128)(2,1)}, bf16[1536,256]{1,0:T(8,128)(2,1)}, f32[1536,256]{1,0:T(8,128)}, bf16[4,3,208,128]{3,2,1,0:T(8,128)(2,1)}, bf16[...) custom-call(s32[4]{0:T(128)} %pad_add_fusion.place_ref, f32[1536,256]{1,0:T(8,128)} %get-tuple-element.37.middle_ref, ...), custom_call_target="tpu_custom_call" | custom-call | flops 5000000000 | bytes 10000000 | tf_op jit(solution)/shard_map/feed/pallas_call | solution.py:479
  62.2 4.3 %all-to-all-start.1 = ((bf16[8,4,48,256]{3,2,1,0:T(8,128)(2,1)}), bf16[8,4,48,256]{3,2,1,0:T(8,128)(2,1)S(1)}, u32[]{:S(2)}, u32[]{:S(2)}) async-start(bf16[8,4,48,256]{3,2,1,0:T(8,128)(2,1)} %bitcast.68), calls=%async_computation.1 | async-start | bytes 1572864 | tf_op jit(solution)/shard_map/all_to_all | solution.py:415
  67.3 1.2 %fusion.10 = (bf16[4,3,208,128]{3,2,1,0:T(8,128)(2,1)S(1)}, f32[4,3,208,128]{3,2,1,0:T(8,128)S(1)}) fusion(bf16[4,3,208,128]{3,2,1,0:T(8,128)(2,1)} %copy-done.2, bf16[4,3,208,128]{3,2,1,0:T(8,128)(2,1)S(1)} %copy-done.1), kind=kLoop, calls=%fused_computation.28 | loop fusion | flops 1277952 | bytes 3194880 | tf_op jit(solution)/shard_map/convert_element_type | solution.py:529
  69.3 2.9 %collective-permute-start.13 = (bf16[3,208,128]{2,1,0:T(8,128)(2,1)}, bf16[3,208,128]{2,1,0:T(8,128)(2,1)S(1)}, u32[]{:S(2)}, u32[]{:S(2)}) collective-permute-start(bf16[3,208,128]{2,1,0:T(8,128)(2,1)} %get-tuple-element.60), channel_id=1, source_target_pairs={{0,6},{2,4},{4,2},{6,0},{8,14},{10,12},{12,10},{14,8},{16,22},{18,... | collective-permute-start | bytes 479240 | tf_op jit(solution)/shard_map/ppermute | solution.py:422
  72.8 10.4 %attend_back.1 = (bf16[32,48,256]{2,1,0:T(8,128)(2,1)}, bf16[4,1,208,128]{3,2,1,0:T(8,128)(2,1)}, bf16[4,1,208,128]{3,2,1,0:T(8,128)(2,1)}) custom-call(s32[4]{0:T(128)} %pad_add_fusion.place_ref, bf16[8,3,2,4,16,256]{5,4,3,2,1,0:T(8,128)(2,1)} %copy-done, bf16[1536,768]{1,0:T(8,128)(2,1)} %get-tuple-element.35.packed_ref, ...), custom_call_target="tpu_custom_call" | custom-call | flops 10000000000 | bytes 8000000 | tf_op jit(solution)/shard_map/attend_back/pallas_call | solution.py:536
  83.1 5.1 %all-to-all-start.2 = ((bf16[8,4,48,256]{3,2,1,0:T(8,128)(2,1)}), bf16[8,4,48,256]{3,2,1,0:T(8,128)(2,1)S(1)}, u32[]{:S(2)}, u32[]{:S(2)}) async-start(bf16[8,4,48,256]{3,2,1,0:T(8,128)(2,1)} %bitcast.67), calls=%async_computation.2 | async-start | bytes 1572864 | tf_op jit(solution)/shard_map/all_to_all | solution.py:415
  90.9 1.5 %collective-permute-done.14 = bf16[4,1,208,128]{3,2,1,0:T(8,128)(2,1)S(1)} collective-permute-done((bf16[4,1,208,128]{3,2,1,0:T(8,128)(2,1)S(1)}, bf16[4,1,208,128]{3,2,1,0:T(8,128)(2,1)S(1)}, u32[]{:S(2)}, u32[]{:S(2)}) %collective-permute-start.14) | collective-permute-done | bytes 213024 | tf_op jit(solution)/shard_map/ppermute | solution.py:425
  92.4 3.0 %collective-permute-start.17 = (bf16[1,208,128]{2,1,0:T(8,128)(2,1)S(1)}, bf16[1,208,128]{2,1,0:T(8,128)(2,1)S(1)}, u32[]{:S(2)}, u32[]{:S(2)}) collective-permute-start(bf16[1,208,128]{2,1,0:T(8,128)(2,1)S(1)} %get-tuple-element.68), channel_id=1, source_target_pairs={{0,6},{2,4},{4,2},{6,0},{8,14},{10,12},{12,10},{14,8},{16,22},{18,... | collective-permute-start | bytes 159752 | tf_op jit(solution)/shard_map/ppermute | solution.py:422
  96.0 4.7 %collective-permute-done.17 = bf16[1,208,128]{2,1,0:T(8,128)(2,1)S(1)} collective-permute-done((bf16[1,208,128]{2,1,0:T(8,128)(2,1)S(1)}, bf16[1,208,128]{2,1,0:T(8,128)(2,1)S(1)}, u32[]{:S(2)}, u32[]{:S(2)}) %collective-permute-start.17) | collective-permute-done | bytes 53280 | tf_op jit(solution)/shard_map/ppermute | solution.py:422
  101.5 3.0 %collective-permute-start.20 = (bf16[208,128]{1,0:T(8,128)(2,1)S(1)}, bf16[208,128]{1,0:T(8,128)(2,1)S(1)}, u32[]{:S(2)}, u32[]{:S(2)}) collective-permute-start(bf16[208,128]{1,0:T(8,128)(2,1)S(1)} %get-tuple-element.65), channel_id=1, source_target_pairs={{0,24},{2,26},{4,28},{6,30},{8,16},{10,18},{12,20},{14,22},{16,8},... | collective-permute-start | bytes 159752 | tf_op jit(solution)/shard_map/ppermute | solution.py:422
  104.5 1.5 %collective-permute-start.18 = (bf16[208,128]{1,0:T(8,128)(2,1)S(1)}, bf16[208,128]{1,0:T(8,128)(2,1)S(1)}, u32[]{:S(2)}, u32[]{:S(2)}) collective-permute-start(bf16[208,128]{1,0:T(8,128)(2,1)S(1)} %get-tuple-element.64), channel_id=1, source_target_pairs={{0,8},{2,10},{4,12},{6,14},{8,0},{10,2},{12,4},{14,6},{16,24},{18,... | collective-permute-start | bytes 159752 | tf_op jit(solution)/shard_map/ppermute | solution.py:422
  106.2 1.3 %copy.8 = f32[4,8,48,256]{3,2,1,0:T(8,128)} copy(f32[4,8,48,256]{3,2,0,1:T(8,128)S(1)} %convert_bitcast_fusion) | data formatting | bytes 3145728 | tf_op jit(solution)/shard_map/convert_element_type | solution.py:572
  108.1 1.9 %collective-permute-done.19 = bf16[208,128]{1,0:T(8,128)(2,1)S(1)} collective-permute-done((bf16[208,128]{1,0:T(8,128)(2,1)S(1)}, bf16[208,128]{1,0:T(8,128)(2,1)S(1)}, u32[]{:S(2)}, u32[]{:S(2)}) %collective-permute-start.19) | collective-permute-done | bytes 53280 | tf_op jit(solution)/shard_map/ppermute | solution.py:422
  (77 shorter events, 14.8 us)
Async XLA Ops:
  2.5 8.4 %collective-permute-start.2 = (bf16[208,128]{1,0:T(8,128)(2,1)S(1)}, bf16[208,128]{1,0:T(8,128)(2,1)S(1)}, u32[]{:S(2)}, u32[]{:S(2)}) collective-permute-start(bf16[208,128]{1,0:T(8,128)(2,1)S(1)} %bitcast.71), channel_id=1, source_target_pairs={{0,24},{2,26},{4,28},{6,30},{8,16},{10,18},{12,20},{14,22},{16,8},... | collective-permute-start | bytes 159752 | tf_op jit(solution)/shard_map/ppermute | solution.py:422
  7.6 5.0 %collective-permute-start.1 = (bf16[208,128]{1,0:T(8,128)(2,1)S(1)}, bf16[208,128]{1,0:T(8,128)(2,1)S(1)}, u32[]{:S(2)}, u32[]{:S(2)}) collective-permute-start(bf16[208,128]{1,0:T(8,128)(2,1)S(1)} %bitcast.72), channel_id=1, source_target_pairs={{0,16},{2,18},{4,20},{6,22},{8,24},{10,26},{12,28},{14,30},{16,0},... | collective-permute-start | bytes 159752 | tf_op jit(solution)/shard_map/ppermute | solution.py:422
  7.6 5.0 %collective-permute-start = (bf16[208,128]{1,0:T(8,128)(2,1)S(1)}, bf16[208,128]{1,0:T(8,128)(2,1)S(1)}, u32[]{:S(2)}, u32[]{:S(2)}) collective-permute-start(bf16[208,128]{1,0:T(8,128)(2,1)S(1)} %bitcast.73), channel_id=1, source_target_pairs={{0,8},{2,10},{4,12},{6,14},{8,0},{10,2},{12,4},{14,6},{16,24},{18,... | collective-permute-start | bytes 159752 | tf_op jit(solution)/shard_map/ppermute | solution.py:422
  12.7 8.3 %collective-permute-start.3 = (bf16[4,208,128]{2,1,0:T(8,128)(2,1)S(1)}, bf16[4,208,128]{2,1,0:T(8,128)(2,1)S(1)}, u32[]{:S(2)}, u32[]{:S(2)}) collective-permute-start(bf16[4,208,128]{2,1,0:T(8,128)(2,1)S(1)} %pad_maximum_fusion.1.refs_0_), channel_id=1, source_target_pairs={{0,2},{2,0},{4,6},{6,4},{8,10},{10,8},{12,14},{14,12},{16,18},{18,... | collective-permute-start | bytes 638984 | tf_op jit(solution)/shard_map/ppermute | solution.py:422
  14.3 12.9 %collective-permute-start.4 = (bf16[4,208,128]{2,1,0:T(8,128)(2,1)S(1)}, bf16[4,208,128]{2,1,0:T(8,128)(2,1)S(1)}, u32[]{:S(2)}, u32[]{:S(2)}) collective-permute-start(bf16[4,208,128]{2,1,0:T(8,128)(2,1)S(1)} %pad_maximum_fusion.1.refs_0_), channel_id=1, source_target_pairs={{0,4},{2,6},{4,0},{6,2},{8,12},{10,14},{12,8},{14,10},{16,20},{18,... | collective-permute-start | bytes 638984 | tf_op jit(solution)/shard_map/ppermute | solution.py:422
  15.8 17.6 %collective-permute-start.5 = (bf16[4,208,128]{2,1,0:T(8,128)(2,1)S(1)}, bf16[4,208,128]{2,1,0:T(8,128)(2,1)S(1)}, u32[]{:S(2)}, u32[]{:S(2)}) collective-permute-start(bf16[4,208,128]{2,1,0:T(8,128)(2,1)S(1)} %pad_maximum_fusion.1.refs_0_), channel_id=1, source_target_pairs={{0,6},{2,4},{4,2},{6,0},{8,14},{10,12},{12,10},{14,8},{16,22},{18,... | collective-permute-start | bytes 638984 | tf_op jit(solution)/shard_map/ppermute | solution.py:422
  16.3 25.3 %all-to-all-start = ((bf16[8,3,2,4,16,256]{5,4,3,2,1,0:T(8,128)(2,1)}), bf16[8,3,2,4,16,256]{5,4,3,2,1,0:T(8,128)(2,1)S(1)}, u32[]{:S(2)}, u32[]{:S(2)}) async-start(bf16[8,3,2,4,16,256]{5,4,3,2,1,0:T(8,128)(2,1)} %cut.1), calls=%async_computation | async-start | bytes 3145728 | tf_op jit(solution)/shard_map/all_to_all | solution.py:415
  20.3 13.7 %collective-permute-start.6 = (bf16[4,208,128]{2,1,0:T(8,128)(2,1)S(1)}, bf16[4,208,128]{2,1,0:T(8,128)(2,1)S(1)}, u32[]{:S(2)}, u32[]{:S(2)}) collective-permute-start(bf16[4,208,128]{2,1,0:T(8,128)(2,1)S(1)} %pad_maximum_fusion.1.refs_0_), channel_id=1, source_target_pairs={{0,1},{1,0},{2,3},{3,2},{4,5},{5,4},{6,7},{7,6},{8,9},{9,8},{10,11... | collective-permute-start | bytes 638984 | tf_op jit(solution)/shard_map/ppermute | solution.py:425
  21.0 13.0 %collective-permute-start.7 = (bf16[4,208,128]{2,1,0:T(8,128)(2,1)S(1)}, bf16[4,208,128]{2,1,0:T(8,128)(2,1)S(1)}, u32[]{:S(2)}, u32[]{:S(2)}) collective-permute-start(bf16[4,208,128]{2,1,0:T(8,128)(2,1)S(1)} %collective-permute-done.3.refs_1_), channel_id=1, source_target_pairs={{0,1},{1,0},{2,3},{3,2},{4,5},{5,4},{6,7},{7,6},{8,9},{9,8},{10,11... | collective-permute-start | bytes 638984 | tf_op jit(solution)/shard_map/ppermute | solution.py:425
  27.2 6.8 %collective-permute-start.8 = (bf16[4,208,128]{2,1,0:T(8,128)(2,1)S(1)}, bf16[4,208,128]{2,1,0:T(8,128)(2,1)S(1)}, u32[]{:S(2)}, u32[]{:S(2)}) collective-permute-start(bf16[4,208,128]{2,1,0:T(8,128)(2,1)S(1)} %collective-permute-done.4.refs_2_), channel_id=1, source_target_pairs={{0,1},{1,0},{2,3},{3,2},{4,5},{5,4},{6,7},{7,6},{8,9},{9,8},{10,11... | collective-permute-start | bytes 638984 | tf_op jit(solution)/shard_map/ppermute | solution.py:425
  33.4 1.5 %collective-permute-start.9 = (bf16[4,208,128]{2,1,0:T(8,128)(2,1)S(1)}, bf16[4,208,128]{2,1,0:T(8,128)(2,1)S(1)}, u32[]{:S(2)}, u32[]{:S(2)}) collective-permute-start(bf16[4,208,128]{2,1,0:T(8,128)(2,1)S(1)} %collective-permute-done.5.refs_3_), channel_id=1, source_target_pairs={{0,1},{1,0},{2,3},{3,2},{4,5},{5,4},{6,7},{7,6},{8,9},{9,8},{10,11... | collective-permute-start | bytes 638984 | tf_op jit(solution)/shard_map/ppermute | solution.py:425
  62.1 4.3 %collective-permute-start.10 = (bf16[4,3,208,128]{3,2,1,0:T(8,128)(2,1)}, bf16[4,3,208,128]{3,2,1,0:T(8,128)(2,1)S(1)}, u32[]{:S(2)}, u32[]{:S(2)}) collective-permute-start(bf16[4,3,208,128]{3,2,1,0:T(8,128)(2,1)} %get-tuple-element.49), channel_id=1, source_target_pairs={{0,1},{1,0},{2,3},{3,2},{4,5},{5,4},{6,7},{7,6},{8,9},{9,8},{10,11... | collective-permute-start | bytes 1916936 | tf_op jit(solution)/shard_map/ppermute | solution.py:425
  62.2 21.0 %all-to-all-start.1 = ((bf16[8,4,48,256]{3,2,1,0:T(8,128)(2,1)}), bf16[8,4,48,256]{3,2,1,0:T(8,128)(2,1)S(1)}, u32[]{:S(2)}, u32[]{:S(2)}) async-start(bf16[8,4,48,256]{3,2,1,0:T(8,128)(2,1)} %bitcast.68), calls=%async_computation.1 | async-start | bytes 1572864 | tf_op jit(solution)/shard_map/all_to_all | solution.py:415
  69.3 19.0 %collective-permute-start.13 = (bf16[3,208,128]{2,1,0:T(8,128)(2,1)}, bf16[3,208,128]{2,1,0:T(8,128)(2,1)S(1)}, u32[]{:S(2)}, u32[]{:S(2)}) collective-permute-start(bf16[3,208,128]{2,1,0:T(8,128)(2,1)} %get-tuple-element.60), channel_id=1, source_target_pairs={{0,6},{2,4},{4,2},{6,0},{8,14},{10,12},{12,10},{14,8},{16,22},{18,... | collective-permute-start | bytes 479240 | tf_op jit(solution)/shard_map/ppermute | solution.py:422
  72.2 16.1 %collective-permute-start.12 = (bf16[3,208,128]{2,1,0:T(8,128)(2,1)}, bf16[3,208,128]{2,1,0:T(8,128)(2,1)S(1)}, u32[]{:S(2)}, u32[]{:S(2)}) collective-permute-start(bf16[3,208,128]{2,1,0:T(8,128)(2,1)} %get-tuple-element.61), channel_id=1, source_target_pairs={{0,4},{2,6},{4,0},{6,2},{8,12},{10,14},{12,8},{14,10},{16,20},{18,... | collective-permute-start | bytes 479240 | tf_op jit(solution)/shard_map/ppermute | solution.py:422
  72.8 15.5 %collective-permute-start.11 = (bf16[3,208,128]{2,1,0:T(8,128)(2,1)S(1)}, bf16[3,208,128]{2,1,0:T(8,128)(2,1)S(1)}, u32[]{:S(2)}, u32[]{:S(2)}) collective-permute-start(bf16[3,208,128]{2,1,0:T(8,128)(2,1)S(1)} %get-tuple-element.59), channel_id=1, source_target_pairs={{0,2},{2,0},{4,6},{6,4},{8,10},{10,8},{12,14},{14,12},{16,18},{18,... | collective-permute-start | bytes 479240 | tf_op jit(solution)/shard_map/ppermute | solution.py:422
  83.1 18.3 %all-to-all-start.2 = ((bf16[8,4,48,256]{3,2,1,0:T(8,128)(2,1)}), bf16[8,4,48,256]{3,2,1,0:T(8,128)(2,1)S(1)}, u32[]{:S(2)}, u32[]{:S(2)}) async-start(bf16[8,4,48,256]{3,2,1,0:T(8,128)(2,1)} %bitcast.67), calls=%async_computation.2 | async-start | bytes 1572864 | tf_op jit(solution)/shard_map/all_to_all | solution.py:415
  90.9 1.5 %collective-permute-start.14 = (bf16[4,1,208,128]{3,2,1,0:T(8,128)(2,1)S(1)}, bf16[4,1,208,128]{3,2,1,0:T(8,128)(2,1)S(1)}, u32[]{:S(2)}, u32[]{:S(2)}) collective-permute-start(bf16[4,1,208,128]{3,2,1,0:T(8,128)(2,1)S(1)} %copy-done.13), channel_id=1, source_target_pairs={{0,1},{1,0},{2,3},{3,2},{4,5},{5,4},{6,7},{7,6},{8,9},{9,8},{10,11... | collective-permute-start | bytes 638984 | tf_op jit(solution)/shard_map/ppermute | solution.py:425
  92.4 8.3 %collective-permute-start.17 = (bf16[1,208,128]{2,1,0:T(8,128)(2,1)S(1)}, bf16[1,208,128]{2,1,0:T(8,128)(2,1)S(1)}, u32[]{:S(2)}, u32[]{:S(2)}) collective-permute-start(bf16[1,208,128]{2,1,0:T(8,128)(2,1)S(1)} %get-tuple-element.68), channel_id=1, source_target_pairs={{0,6},{2,4},{4,2},{6,0},{8,14},{10,12},{12,10},{14,8},{16,22},{18,... | collective-permute-start | bytes 159752 | tf_op jit(solution)/shard_map/ppermute | solution.py:422
  95.4 5.9 %collective-permute-start.16 = (bf16[1,208,128]{2,1,0:T(8,128)(2,1)S(1)}, bf16[1,208,128]{2,1,0:T(8,128)(2,1)S(1)}, u32[]{:S(2)}, u32[]{:S(2)}) collective-permute-start(bf16[1,208,128]{2,1,0:T(8,128)(2,1)S(1)} %get-tuple-element.69), channel_id=1, source_target_pairs={{0,4},{2,6},{4,0},{6,2},{8,12},{10,14},{12,8},{14,10},{16,20},{18,... | collective-permute-start | bytes 159752 | tf_op jit(solution)/shard_map/ppermute | solution.py:422
  96.0 5.4 %collective-permute-start.15 = (bf16[1,208,128]{2,1,0:T(8,128)(2,1)S(1)}, bf16[1,208,128]{2,1,0:T(8,128)(2,1)S(1)}, u32[]{:S(2)}, u32[]{:S(2)}) collective-permute-start(bf16[1,208,128]{2,1,0:T(8,128)(2,1)S(1)} %get-tuple-element.67), channel_id=1, source_target_pairs={{0,2},{2,0},{4,6},{6,4},{8,10},{10,8},{12,14},{14,12},{16,18},{18,... | collective-permute-start | bytes 159752 | tf_op jit(solution)/shard_map/ppermute | solution.py:422
  101.5 6.6 %collective-permute-start.20 = (bf16[208,128]{1,0:T(8,128)(2,1)S(1)}, bf16[208,128]{1,0:T(8,128)(2,1)S(1)}, u32[]{:S(2)}, u32[]{:S(2)}) collective-permute-start(bf16[208,128]{1,0:T(8,128)(2,1)S(1)} %get-tuple-element.65), channel_id=1, source_target_pairs={{0,24},{2,26},{4,28},{6,30},{8,16},{10,18},{12,20},{14,22},{16,8},... | collective-permute-start | bytes 159752 | tf_op jit(solution)/shard_map/ppermute | solution.py:422
  104.5 5.5 %collective-permute-start.19 = (bf16[208,128]{1,0:T(8,128)(2,1)S(1)}, bf16[208,128]{1,0:T(8,128)(2,1)S(1)}, u32[]{:S(2)}, u32[]{:S(2)}) collective-permute-start(bf16[208,128]{1,0:T(8,128)(2,1)S(1)} %get-tuple-element.66), channel_id=1, source_target_pairs={{0,16},{2,18},{4,20},{6,22},{8,24},{10,26},{12,28},{14,30},{16,0},... | collective-permute-start | bytes 159752 | tf_op jit(solution)/shard_map/ppermute | solution.py:422
  104.5 5.5 %collective-permute-start.18 = (bf16[208,128]{1,0:T(8,128)(2,1)S(1)}, bf16[208,128]{1,0:T(8,128)(2,1)S(1)}, u32[]{:S(2)}, u32[]{:S(2)}) collective-permute-start(bf16[208,128]{1,0:T(8,128)(2,1)S(1)} %get-tuple-element.64), channel_id=1, source_target_pairs={{0,8},{2,10},{4,12},{6,14},{8,0},{10,2},{12,4},{14,6},{16,24},{18,... | collective-permute-start | bytes 159752 | tf_op jit(solution)/shard_map/ppermute | solution.py:422
  (14 other events, 48.4 us)

commit v4 on v3

v4 whole, which is shorter than its diff:
```python
import jax
import jax.numpy as jnp
from jax import lax
from jax.experimental import pallas as pl
from jax.experimental.pallas import tpu as pltpu
from jax.sharding import PartitionSpec as P

D = 256
FF = 1024
HEADS = 2
HEAD = D // HEADS
TALL = 32
STRIDE = 96
EPSILON = 1e-05
LANES = 128
PLANE = 4
CORES = 2
BLOCK = 16
HALF = 8
TOKENS = TALL * BLOCK
TILE = TALL * HALF
VMEM_BYTES = 60 * 1024 * 1024

ROW_GAIN_ONE = 0
ROW_SHIFT_ONE = 2
ROW_QKV = 4
ROW_OUT = ROW_QKV + 6 * D
ROW_GAIN_TWO = ROW_OUT + 2 * D
ROW_SHIFT_TWO = ROW_GAIN_TWO + 2
ROW_IN = ROW_SHIFT_TWO + 2
ROW_BIAS_IN = ROW_IN + 8 * D
ROW_BACK = ROW_BIAS_IN + 8
ROW_BIAS_BACK = ROW_BACK + 2 * FF
ROWS = ROW_BIAS_BACK + 2

SPAN = 5

F32 = jnp.float32
BF16 = jnp.bfloat16


def nn(left, right):
    return lax.dot_general(left, right, (((1,), (0,)), ((), ())), preferred_element_type=F32)


def nt(left, right):
    return lax.dot_general(left, right, (((1,), (1,)), ((), ())), preferred_element_type=F32)


def tn(left, right):
    return lax.dot_general(left, right, (((0,), (0,)), ((), ())), preferred_element_type=F32)


def center(value):
    offset = value - jnp.mean(value, axis=-1, keepdims=True)
    inverse = lax.rsqrt(jnp.mean(offset * offset, axis=-1, keepdims=True) + EPSILON)
    return offset * inverse, inverse


def center_back(grad_hat, hat, inverse):
    mean_one = jnp.mean(grad_hat, axis=-1, keepdims=True)
    mean_two = jnp.mean(grad_hat * hat, axis=-1, keepdims=True)
    return inverse * (grad_hat - mean_one - hat * mean_two)


def allowed(span):
    key = lax.broadcasted_iota(jnp.int32, (TILE, TILE), 0)
    query = lax.broadcasted_iota(jnp.int32, (TILE, TILE), 1)
    same_column = (key % HALF) == (query % HALF)
    half_tile = TILE // 2
    same_image = (key // half_tile == query // half_tile) | (span >= TALL)
    return same_column & (key <= query) & same_image


class Plan:
    def __init__(self, seq, group, shard):
        self.shard = shard
        self.group = group
        self.deep = seq // PLANE
        self.count = seq * CORES
        self.pairwise = self.deep == 4
        rows = (shard + LANES - 2) // LANES + 2
        self.rows = -(-rows // 16) * 16
        self.lead = -(-(ROW_OUT * LANES) // (PLANE * CORES * shard))

    def first_row(self, device):
        return self.shard * device // LANES


def prepare(plan):
    def kernel(place_ref, *refs):
        sources, rest = refs[: CORES * PLANE], refs[CORES * PLANE :]
        w_qkv, w_out, w_in, w_back, vectors, bias_in, held, flat, sems = rest
        deep_at, plane_at, core_at = place_ref[0], place_ref[1], place_ref[2]
        copies = []
        for core in range(CORES):
            for plane in range(PLANE):
                source = sources[core * PLANE + plane]
                for deep in range(plan.deep):
                    slot = deep ^ deep_at if plan.pairwise else deep
                    copies.append(
                        pltpu.make_async_copy(
                            source.at[deep],
                            held.at[slot, plane ^ plane_at, core ^ core_at],
                            sems.at[len(copies)],
                        )
                    )
        for copy in copies:
            copy.start()
        for copy in copies:
            copy.wait()
        for device in range(plan.count):
            row = plan.first_row(device)
            value = held[device // 8, device // 2 % PLANE, device % CORES].astype(F32)
            if plan.shard * device % LANES:
                before = flat[row : row + 1]
                flat[row : row + plan.rows] = value
                flat[row : row + 1] = flat[row : row + 1] + before
            else:
                flat[row : row + plan.rows] = value
        for ref, row, wide in (
            (w_qkv, ROW_QKV, 6),
            (w_out, ROW_OUT, 2),
            (w_in, ROW_IN, 8),
            (w_back, ROW_BACK, 2),
        ):
            for part in range(wide):
                ref[:, part * LANES : (part + 1) * LANES] = flat[
                    pl.ds(row + part, ref.shape[0], stride=wide)
                ].astype(BF16)
        for index, row in enumerate(
            (ROW_GAIN_ONE, ROW_SHIFT_ONE, ROW_GAIN_TWO, ROW_SHIFT_TWO, ROW_BIAS_BACK)
        ):
            for part in range(2):
                vectors[index : index + 1, part * LANES : (part + 1) * LANES] = flat[
                    row + part : row + part + 1
                ]
        holder = place_ref[3]
        vectors[SPAN : SPAN + 1, :LANES] = held[holder // PLANE, holder % PLANE, core_at][
            plan.rows - 1 :
        ].astype(F32)
        for part in range(8):
            bias_in[0:1, part * LANES : (part + 1) * LANES] = flat[
                ROW_BIAS_IN + part : ROW_BIAS_IN + part + 1
            ]

    shapes = [((D, 3 * D), BF16), ((D, D), BF16), ((D, FF), BF16), ((FF, D), BF16)]
    shapes += [((8, D), F32), ((8, FF), F32)]
    return pl.pallas_call(
        kernel,
        out_shape=[jax.ShapeDtypeStruct(shape, kind) for shape, kind in shapes],
        in_specs=[pl.BlockSpec(memory_space=pltpu.SMEM)]
        + [pl.BlockSpec(memory_space=pl.ANY)] * (CORES * PLANE),
        out_specs=[pl.BlockSpec(memory_space=pltpu.VMEM)] * len(shapes),
        scratch_shapes=[
            pltpu.VMEM((plan.deep, PLANE, CORES, plan.rows, LANES), BF16),
            pltpu.VMEM((ROWS + plan.rows + 8, LANES), F32),
            pltpu.SemaphoreType.DMA((plan.count,)),
        ],
        compiler_params=pltpu.CompilerParams(vmem_limit_bytes=VMEM_BYTES),
        cost_estimate=pl.CostEstimate(flops=25500000000, bytes_accessed=4 * 10**6, transcendentals=0),
        name="prepare",
    )


SUB = 2
LOG2E = 1.4426950408889634
SCORE_RATE = HEAD**-0.5 * LOG2E
PIECE = 128
SLAB = 32
GELU_RATE = (2.0 / jnp.pi) ** 0.5
GELU_CUBE = GELU_RATE * 0.044715


def interleave(*lists):
    keyed = []
    for order, steps in enumerate(lists):
        for index, step in enumerate(steps):
            keyed.append(((index + 0.5) / len(steps), order, index, step))
    for _, _, _, step in sorted(keyed, key=lambda entry: entry[:3]):
        step()


def fold(value):
    return jnp.sum(value.reshape(-1, 8, value.shape[-1]), axis=0)


def column_sum(value):
    return jnp.sum(value, axis=0, keepdims=True)


class Copies:
    def __init__(self, sems):
        self.sems = sems
        self.used = 0

    def start(self, source, target):
        copy = pltpu.make_async_copy(source, target, self.sems.at[self.used])
        self.used += 1
        copy.start()
        return copy


def tile_rows(tile):
    return slice(tile * TILE, (tile + 1) * TILE)


def step_rows(step):
    return slice(step * TOKENS, (step + 1) * TOKENS)


def pieces_of(tile, size):
    return [
        slice(start, start + size) for start in range(tile * TILE, (tile + 1) * TILE, size)
    ]


def split(block):
    width = block.shape[-1]
    return [
        block[:, :, side * HALF : (side + 1) * HALF].reshape(-1, width) for side in range(2)
    ]


def join(left, right):
    width = left.shape[-1]
    return jnp.concatenate(
        [left.reshape(-1, HALF, width), right.reshape(-1, HALF, width)], axis=1
    )


def two_heads(value):
    blank = jnp.zeros((value.shape[0], HEAD), value.dtype)
    return jnp.concatenate(
        [
            jnp.concatenate([value[:, :HEAD], blank], axis=1),
            jnp.concatenate([blank, value[:, HEAD:]], axis=1),
        ],
        axis=0,
    )


def own_heads(value):
    rows = value.shape[0] // 2
    return jnp.concatenate([value[:rows, :HEAD], value[rows:, HEAD:]], axis=1)


def quarters():
    for head in range(HEADS):
        for part in range(TILE // LANES):
            yield (
                slice(head * TILE, head * TILE + (part + 1) * LANES),
                slice(part * LANES, (part + 1) * LANES),
                head,
            )


def caps(cap, keys, part):
    return cap[: keys.stop - keys.start, part]


def clear_later(*refs):
    for ref in refs:
        for head in range(HEADS):
            for part in range(TILE // LANES - 1):
                keys = slice(head * TILE + (part + 1) * LANES, (head + 1) * TILE)
                cut = slice(part * LANES, (part + 1) * LANES)
                ref[:, keys, cut] = jnp.zeros_like(ref[:, keys, cut])


def flatten(flat, base, matrix, row, wide):
    for part in range(wide):
        flat[pl.ds(row - base + part, matrix.shape[0], stride=wide)] = matrix[
            :, part * LANES : (part + 1) * LANES
        ]


def flatten_vector(flat, row, vector):
    for part in range(vector.shape[-1] // LANES):
        flat[row + part : row + part + 1] = vector[:, part * LANES : (part + 1) * LANES]


def send_rows(plan, place_ref, flat, base, refs, low, high):
    plane_at, core_at = place_ref[1], place_ref[2]

    def write(own_core):
        for device in range(low * PLANE * CORES, high * PLANE * CORES):
            row = plan.first_row(device) - base
            ref = refs[(device % CORES) ^ own_core]
            ref[(device // CORES % PLANE) ^ plane_at, device // (PLANE * CORES) - low] = flat[
                row : row + plan.rows
            ].astype(BF16)

    for own_core in range(CORES):
        pl.when(core_at == own_core)(lambda own_core=own_core: write(own_core))


class Sums:
    def __init__(self, **widths):
        for name, width in widths.items():
            setattr(self, name, jnp.zeros((8, width), F32))


def layer(plan, steps, local_rows):
    group, tiles, count = plan.group, 2 * steps, steps * TOKENS
    base = ROW_OUT - 4
    deep = plan.deep - plan.lead
    names = (
        "x_in", "cot_in", "wq", "wo", "wi", "wb", "normed", "packed", "scores", "probs", "cap",
        "attended", "middle", "hats", "inverses", "normed_two", "cots", "inner", "grad_act",
        "activated", "grad_inner", "grad_normed", "branch", "out_blocks", "acc_in", "acc_back",
        "acc_out", "flat", "keep_in", "send_in", "sems",
    )

    def kernel(place_ref, both, w_qkv, w_out, w_in, w_back, vectors, bias_in, *refs):
        packed_out, logsum, out, branch_out, keep, send, first = refs[:7]
        r = dict(zip(names, refs[7:]))
        x_in, cot_in, packed, middle, hats = (
            r[n] for n in ("x_in", "cot_in", "packed", "middle", "hats")
        )
        scores, probs, cap, attended = (r[n] for n in ("scores", "probs", "cap", "attended"))
        normed, normed_two, cots = r["normed"], r["normed_two"], r["cots"]
        inner, grad_act, activated, grad_inner = (
            r[n] for n in ("inner", "grad_act", "activated", "grad_inner")
        )
        inverses, grad_normed, branch, flat = (
            r[n] for n in ("inverses", "grad_normed", "branch", "flat")
        )
        copies = Copies(r["sems"])
        waits = {}
        arriving = [[copies.start(both.at[:, 0, 0], x_in.at[0])]]
        arriving[0] += [copies.start(w_qkv, r["wq"]), copies.start(w_out, r["wo"])]
        arriving.append([copies.start(both.at[:, 0, 1], cot_in.at[0])])
        arriving[1] += [copies.start(w_in, r["wi"]), copies.start(w_back, r["wb"])]
        for step in range(1, steps):
            arriving.append(
                [
                    copies.start(both.at[:, step, 0], x_in.at[step]),
                    copies.start(both.at[:, step, 1], cot_in.at[step]),
                ]
            )
        outs = []

        def arrive():
            for copy in arriving.pop(0):
                copy.wait()

        cap[...] = jnp.where(allowed(vectors[SPAN : SPAN + 1, 0:1]), jnp.inf, -1e30)
        clear_later(probs)
        sums = Sums(gain=D, shift=D, cot=D, **{f"bias{p}": D for p in range(FF // D)})

        def read_tokens(step):
            def one(index):
                members = slice(index * SUB, (index + 1) * SUB)
                value = x_in[step, members].astype(F32)
                hat, _ = center(value)
                hat = hat * vectors[0:1] + vectors[1:2]
                for side, (x_rows, n_rows) in enumerate(zip(split(value), split(hat))):
                    size = x_rows.shape[0]
                    start = (2 * step + side) * TILE + index * size
                    middle[start : start + size] = x_rows
                    normed[start : start + size] = n_rows.astype(BF16)

            return [lambda i=i: one(i) for i in range(group // SUB)]

        def read_cots(step):
            def one(index):
                members = slice(index * SUB, (index + 1) * SUB)
                for side, rows in enumerate(split(cot_in[step, members].astype(F32))):
                    size = rows.shape[0]
                    start = (2 * step + side) * TILE + index * size
                    cots[start : start + size] = rows.astype(BF16)
                    sums.cot = sums.cot + fold(rows)

            return [lambda i=i: one(i) for i in range(group // SUB)]

        def attention(tile):
            rows = tile_rows(tile)
            slot = tile % 2

            def project(part):
                cut = slice(part * D, (part + 1) * D)
                packed[rows, cut] = nn(normed[rows], r["wq"][:, cut]).astype(BF16)

            def score():
                scores[slot] = nt(two_heads(packed[rows, D : 2 * D]), packed[rows, :D])

            def soften(keys, part, head):
                value = jnp.minimum(scores[slot, keys, part] * SCORE_RATE, caps(cap, keys, part))
                peak = jnp.max(value, axis=0, keepdims=True)
                terms = jnp.exp2(value - peak)
                total = jnp.sum(terms, axis=0, keepdims=True)
                probs[slot, keys, part] = (terms * (1.0 / total)).astype(BF16)
                row = tile * HEADS + head
                logsum[row : row + 1, part] = peak + jnp.log2(total)

            def mix():
                attended[rows] = tn(probs[slot], two_heads(packed[rows, 2 * D :])).astype(BF16)

            def add():
                middle[rows] = middle[rows] + nn(attended[rows], r["wo"][...])

            def norm(piece):
                hat, inverse = center(middle[piece])
                hats[piece] = hat
                inverses[piece] = jnp.broadcast_to(inverse, (PIECE, LANES))
                normed_two[piece] = (hat * vectors[2:3] + vectors[3:4]).astype(BF16)

            return (
                [lambda p=p: project(p) for p in range(3)]
                + [score]
                + [lambda q=q: soften(*q) for q in quarters()]
                + [mix, add]
                + [lambda p=p: norm(p) for p in pieces_of(tile, PIECE)]
            )

        def expand(tile, part):
            rows, cut = tile_rows(tile), slice(part * D, (part + 1) * D)
            slot = part % 2

            def up():
                inner[slot] = nn(normed_two[rows], r["wi"][:, cut])

            def down():
                grad_act[slot] = nt(cots[rows], r["wb"][cut, :])

            return up, down

        def activate(tile, part, index):
            cut = slice(part * D, (part + 1) * D)
            slot = part % 2
            inside = slice(index * SLAB, (index + 1) * SLAB)
            rows = slice(tile * TILE + index * SLAB, tile * TILE + (index + 1) * SLAB)
            value = inner[slot, inside] + bias_in[0:1, cut]
            cube = value * (GELU_CUBE * (value * value))
            angle = GELU_RATE * value + cube
            bend = jnp.tanh(angle)
            gate = 0.5 * bend + 0.5
            activated[rows, cut] = (value * gate).astype(BF16)
            slope = gate * ((1.0 - bend) * (angle + (cube + cube)) + 1.0)
            grad = grad_act[slot, inside] * slope
            grad_inner[rows, cut] = grad.astype(BF16)
            name = f"bias{part}"
            setattr(sums, name, getattr(sums, name) + fold(grad))

        def hidden(tile):
            listed = []
            slabs = TILE // SLAB
            for part in range(FF // D):
                ahead = expand(tile, part + 1) if part + 1 < FF // D else ()
                for index in range(slabs):
                    if ahead and index % (slabs // 2) == 0:
                        listed.append(ahead[index // (slabs // 2)])
                    listed.append(lambda p=part, i=index: activate(tile, p, i))
            return listed

        def finish(tile):
            rows = tile_rows(tile)

            def second():
                middle[rows] = middle[rows] + nn(activated[rows], r["wb"][...])

            def back():
                grad_normed[rows] = nt(grad_inner[rows], r["wi"][...])

            def norm_back(piece):
                hat, grad = hats[piece], grad_normed[piece]
                inverse = jnp.concatenate([inverses[piece]] * 2, axis=1)
                sums.gain = sums.gain + fold(grad * hat)
                sums.shift = sums.shift + fold(grad)
                grad = cots[piece].astype(F32) + center_back(grad * vectors[2:3], hat, inverse)
                branch[piece] = grad.astype(BF16)

            return [second, back] + [lambda p=p: norm_back(p) for p in pieces_of(tile, PIECE)]

        def release(step):
            rows = step_rows(step)
            kept = {}

            def write(index):
                part = TALL // 4
                sides = []
                for side in range(2):
                    start = (2 * step + side) * TILE + index * part * HALF
                    sides.append(middle[start : start + part * HALF] + vectors[4:5])
                block = r["out_blocks"].at[step]
                block[index * part : (index + 1) * part] = join(*sides).astype(BF16)

            def turn_cots():
                kept["cots"] = cots[rows].T

            def turn_normed():
                kept["normed"] = normed_two[rows].T

            def add_to(ref, cut, value):
                if step == 0:
                    ref[:, cut] = value
                else:
                    ref[:, cut] += value

            def weigh(part):
                cut = slice(part * D, (part + 1) * D)
                add_to(r["acc_back"], cut, nn(kept["cots"], activated[rows, cut]))

            def weigh_in(part):
                cut = slice(part * D, (part + 1) * D)
                add_to(r["acc_in"], cut, nn(kept["normed"], grad_inner[rows, cut]))

            def weigh_out():
                add_to(r["acc_out"], slice(0, D), tn(attended[rows], branch[rows]))

            listed = [turn_cots, turn_normed]
            for part in range(FF // D):
                listed.append(lambda p=part: weigh(p))
                listed.append(lambda p=part: weigh_in(p))
                listed.append(lambda p=part: write(p))
            return listed + [weigh_out]

        def send_packed(step):
            rows = step_rows(step)
            outs.append(copies.start(packed.at[rows], packed_out.at[rows]))

        def send_step(step):
            rows = step_rows(step)
            outs.append(copies.start(branch.at[rows], branch_out.at[rows]))
            outs.append(
                copies.start(
                    r["out_blocks"].at[step], out.at[:, step * BLOCK : (step + 1) * BLOCK]
                )
            )

        arrive()
        for one in read_tokens(0) + attention(0):
            one()
        arrive()
        for one in read_cots(0) + list(expand(0, 0)):
            one()
        for tile in range(tiles):
            if tile % 2 and tile + 1 < tiles:
                arrive()
                send_packed(tile // 2)
                if tile > 3:
                    send_step((tile - 5) // 2)
            lists = [hidden(tile)]
            if tile + 1 < tiles:
                before = read_tokens((tile + 1) // 2) if tile % 2 else []
                after = list(expand(tile + 1, 0))
                if tile % 2:
                    after = read_cots((tile + 1) // 2) + after
                lists.append(before + attention(tile + 1) + after)
            if tile:
                lists.append(finish(tile - 1))
            if tile > 1 and tile % 2:
                lists.append(release((tile - 3) // 2))
            interleave(*lists)
        last = steps - 1
        send_packed(last)
        for step in range(max(0, (tiles - 1 - 5 + 1) // 2), last):
            send_step(step)
        for one in finish(tiles - 1):
            one()
        for one in release(last):
            one()
        send_step(last)
        flatten(flat, base, r["acc_back"][...].T, ROW_BACK, 2)
        flatten(flat, base, r["acc_in"][...], ROW_IN, 8)
        flatten(flat, base, r["acc_out"][...], ROW_OUT, 2)
        flatten_vector(flat, ROW_GAIN_TWO - base, column_sum(sums.gain))
        flatten_vector(flat, ROW_SHIFT_TWO - base, column_sum(sums.shift))
        flatten_vector(flat, ROW_BIAS_BACK - base, column_sum(sums.cot))
        for part in range(FF // D):
            flatten_vector(
                flat, ROW_BIAS_IN - base + 2 * part, column_sum(getattr(sums, f"bias{part}"))
            )
        first[...] = flat[ROW_OUT - base : ROW_OUT - base + 8]
        send_rows(
            plan, place_ref, flat, base, (r["keep_in"], r["send_in"]), plan.lead, plan.deep
        )
        outs.append(copies.start(r["send_in"], send))
        outs.append(copies.start(r["keep_in"], keep))
        for copy in outs:
            copy.wait()

    vmem = pl.BlockSpec(memory_space=pltpu.VMEM)
    hbm = pl.BlockSpec(memory_space=pl.ANY)
    shape = jax.ShapeDtypeStruct
    parts = (PLANE, deep, plan.rows, LANES)
    moved = pltpu.VMEM((steps, group, local_rows, BLOCK, D), BF16)
    wide = lambda width, kind: pltpu.VMEM((count, width), kind)
    pair = lambda rows, kind: pltpu.VMEM((2, rows, TILE), kind)
    scratch = dict(
        x_in=moved,
        cot_in=moved,
        wq=pltpu.VMEM((D, 3 * D), BF16),
        wo=pltpu.VMEM((D, D), BF16),
        wi=pltpu.VMEM((D, FF), BF16),
        wb=pltpu.VMEM((FF, D), BF16),
        normed=wide(D, BF16),
        packed=wide(3 * D, BF16),
        scores=pair(HEADS * TILE, F32),
        probs=pair(HEADS * TILE, BF16),
        cap=pltpu.VMEM((TILE, TILE), F32),
        attended=wide(D, BF16),
        middle=wide(D, F32),
        hats=wide(D, F32),
        inverses=wide(LANES, F32),
        normed_two=wide(D, BF16),
        cots=wide(D, BF16),
        inner=pair(TILE, F32),
        grad_act=pair(TILE, F32),
        activated=wide(FF, BF16),
        grad_inner=wide(FF, BF16),
        grad_normed=wide(D, F32),
        branch=wide(D, BF16),
        out_blocks=pltpu.VMEM((steps, TALL, BLOCK, D), BF16),
        acc_in=pltpu.VMEM((D, FF), F32),
        acc_back=pltpu.VMEM((D, FF), F32),
        acc_out=pltpu.VMEM((D, D), F32),
        flat=pltpu.VMEM((ROWS - base + plan.rows, LANES), F32),
        keep_in=pltpu.VMEM(parts, BF16),
        send_in=pltpu.VMEM(parts, BF16),
        sems=pltpu.SemaphoreType.DMA((6 + 5 * steps,)),
    )
    return pl.pallas_call(
        kernel,
        in_specs=[pl.BlockSpec(memory_space=pltpu.SMEM)] + [hbm] * 5 + [vmem] * 2,
        out_specs=[hbm, vmem, hbm, hbm, hbm, hbm, vmem],
        out_shape=[
            shape((count, 3 * D), BF16),
            shape((-(-tiles * HEADS // 8) * 8, TILE), F32),
            shape((TALL, steps * BLOCK, D), BF16),
            shape((count, D), BF16),
            shape(parts, BF16),
            shape(parts, BF16),
            shape((8, LANES), F32),
        ],
        scratch_shapes=[scratch[name] for name in names],
        compiler_params=pltpu.CompilerParams(vmem_limit_bytes=VMEM_BYTES),
        cost_estimate=pl.CostEstimate(
            flops=15 * 10**9, bytes_accessed=10**7, transcendentals=2 * 10**6
        ),
        name="layer",
    )


def back(plan, steps, local_rows):
    group, tiles, count = plan.group, 2 * steps, steps * TOKENS
    names = (
        "x_in", "packed_in", "branch_in", "wq", "wo", "hats", "inverses", "normed", "grad_att",
        "scores", "grad_probs", "probs", "grad_scores", "grad_packed", "grad_normed", "x_blocks",
        "cap", "acc", "flat", "keep_in", "send_in", "sems",
    )

    def kernel(place_ref, both, packed, branch, w_qkv, w_out, vectors, logsum, first, *refs):
        grad_x, keep, send = refs[:3]
        r = dict(zip(names, refs[3:]))
        x_in, packed_in, branch_in = r["x_in"], r["packed_in"], r["branch_in"]
        hats, inverses, normed, cap = r["hats"], r["inverses"], r["normed"], r["cap"]
        grad_att, scores, grad_probs = r["grad_att"], r["scores"], r["grad_probs"]
        probs, grad_scores = r["probs"], r["grad_scores"]
        grad_packed, grad_normed, flat = r["grad_packed"], r["grad_normed"], r["flat"]
        copies = Copies(r["sems"])
        arriving = []
        for step in range(steps):
            rows = step_rows(step)
            arriving.append([copies.start(branch.at[rows], branch_in.at[rows])])
            if step == 0:
                arriving[0].append(copies.start(w_out, r["wo"]))
            arriving[step].append(copies.start(packed.at[rows], packed_in.at[rows]))
            arriving[step].append(copies.start(both.at[:, step, 0], x_in.at[step]))
            if step == 0:
                arriving[0].append(copies.start(w_qkv, r["wq"]))

        def arrive():
            for copy in arriving.pop(0):
                copy.wait()

        outs = []
        cap[...] = jnp.where(allowed(vectors[SPAN : SPAN + 1, 0:1]), jnp.inf, -1e30)
        clear_later(probs, grad_scores)
        sums = Sums(gain=D, shift=D)
        scale = HEAD**-0.5

        def start(tile):
            rows, slot = tile_rows(tile), tile % 2

            def project():
                grad_att[rows] = nt(branch_in[rows], r["wo"][...]).astype(BF16)

            def score():
                scores[slot] = nt(two_heads(packed_in[rows, D : 2 * D]), packed_in[rows, :D])

            def spread():
                grad_probs[slot] = nt(two_heads(packed_in[rows, 2 * D :]), grad_att[rows])

            return [project, score, spread]

        def soften(tile):
            slot = tile % 2

            def one(keys, part, head):
                value = jnp.minimum(scores[slot, keys, part] * SCORE_RATE, caps(cap, keys, part))
                row = tile * HEADS + head
                prob = jnp.exp2(value - logsum[row : row + 1, part])
                weighted = prob * grad_probs[slot, keys, part]
                total = jnp.sum(weighted, axis=0, keepdims=True)
                probs[slot, keys, part] = prob.astype(BF16)
                grad_scores[slot, keys, part] = (weighted - prob * total).astype(BF16)

            return [lambda q=q: one(*q) for q in quarters()]

        def gather(tile):
            rows, slot = tile_rows(tile), tile % 2

            def queries():
                wide = two_heads(packed_in[rows, D : 2 * D])
                grad_packed[rows, :D] = (tn(grad_scores[slot], wide) * scale).astype(BF16)

            def keys():
                value = own_heads(nn(grad_scores[slot], packed_in[rows, :D]))
                grad_packed[rows, D : 2 * D] = (value * scale).astype(BF16)

            def values():
                value = own_heads(nn(probs[slot], grad_att[rows]))
                grad_packed[rows, 2 * D :] = value.astype(BF16)

            return [queries, keys, values]

        def read_tokens(step):
            def one(index):
                members = slice(index * SUB, (index + 1) * SUB)
                hat, inverse = center(x_in[step, members].astype(F32))
                inverse = jnp.broadcast_to(inverse, hat.shape[:-1] + (LANES,))
                for side, (h_rows, i_rows) in enumerate(zip(split(hat), split(inverse))):
                    size = h_rows.shape[0]
                    begin = (2 * step + side) * TILE + index * size
                    hats[begin : begin + size] = h_rows
                    inverses[begin : begin + size] = i_rows
                    normed[begin : begin + size] = (
                        h_rows * vectors[0:1] + vectors[1:2]
                    ).astype(BF16)

            return [lambda i=i: one(i) for i in range(group // SUB)]

        def finish(tile):
            rows = tile_rows(tile)

            def spread():
                grad_normed[rows] = nt(grad_packed[rows], r["wq"][...])

            def norm_back(piece):
                hat, grad = hats[piece], grad_normed[piece]
                inverse = jnp.concatenate([inverses[piece]] * 2, axis=1)
                sums.gain = sums.gain + fold(grad * hat)
                sums.shift = sums.shift + fold(grad)
                grad = branch_in[piece].astype(F32) + center_back(
                    grad * vectors[0:1], hat, inverse
                )
                grad_normed[piece] = grad

            return [spread] + [lambda p=p: norm_back(p) for p in pieces_of(tile, PIECE)]

        def release(step):
            rows = step_rows(step)
            kept = {}

            def write(index):
                part = TALL // 4
                sides = []
                for side in range(2):
                    begin = (2 * step + side) * TILE + index * part * HALF
                    sides.append(grad_normed[begin : begin + part * HALF])
                block = r["x_blocks"].at[step]
                block[index * part : (index + 1) * part] = join(*sides).astype(BF16)

            def turn():
                kept["normed"] = normed[rows].T

            def weigh(part):
                cut = slice(part * D, (part + 1) * D)
                value = nn(kept["normed"], grad_packed[rows, cut])
                if step == 0:
                    r["acc"][:, cut] = value
                else:
                    r["acc"][:, cut] += value

            return (
                [lambda i=i: write(i) for i in range(4)]
                + [turn]
                + [lambda p=p: weigh(p) for p in range(3)]
            )

        def send_step(step):
            outs.append(
                copies.start(
                    r["x_blocks"].at[step], grad_x.at[:, step * BLOCK : (step + 1) * BLOCK]
                )
            )

        arrive()
        for one in start(0):
            one()
        for tile in range(tiles):
            if tile % 2 and tile + 1 < tiles:
                arrive()
            lists = [soften(tile) + gather(tile)]
            if tile + 1 < tiles:
                lists.append(start(tile + 1))
            if tile % 2 == 0:
                lists.append(read_tokens(tile // 2))
            if tile:
                lists.append(finish(tile - 1))
            if tile > 1 and tile % 2:
                lists.append(release((tile - 3) // 2))
            interleave(*lists)
        for one in finish(tiles - 1):
            one()
        for step in range(steps - 1):
            send_step(step)
        for one in release(steps - 1):
            one()
        send_step(steps - 1)
        flatten(flat, 0, r["acc"][...], ROW_QKV, 6)
        flatten_vector(flat, ROW_GAIN_ONE, column_sum(sums.gain))
        flatten_vector(flat, ROW_SHIFT_ONE, column_sum(sums.shift))
        flat[ROW_OUT : ROW_OUT + 8] = first[...]
        send_rows(plan, place_ref, flat, 0, (r["keep_in"], r["send_in"]), 0, plan.lead)
        outs.append(copies.start(r["send_in"], send))
        outs.append(copies.start(r["keep_in"], keep))
        for copy in outs:
            copy.wait()

    vmem = pl.BlockSpec(memory_space=pltpu.VMEM)
    hbm = pl.BlockSpec(memory_space=pl.ANY)
    shape = jax.ShapeDtypeStruct
    parts = (PLANE, plan.lead, plan.rows, LANES)
    wide = lambda width, kind: pltpu.VMEM((count, width), kind)
    pair = lambda kind: pltpu.VMEM((2, HEADS * TILE, TILE), kind)
    scratch = dict(
        x_in=pltpu.VMEM((steps, group, local_rows, BLOCK, D), BF16),
        packed_in=wide(3 * D, BF16),
        branch_in=wide(D, BF16),
        wq=pltpu.VMEM((D, 3 * D), BF16),
        wo=pltpu.VMEM((D, D), BF16),
        hats=wide(D, F32),
        inverses=wide(LANES, F32),
        normed=wide(D, BF16),
        grad_att=wide(D, BF16),
        scores=pair(F32),
        grad_probs=pair(F32),
        probs=pair(BF16),
        grad_scores=pair(BF16),
        grad_packed=wide(3 * D, BF16),
        grad_normed=wide(D, F32),
        x_blocks=pltpu.VMEM((steps, TALL, BLOCK, D), BF16),
        cap=pltpu.VMEM((TILE, TILE), F32),
        acc=pltpu.VMEM((D, 3 * D), F32),
        flat=pltpu.VMEM((ROW_OUT + plan.rows + 8, LANES), F32),
        keep_in=pltpu.VMEM(parts, BF16),
        send_in=pltpu.VMEM(parts, BF16),
        sems=pltpu.SemaphoreType.DMA((4 + 4 * steps,)),
    )
    return pl.pallas_call(
        kernel,
        in_specs=[pl.BlockSpec(memory_space=pltpu.SMEM)] + [hbm] * 5 + [vmem] * 3,
        out_specs=[hbm] * 3,
        out_shape=[
            shape((TALL, steps * BLOCK, D), BF16),
            shape(parts, BF16),
            shape(parts, BF16),
        ],
        scratch_shapes=[scratch[name] for name in names],
        compiler_params=pltpu.CompilerParams(vmem_limit_bytes=VMEM_BYTES),
        cost_estimate=pl.CostEstimate(
            flops=10 * 10**9, bytes_accessed=8 * 10**6, transcendentals=10**6
        ),
        name="back",
    )


def cut_kernel(group, steps):
    def kernel(rows_ref, cot_ref, out_ref):
        for member in range(group):
            for step in range(steps):
                column = (member * steps + step) * BLOCK
                for kind, ref in enumerate((rows_ref, cot_ref)):
                    out_ref[member, step, kind] = ref[:, column : column + BLOCK]

    return kernel


def local(mesh_shape, tokens, column_rows, cotangent, flat_params):
    seq = mesh_shape["seq"]
    local_rows, columns = tokens.shape[1], tokens.shape[2]
    group = TALL // local_rows
    owned = columns // group
    steps = owned // BLOCK
    plan = Plan(seq, group, flat_params.shape[0])
    seq_at = lax.axis_index("seq")
    core_at = lax.axis_index("dp")
    deep_at, plane_at = seq_at // PLANE, seq_at % PLANE
    holder = seq_at % group * owned // STRIDE * (seq * STRIDE // columns)
    place = jnp.stack([deep_at, plane_at, core_at, holder]).astype(jnp.int32)
    shift = plan.shard * (seq_at * CORES + core_at) % LANES
    groups = [[group * g + i for i in range(group)] for g in range(seq // group)]
    deep_groups = [[PLANE * z + q for z in range(plan.deep)] for q in range(PLANE)]

    def exchange(blocks):
        return lax.all_to_all(blocks, "seq", 0, 0, axis_index_groups=groups, tiled=True)

    def to_rows(cols):
        moved = exchange(cols.reshape(group, local_rows, owned, D))
        return moved.transpose(1, 0, 2, 3).reshape(tokens.shape)

    def swap_seq(value, distance):
        return lax.ppermute(value, "seq", [(i, i ^ distance) for i in range(seq)])

    def swap_core(value):
        return lax.ppermute(value, "dp", [(0, 1), (1, 0)])

    blank = jnp.zeros((plan.rows - 1) * LANES, BF16)
    blank = jnp.concatenate([blank, jnp.broadcast_to(column_rows[0, 0].astype(BF16), (LANES,))])
    own = lax.dynamic_update_slice(blank, flat_params, (shift,)).reshape(plan.rows, LANES)
    if plan.pairwise:
        arrived = [swap_seq(own, PLANE * k) for k in range(1, plan.deep)]
        deep = jnp.stack([own] + arrived)
    else:
        arrived = [own]
        deep = lax.all_gather(own, "seq", axis=0, axis_index_groups=deep_groups)
    vmem = pl.BlockSpec(memory_space=pltpu.VMEM)
    both = pl.pallas_call(
        cut_kernel(group, steps),
        out_shape=jax.ShapeDtypeStruct((group, steps, 2, local_rows, BLOCK, D), BF16),
        in_specs=[vmem, vmem],
        out_specs=vmem,
        compiler_params=pltpu.CompilerParams(vmem_limit_bytes=VMEM_BYTES),
        name="cut",
    )(tokens.reshape(local_rows, columns, D), cotangent.reshape(local_rows, columns, D))
    deep, both = lax.optimization_barrier((deep, both))
    both = exchange(both)
    plane = [deep] + [swap_seq(deep, k) for k in range(1, PLANE)]
    pieces = plane + [swap_core(piece) for piece in plane]
    w_qkv, w_out, w_in, w_back, vectors, bias_in = prepare(plan)(place, *pieces)

    packed, logsum, out, branch, keep, send, first = layer(plan, steps, local_rows)(
        place, both, w_qkv, w_out, w_in, w_back, vectors, bias_in
    )

    layer_out = to_rows(out)

    def core_sum(keep, send):
        return keep.astype(F32) + swap_core(send).astype(F32)

    def plane_sum(value):
        total = value[0]
        sent = value.astype(BF16)
        for k in range(1, PLANE):
            total = total + swap_seq(sent[k], k).astype(F32)
        return total

    later = plane_sum(core_sum(keep, send))

    grad_x, lead_keep, lead_send = back(plan, steps, local_rows)(
        place, both, packed, branch, w_qkv, w_out, vectors, logsum, first
    )
    (lead_keep, lead_send), layer_out, later = lax.optimization_barrier(
        ((lead_keep, lead_send), layer_out, later)
    )
    total = jnp.concatenate([plane_sum(core_sum(lead_keep, lead_send)), later], axis=0)
    moved_x = exchange(grad_x.reshape(group, local_rows, owned, D))
    total, moved_x = lax.optimization_barrier((total, moved_x))
    input_grad = moved_x.transpose(1, 0, 2, 3).reshape(tokens.shape).astype(F32)
    if plan.pairwise:
        sent = total.astype(BF16)
        result = lax.dynamic_index_in_dim(total, deep_at, 0, keepdims=False)
        for k in range(1, plan.deep):
            piece = lax.dynamic_index_in_dim(sent, deep_at ^ k, 0, keepdims=False)
            result = result + swap_seq(piece, PLANE * k).astype(F32)
    else:
        moved = lax.all_to_all(
            total.astype(BF16), "seq", 0, 0, axis_index_groups=deep_groups, tiled=True
        )
        result = jnp.sum(moved.astype(F32), axis=0)
    param_grad = lax.dynamic_slice(result.reshape(-1), (shift,), (plan.shard,))
    return layer_out, input_grad, param_grad


def solution(mesh):
    shape = dict(mesh.shape)
    rows = P("dp", "seq", None, None)
    flat = P(("seq", "dp"))
    return jax.shard_map(
        lambda *args: local(shape, *args),
        mesh=mesh,
        in_specs=(rows, P("dp", "seq"), rows, flat),
        out_specs=(rows, rows, flat),
        check_vma=False,
    )
```

time: 111 us -> 106 us (0.955)
  Pallas kernels: 36.2 us -> 30.6 us
    pallas_call x3 -> x2, Pallas kernels: 29.7 us -> 24.2 us  [the longest x1 15.9 us: local(): layer(plan, steps, local_rows)]
  transfers between devices with their start and end apart: 24 -> 24, of which waited for: 11 -> 11; matrix products, arithmetic and copies ran while one was open for 6% -> 6% of each run, Pallas kernels for 15% -> 14%
where the time goes in v4:
time: 106 us; the launch traced here: 105 us
  starting transfers between devices  34.4 us (32%)
  Pallas kernels  30.6 us (29%)
  waiting for transfers between devices  27 us (25%)
  local copies, waits for them, and re-layouts  8.36 us (8%)
  other arithmetic  3.9 us (4%)
    ppermute x15, waiting for transfers between devices, swap_seq(): return lax.ppermute(value, 'seq', [(i, i ^ distance) for i in range(seq)])  22.6 us
    ppermute x15, starting transfers between devices, swap_seq(): return lax.ppermute(value, 'seq', [(i, i ^ distance) for i in range(seq)])  20.9 us
    pallas_call x1, Pallas kernels, local(): layer(plan, steps, local_rows)  15.9 us
    all_to_all x3, starting transfers between devices, exchange(): lax.all_to_all(blocks, 'seq', 0, 0, axis_index_groups=groups, tiled=True)  13.4 us
    pallas_call x1, Pallas kernels, local(): back(plan, steps, local_rows)  8.29 us
    pallas_call x1, Pallas kernels, local(): w_qkv, w_out, w_in, w_back, vectors, bias_in = prepare(plan)(place, *pieces)  3.85 us
    unnamed x28, local copies, waits for them, and re-layouts  3.39 us
    pallas_call x1, Pallas kernels, local(): pl.pallas_call(cut_kernel(group, steps), out_shape=jax.ShapeDtypeStruct((...  2.61 us
  transfers between devices with their start and end apart: 24, of which 11 were waited for; matrix products, arithmetic and copies ran while one was open for 6% of the time, Pallas kernels for 14%

profile of v4, /device:TPU:0, one launch (start us, length us, event | category | flops | bytes accessed | tf_op | source)
XLA Modules:
  0.0 105.3 jit_solution(9279460079656383668)
XLA Ops:
  1.4 1.2 %dynamic_update_slice.3 = bf16[26624]{0:T(1024)(128)(2,1)S(1)} dynamic-update-slice(bf16[26624]{0:T(1024)(128)(2,1)S(1)} %concatenate.6, bf16[24648]{0:T(1024)(128)(2,1)} %param.7, s32[]{:T(128)S(6)} %select_n.45) | dynamic-update-slice | bytes 98596 | tf_op jit(solution)/shard_map/dynamic_update_slice | solution.py:923
  2.5 5.1 %collective-permute-start.2 = (bf16[208,128]{1,0:T(8,128)(2,1)S(1)}, bf16[208,128]{1,0:T(8,128)(2,1)S(1)}, u32[]{:S(2)}, u32[]{:S(2)}) collective-permute-start(bf16[208,128]{1,0:T(8,128)(2,1)S(1)} %bitcast.71), channel_id=1, source_target_pairs={{0,24},{2,26},{4,28},{6,30},{8,16},{10,18},{12,20},{14,22},{16,8},... | collective-permute-start | bytes 159752 | tf_op jit(solution)/shard_map/ppermute | solution.py:916
  8.3 2.6 %cut.1 = bf16[8,3,2,4,16,256]{5,4,3,2,1,0:T(8,128)(2,1)} custom-call(bf16[4,384,256]{2,1,0:T(8,128)(2,1)} %bitcast.69, bf16[4,384,256]{2,1,0:T(8,128)(2,1)} %bitcast.70), custom_call_target="tpu_custom_call" | custom-call | tf_op jit(solution)/shard_map/cut/pallas_call | solution.py:931
  10.9 1.8 %collective-permute-done.1 = bf16[208,128]{1,0:T(8,128)(2,1)S(1)} collective-permute-done((bf16[208,128]{1,0:T(8,128)(2,1)S(1)}, bf16[208,128]{1,0:T(8,128)(2,1)S(1)}, u32[]{:S(2)}, u32[]{:S(2)}) %collective-permute-start.1) | collective-permute-done | bytes 53280 | tf_op jit(solution)/shard_map/ppermute | solution.py:916
  12.7 1.6 %collective-permute-start.3 = (bf16[4,208,128]{2,1,0:T(8,128)(2,1)S(1)}, bf16[4,208,128]{2,1,0:T(8,128)(2,1)S(1)}, u32[]{:S(2)}, u32[]{:S(2)}) collective-permute-start(bf16[4,208,128]{2,1,0:T(8,128)(2,1)S(1)} %pad_maximum_fusion.1.refs_0_), channel_id=1, source_target_pairs={{0,2},{2,0},{4,6},{6,4},{8,10},{10,8},{12,14},{14,12},{16,18},{18,... | collective-permute-start | bytes 638984 | tf_op jit(solution)/shard_map/ppermute | solution.py:916
  14.3 1.5 %collective-permute-start.4 = (bf16[4,208,128]{2,1,0:T(8,128)(2,1)S(1)}, bf16[4,208,128]{2,1,0:T(8,128)(2,1)S(1)}, u32[]{:S(2)}, u32[]{:S(2)}) collective-permute-start(bf16[4,208,128]{2,1,0:T(8,128)(2,1)S(1)} %pad_maximum_fusion.1.refs_0_), channel_id=1, source_target_pairs={{0,4},{2,6},{4,0},{6,2},{8,12},{10,14},{12,8},{14,10},{16,20},{18,... | collective-permute-start | bytes 638984 | tf_op jit(solution)/shard_map/ppermute | solution.py:916
  16.3 4.0 %all-to-all-start = ((bf16[8,3,2,4,16,256]{5,4,3,2,1,0:T(8,128)(2,1)}), bf16[8,3,2,4,16,256]{5,4,3,2,1,0:T(8,128)(2,1)S(1)}, u32[]{:S(2)}, u32[]{:S(2)}) async-start(bf16[8,3,2,4,16,256]{5,4,3,2,1,0:T(8,128)(2,1)} %cut.1), calls=%async_computation | async-start | bytes 3145728 | tf_op jit(solution)/shard_map/all_to_all | solution.py:909
  21.0 6.2 %collective-permute-done.4.refs_2_ = bf16[4,208,128]{2,1,0:T(8,128)(2,1)S(1)} collective-permute-done((bf16[4,208,128]{2,1,0:T(8,128)(2,1)S(1)}, bf16[4,208,128]{2,1,0:T(8,128)(2,1)S(1)}, u32[]{:S(2)}, u32[]{:S(2)}) %collective-permute-start.4) | collective-permute-done | bytes 213024 | tf_op jit(solution)/shard_map/ppermute | solution.py:916
  27.2 6.1 %collective-permute-done.5.refs_3_ = bf16[4,208,128]{2,1,0:T(8,128)(2,1)S(1)} collective-permute-done((bf16[4,208,128]{2,1,0:T(8,128)(2,1)S(1)}, bf16[4,208,128]{2,1,0:T(8,128)(2,1)S(1)}, u32[]{:S(2)}, u32[]{:S(2)}) %collective-permute-start.5) | collective-permute-done | bytes 213024 | tf_op jit(solution)/shard_map/ppermute | solution.py:916
  35.6 3.8 %prepare.1 = (bf16[256,768]{1,0:T(8,128)(2,1)}, bf16[256,256]{1,0:T(8,128)(2,1)}, bf16[256,1024]{1,0:T(8,128)(2,1)}, bf16[1024,256]{1,0:T(8,128)(2,1)}, f32[8,256]{1,0:T(8,128)}, /*index=5*/f32[8,1024]{1,0:T(8,128)}) custom-call(s32[4]{0:T(128)} %pad_add_fusion.place_ref, bf16[4,208,128]{2,1,0:T(8,128)(2,1)} %copy-done.3, bf16[4,208,128]{2,1,0:T(8,128)(2,1)} %copy-done.6, ...), custom_call_target="tpu_custom_call" | custom-call | flops 25500000256 | bytes 4000000 | tf_op jit(solution)/shard_map/prepare/pallas_call | solution.py:943
  39.4 2.1 %all-to-all-done.both = bf16[8,3,2,4,16,256]{5,4,3,2,1,0:T(8,128)(2,1)S(1)} async-done(((bf16[8,3,2,4,16,256]{5,4,3,2,1,0:T(8,128)(2,1)}), bf16[8,3,2,4,16,256]{5,4,3,2,1,0:T(8,128)(2,1)S(1)}, u32[]{:S(2)}, u32[]{:S(2)}) %all-to-all-start) | async-done | bytes 1572896 | tf_op jit(solution)/shard_map/all_to_all | solution.py:909
  42.7 15.9 %layer.1 = (bf16[1536,768]{1,0:T(8,128)(2,1)}, f32[16,256]{1,0:T(8,128)}, bf16[32,48,256]{2,1,0:T(8,128)(2,1)}, bf16[1536,256]{1,0:T(8,128)(2,1)}, bf16[4,3,208,...) custom-call(s32[4]{0:T(128)} %pad_add_fusion.place_ref, ...), custom_call_target="tpu_custom_call" | custom-call | flops 15000000512 | bytes 10000000 | tf_op jit(solution)/shard_map/layer/pallas_call | solution.py:945
  58.7 4.3 %all-to-all-start.1 = ((bf16[8,4,48,256]{3,2,1,0:T(8,128)(2,1)}), bf16[8,4,48,256]{3,2,1,0:T(8,128)(2,1)S(1)}, u32[]{:S(2)}, u32[]{:S(2)}) async-start(bf16[8,4,48,256]{3,2,1,0:T(8,128)(2,1)} %bitcast.68), calls=%async_computation.1 | async-start | bytes 1572864 | tf_op jit(solution)/shard_map/all_to_all | solution.py:909
  63.8 1.2 %fusion.10 = (bf16[4,3,208,128]{3,2,1,0:T(8,128)(2,1)S(1)}, f32[4,3,208,128]{3,2,1,0:T(8,128)S(1)}) fusion(bf16[4,3,208,128]{3,2,1,0:T(8,128)(2,1)} %copy-done.2, bf16[4,3,208,128]{3,2,1,0:T(8,128)(2,1)S(1)} %copy-done.1), kind=kLoop, calls=%fused_computation.28 | loop fusion | flops 1277952 | bytes 3194880 | tf_op jit(solution)/shard_map/convert_element_type | solution.py:956
  65.8 2.9 %collective-permute-start.13 = (bf16[3,208,128]{2,1,0:T(8,128)(2,1)}, bf16[3,208,128]{2,1,0:T(8,128)(2,1)S(1)}, u32[]{:S(2)}, u32[]{:S(2)}) collective-permute-start(bf16[3,208,128]{2,1,0:T(8,128)(2,1)} %get-tuple-element.54), channel_id=1, source_target_pairs={{0,6},{2,4},{4,2},{6,0},{8,14},{10,12},{12,10},{14,8},{16,22},{18,... | collective-permute-start | bytes 479240 | tf_op jit(solution)/shard_map/ppermute | solution.py:916
  69.3 8.3 %back.1 = (bf16[32,48,256]{2,1,0:T(8,128)(2,1)}, bf16[4,1,208,128]{3,2,1,0:T(8,128)(2,1)}, bf16[4,1,208,128]{3,2,1,0:T(8,128)(2,1)}) custom-call(s32[4]{0:T(128)} %pad_add_fusion.place_ref, bf16[8,3,2,4,16,256]{5,4,3,2,1,0:T(8,128)(2,1)} %copy-done, bf16[1536,768]{1,0:T(8,128)(2,1)} %get-tuple-element.35.packed, bf16[1536,256]{1,0:T(8,128)(2,1)} %get-tuple-element.36.branch, ...), custom_call_target="tpu_custom_call" | custom-call | flops 10000000000 | bytes 8000000 | tf_op jit(solution)/shard_map/back/pallas_call | solution.py:963
  77.6 5.1 %all-to-all-start.2 = ((bf16[8,4,48,256]{3,2,1,0:T(8,128)(2,1)}), bf16[8,4,48,256]{3,2,1,0:T(8,128)(2,1)S(1)}, u32[]{:S(2)}, u32[]{:S(2)}) async-start(bf16[8,4,48,256]{3,2,1,0:T(8,128)(2,1)} %bitcast.67), calls=%async_computation.2 | async-start | bytes 1572864 | tf_op jit(solution)/shard_map/all_to_all | solution.py:909
  85.4 1.5 %collective-permute-done.14 = bf16[4,1,208,128]{3,2,1,0:T(8,128)(2,1)S(1)} collective-permute-done((bf16[4,1,208,128]{3,2,1,0:T(8,128)(2,1)S(1)}, bf16[4,1,208,128]{3,2,1,0:T(8,128)(2,1)S(1)}, u32[]{:S(2)}, u32[]{:S(2)}) %collective-permute-start.14) | collective-permute-done | bytes 213024 | tf_op jit(solution)/shard_map/ppermute | solution.py:919
  87.0 3.0 %collective-permute-start.17 = (bf16[1,208,128]{2,1,0:T(8,128)(2,1)S(1)}, bf16[1,208,128]{2,1,0:T(8,128)(2,1)S(1)}, u32[]{:S(2)}, u32[]{:S(2)}) collective-permute-start(bf16[1,208,128]{2,1,0:T(8,128)(2,1)S(1)} %get-tuple-element.62), channel_id=1, source_target_pairs={{0,6},{2,4},{4,2},{6,0},{8,14},{10,12},{12,10},{14,8},{16,22},{18,... | collective-permute-start | bytes 159752 | tf_op jit(solution)/shard_map/ppermute | solution.py:916
  90.6 4.7 %collective-permute-done.17 = bf16[1,208,128]{2,1,0:T(8,128)(2,1)S(1)} collective-permute-done((bf16[1,208,128]{2,1,0:T(8,128)(2,1)S(1)}, bf16[1,208,128]{2,1,0:T(8,128)(2,1)S(1)}, u32[]{:S(2)}, u32[]{:S(2)}) %collective-permute-start.17) | collective-permute-done | bytes 53280 | tf_op jit(solution)/shard_map/ppermute | solution.py:916
  96.0 3.0 %collective-permute-start.20 = (bf16[208,128]{1,0:T(8,128)(2,1)S(1)}, bf16[208,128]{1,0:T(8,128)(2,1)S(1)}, u32[]{:S(2)}, u32[]{:S(2)}) collective-permute-start(bf16[208,128]{1,0:T(8,128)(2,1)S(1)} %get-tuple-element.59), channel_id=1, source_target_pairs={{0,24},{2,26},{4,28},{6,30},{8,16},{10,18},{12,20},{14,22},{16,8},... | collective-permute-start | bytes 159752 | tf_op jit(solution)/shard_map/ppermute | solution.py:916
  99.0 1.5 %collective-permute-start.18 = (bf16[208,128]{1,0:T(8,128)(2,1)S(1)}, bf16[208,128]{1,0:T(8,128)(2,1)S(1)}, u32[]{:S(2)}, u32[]{:S(2)}) collective-permute-start(bf16[208,128]{1,0:T(8,128)(2,1)S(1)} %get-tuple-element.58), channel_id=1, source_target_pairs={{0,8},{2,10},{4,12},{6,14},{8,0},{10,2},{12,4},{14,6},{16,24},{18,... | collective-permute-start | bytes 159752 | tf_op jit(solution)/shard_map/ppermute | solution.py:916
  100.7 1.3 %copy.8 = f32[4,8,48,256]{3,2,1,0:T(8,128)} copy(f32[4,8,48,256]{3,2,0,1:T(8,128)S(1)} %convert_bitcast_fusion) | data formatting | bytes 3145728 | tf_op jit(solution)/shard_map/convert_element_type | solution.py:972
  102.6 1.9 %collective-permute-done.19 = bf16[208,128]{1,0:T(8,128)(2,1)S(1)} collective-permute-done((bf16[208,128]{1,0:T(8,128)(2,1)S(1)}, bf16[208,128]{1,0:T(8,128)(2,1)S(1)}, u32[]{:S(2)}, u32[]{:S(2)}) %collective-permute-start.19) | collective-permute-done | bytes 53280 | tf_op jit(solution)/shard_map/ppermute | solution.py:916
  (76 shorter events, 13.7 us)
Async XLA Ops:
  2.5 8.4 %collective-permute-start.2 = (bf16[208,128]{1,0:T(8,128)(2,1)S(1)}, bf16[208,128]{1,0:T(8,128)(2,1)S(1)}, u32[]{:S(2)}, u32[]{:S(2)}) collective-permute-start(bf16[208,128]{1,0:T(8,128)(2,1)S(1)} %bitcast.71), channel_id=1, source_target_pairs={{0,24},{2,26},{4,28},{6,30},{8,16},{10,18},{12,20},{14,22},{16,8},... | collective-permute-start | bytes 159752 | tf_op jit(solution)/shard_map/ppermute | solution.py:916
  7.6 5.0 %collective-permute-start.1 = (bf16[208,128]{1,0:T(8,128)(2,1)S(1)}, bf16[208,128]{1,0:T(8,128)(2,1)S(1)}, u32[]{:S(2)}, u32[]{:S(2)}) collective-permute-start(bf16[208,128]{1,0:T(8,128)(2,1)S(1)} %bitcast.72), channel_id=1, source_target_pairs={{0,16},{2,18},{4,20},{6,22},{8,24},{10,26},{12,28},{14,30},{16,0},... | collective-permute-start | bytes 159752 | tf_op jit(solution)/shard_map/ppermute | solution.py:916
  7.6 5.0 %collective-permute-start = (bf16[208,128]{1,0:T(8,128)(2,1)S(1)}, bf16[208,128]{1,0:T(8,128)(2,1)S(1)}, u32[]{:S(2)}, u32[]{:S(2)}) collective-permute-start(bf16[208,128]{1,0:T(8,128)(2,1)S(1)} %bitcast.73), channel_id=1, source_target_pairs={{0,8},{2,10},{4,12},{6,14},{8,0},{10,2},{12,4},{14,6},{16,24},{18,... | collective-permute-start | bytes 159752 | tf_op jit(solution)/shard_map/ppermute | solution.py:916
  12.7 8.3 %collective-permute-start.3 = (bf16[4,208,128]{2,1,0:T(8,128)(2,1)S(1)}, bf16[4,208,128]{2,1,0:T(8,128)(2,1)S(1)}, u32[]{:S(2)}, u32[]{:S(2)}) collective-permute-start(bf16[4,208,128]{2,1,0:T(8,128)(2,1)S(1)} %pad_maximum_fusion.1.refs_0_), channel_id=1, source_target_pairs={{0,2},{2,0},{4,6},{6,4},{8,10},{10,8},{12,14},{14,12},{16,18},{18,... | collective-permute-start | bytes 638984 | tf_op jit(solution)/shard_map/ppermute | solution.py:916
  14.3 12.9 %collective-permute-start.4 = (bf16[4,208,128]{2,1,0:T(8,128)(2,1)S(1)}, bf16[4,208,128]{2,1,0:T(8,128)(2,1)S(1)}, u32[]{:S(2)}, u32[]{:S(2)}) collective-permute-start(bf16[4,208,128]{2,1,0:T(8,128)(2,1)S(1)} %pad_maximum_fusion.1.refs_0_), channel_id=1, source_target_pairs={{0,4},{2,6},{4,0},{6,2},{8,12},{10,14},{12,8},{14,10},{16,20},{18,... | collective-permute-start | bytes 638984 | tf_op jit(solution)/shard_map/ppermute | solution.py:916
  15.8 17.6 %collective-permute-start.5 = (bf16[4,208,128]{2,1,0:T(8,128)(2,1)S(1)}, bf16[4,208,128]{2,1,0:T(8,128)(2,1)S(1)}, u32[]{:S(2)}, u32[]{:S(2)}) collective-permute-start(bf16[4,208,128]{2,1,0:T(8,128)(2,1)S(1)} %pad_maximum_fusion.1.refs_0_), channel_id=1, source_target_pairs={{0,6},{2,4},{4,2},{6,0},{8,14},{10,12},{12,10},{14,8},{16,22},{18,... | collective-permute-start | bytes 638984 | tf_op jit(solution)/shard_map/ppermute | solution.py:916
  16.3 25.3 %all-to-all-start = ((bf16[8,3,2,4,16,256]{5,4,3,2,1,0:T(8,128)(2,1)}), bf16[8,3,2,4,16,256]{5,4,3,2,1,0:T(8,128)(2,1)S(1)}, u32[]{:S(2)}, u32[]{:S(2)}) async-start(bf16[8,3,2,4,16,256]{5,4,3,2,1,0:T(8,128)(2,1)} %cut.1), calls=%async_computation | async-start | bytes 3145728 | tf_op jit(solution)/shard_map/all_to_all | solution.py:909
  20.3 13.7 %collective-permute-start.6 = (bf16[4,208,128]{2,1,0:T(8,128)(2,1)S(1)}, bf16[4,208,128]{2,1,0:T(8,128)(2,1)S(1)}, u32[]{:S(2)}, u32[]{:S(2)}) collective-permute-start(bf16[4,208,128]{2,1,0:T(8,128)(2,1)S(1)} %pad_maximum_fusion.1.refs_0_), channel_id=1, source_target_pairs={{0,1},{1,0},{2,3},{3,2},{4,5},{5,4},{6,7},{7,6},{8,9},{9,8},{10,11... | collective-permute-start | bytes 638984 | tf_op jit(solution)/shard_map/ppermute | solution.py:919
  21.0 13.0 %collective-permute-start.7 = (bf16[4,208,128]{2,1,0:T(8,128)(2,1)S(1)}, bf16[4,208,128]{2,1,0:T(8,128)(2,1)S(1)}, u32[]{:S(2)}, u32[]{:S(2)}) collective-permute-start(bf16[4,208,128]{2,1,0:T(8,128)(2,1)S(1)} %collective-permute-done.3.refs_1_), channel_id=1, source_target_pairs={{0,1},{1,0},{2,3},{3,2},{4,5},{5,4},{6,7},{7,6},{8,9},{9,8},{10,11... | collective-permute-start | bytes 638984 | tf_op jit(solution)/shard_map/ppermute | solution.py:919
  27.2 6.8 %collective-permute-start.8 = (bf16[4,208,128]{2,1,0:T(8,128)(2,1)S(1)}, bf16[4,208,128]{2,1,0:T(8,128)(2,1)S(1)}, u32[]{:S(2)}, u32[]{:S(2)}) collective-permute-start(bf16[4,208,128]{2,1,0:T(8,128)(2,1)S(1)} %collective-permute-done.4.refs_2_), channel_id=1, source_target_pairs={{0,1},{1,0},{2,3},{3,2},{4,5},{5,4},{6,7},{7,6},{8,9},{9,8},{10,11... | collective-permute-start | bytes 638984 | tf_op jit(solution)/shard_map/ppermute | solution.py:919
  33.4 1.5 %collective-permute-start.9 = (bf16[4,208,128]{2,1,0:T(8,128)(2,1)S(1)}, bf16[4,208,128]{2,1,0:T(8,128)(2,1)S(1)}, u32[]{:S(2)}, u32[]{:S(2)}) collective-permute-start(bf16[4,208,128]{2,1,0:T(8,128)(2,1)S(1)} %collective-permute-done.5.refs_3_), channel_id=1, source_target_pairs={{0,1},{1,0},{2,3},{3,2},{4,5},{5,4},{6,7},{7,6},{8,9},{9,8},{10,11... | collective-permute-start | bytes 638984 | tf_op jit(solution)/shard_map/ppermute | solution.py:919
  58.6 4.4 %collective-permute-start.10 = (bf16[4,3,208,128]{3,2,1,0:T(8,128)(2,1)}, bf16[4,3,208,128]{3,2,1,0:T(8,128)(2,1)S(1)}, u32[]{:S(2)}, u32[]{:S(2)}) collective-permute-start(bf16[4,3,208,128]{3,2,1,0:T(8,128)(2,1)} %get-tuple-element.43), channel_id=1, source_target_pairs={{0,1},{1,0},{2,3},{3,2},{4,5},{5,4},{6,7},{7,6},{8,9},{9,8},{10,11... | collective-permute-start | bytes 1916936 | tf_op jit(solution)/shard_map/ppermute | solution.py:919
  58.7 18.9 %all-to-all-start.1 = ((bf16[8,4,48,256]{3,2,1,0:T(8,128)(2,1)}), bf16[8,4,48,256]{3,2,1,0:T(8,128)(2,1)S(1)}, u32[]{:S(2)}, u32[]{:S(2)}) async-start(bf16[8,4,48,256]{3,2,1,0:T(8,128)(2,1)} %bitcast.68), calls=%async_computation.1 | async-start | bytes 1572864 | tf_op jit(solution)/shard_map/all_to_all | solution.py:909
  65.8 16.9 %collective-permute-start.13 = (bf16[3,208,128]{2,1,0:T(8,128)(2,1)}, bf16[3,208,128]{2,1,0:T(8,128)(2,1)S(1)}, u32[]{:S(2)}, u32[]{:S(2)}) collective-permute-start(bf16[3,208,128]{2,1,0:T(8,128)(2,1)} %get-tuple-element.54), channel_id=1, source_target_pairs={{0,6},{2,4},{4,2},{6,0},{8,14},{10,12},{12,10},{14,8},{16,22},{18,... | collective-permute-start | bytes 479240 | tf_op jit(solution)/shard_map/ppermute | solution.py:916
  68.8 14.0 %collective-permute-start.12 = (bf16[3,208,128]{2,1,0:T(8,128)(2,1)}, bf16[3,208,128]{2,1,0:T(8,128)(2,1)S(1)}, u32[]{:S(2)}, u32[]{:S(2)}) collective-permute-start(bf16[3,208,128]{2,1,0:T(8,128)(2,1)} %get-tuple-element.55), channel_id=1, source_target_pairs={{0,4},{2,6},{4,0},{6,2},{8,12},{10,14},{12,8},{14,10},{16,20},{18,... | collective-permute-start | bytes 479240 | tf_op jit(solution)/shard_map/ppermute | solution.py:916
  69.3 13.5 %collective-permute-start.11 = (bf16[3,208,128]{2,1,0:T(8,128)(2,1)S(1)}, bf16[3,208,128]{2,1,0:T(8,128)(2,1)S(1)}, u32[]{:S(2)}, u32[]{:S(2)}) collective-permute-start(bf16[3,208,128]{2,1,0:T(8,128)(2,1)S(1)} %get-tuple-element.53), channel_id=1, source_target_pairs={{0,2},{2,0},{4,6},{6,4},{8,10},{10,8},{12,14},{14,12},{16,18},{18,... | collective-permute-start | bytes 479240 | tf_op jit(solution)/shard_map/ppermute | solution.py:916
  77.6 18.3 %all-to-all-start.2 = ((bf16[8,4,48,256]{3,2,1,0:T(8,128)(2,1)}), bf16[8,4,48,256]{3,2,1,0:T(8,128)(2,1)S(1)}, u32[]{:S(2)}, u32[]{:S(2)}) async-start(bf16[8,4,48,256]{3,2,1,0:T(8,128)(2,1)} %bitcast.67), calls=%async_computation.2 | async-start | bytes 1572864 | tf_op jit(solution)/shard_map/all_to_all | solution.py:909
  85.4 1.5 %collective-permute-start.14 = (bf16[4,1,208,128]{3,2,1,0:T(8,128)(2,1)S(1)}, bf16[4,1,208,128]{3,2,1,0:T(8,128)(2,1)S(1)}, u32[]{:S(2)}, u32[]{:S(2)}) collective-permute-start(bf16[4,1,208,128]{3,2,1,0:T(8,128)(2,1)S(1)} %copy-done.13), channel_id=1, source_target_pairs={{0,1},{1,0},{2,3},{3,2},{4,5},{5,4},{6,7},{7,6},{8,9},{9,8},{10,11... | collective-permute-start | bytes 638984 | tf_op jit(solution)/shard_map/ppermute | solution.py:919
  87.0 8.3 %collective-permute-start.17 = (bf16[1,208,128]{2,1,0:T(8,128)(2,1)S(1)}, bf16[1,208,128]{2,1,0:T(8,128)(2,1)S(1)}, u32[]{:S(2)}, u32[]{:S(2)}) collective-permute-start(bf16[1,208,128]{2,1,0:T(8,128)(2,1)S(1)} %get-tuple-element.62), channel_id=1, source_target_pairs={{0,6},{2,4},{4,2},{6,0},{8,14},{10,12},{12,10},{14,8},{16,22},{18,... | collective-permute-start | bytes 159752 | tf_op jit(solution)/shard_map/ppermute | solution.py:916
  89.9 6.0 %collective-permute-start.16 = (bf16[1,208,128]{2,1,0:T(8,128)(2,1)S(1)}, bf16[1,208,128]{2,1,0:T(8,128)(2,1)S(1)}, u32[]{:S(2)}, u32[]{:S(2)}) collective-permute-start(bf16[1,208,128]{2,1,0:T(8,128)(2,1)S(1)} %get-tuple-element.63), channel_id=1, source_target_pairs={{0,4},{2,6},{4,0},{6,2},{8,12},{10,14},{12,8},{14,10},{16,20},{18,... | collective-permute-start | bytes 159752 | tf_op jit(solution)/shard_map/ppermute | solution.py:916
  90.5 5.4 %collective-permute-start.15 = (bf16[1,208,128]{2,1,0:T(8,128)(2,1)S(1)}, bf16[1,208,128]{2,1,0:T(8,128)(2,1)S(1)}, u32[]{:S(2)}, u32[]{:S(2)}) collective-permute-start(bf16[1,208,128]{2,1,0:T(8,128)(2,1)S(1)} %get-tuple-element.61), channel_id=1, source_target_pairs={{0,2},{2,0},{4,6},{6,4},{8,10},{10,8},{12,14},{14,12},{16,18},{18,... | collective-permute-start | bytes 159752 | tf_op jit(solution)/shard_map/ppermute | solution.py:916
  96.0 6.6 %collective-permute-start.20 = (bf16[208,128]{1,0:T(8,128)(2,1)S(1)}, bf16[208,128]{1,0:T(8,128)(2,1)S(1)}, u32[]{:S(2)}, u32[]{:S(2)}) collective-permute-start(bf16[208,128]{1,0:T(8,128)(2,1)S(1)} %get-tuple-element.59), channel_id=1, source_target_pairs={{0,24},{2,26},{4,28},{6,30},{8,16},{10,18},{12,20},{14,22},{16,8},... | collective-permute-start | bytes 159752 | tf_op jit(solution)/shard_map/ppermute | solution.py:916
  99.0 5.5 %collective-permute-start.19 = (bf16[208,128]{1,0:T(8,128)(2,1)S(1)}, bf16[208,128]{1,0:T(8,128)(2,1)S(1)}, u32[]{:S(2)}, u32[]{:S(2)}) collective-permute-start(bf16[208,128]{1,0:T(8,128)(2,1)S(1)} %get-tuple-element.60), channel_id=1, source_target_pairs={{0,16},{2,18},{4,20},{6,22},{8,24},{10,26},{12,28},{14,30},{16,0},... | collective-permute-start | bytes 159752 | tf_op jit(solution)/shard_map/ppermute | solution.py:916
  99.0 5.5 %collective-permute-start.18 = (bf16[208,128]{1,0:T(8,128)(2,1)S(1)}, bf16[208,128]{1,0:T(8,128)(2,1)S(1)}, u32[]{:S(2)}, u32[]{:S(2)}) collective-permute-start(bf16[208,128]{1,0:T(8,128)(2,1)S(1)} %get-tuple-element.58), channel_id=1, source_target_pairs={{0,8},{2,10},{4,12},{6,14},{8,0},{10,2},{12,4},{14,6},{16,24},{18,... | collective-permute-start | bytes 159752 | tf_op jit(solution)/shard_map/ppermute | solution.py:916
  (14 other events, 48.5 us)

commit v5 on v4

--- a/solution.py
+++ b/solution.py
@@ -19,7 +19,7 @@
 HALF = 8
 TOKENS = TALL * BLOCK
 TILE = TALL * HALF
-VMEM_BYTES = 60 * 1024 * 1024
+VMEM_BYTES = 63 * 1024 * 1024
 
 ROW_GAIN_ONE = 0
 ROW_SHIFT_ONE = 2
@@ -280,19 +280,15 @@
         flat[row + part : row + part + 1] = vector[:, part * LANES : (part + 1) * LANES]
 
 
-def send_rows(plan, place_ref, flat, base, refs, low, high):
+def send_rows(plan, place_ref, flat, base, parts, low, high):
     plane_at, core_at = place_ref[1], place_ref[2]
-
-    def write(own_core):
-        for device in range(low * PLANE * CORES, high * PLANE * CORES):
-            row = plan.first_row(device) - base
-            ref = refs[(device % CORES) ^ own_core]
-            ref[(device // CORES % PLANE) ^ plane_at, device // (PLANE * CORES) - low] = flat[
-                row : row + plan.rows
-            ].astype(BF16)
-
-    for own_core in range(CORES):
-        pl.when(core_at == own_core)(lambda own_core=own_core: write(own_core))
+    for device in range(low * PLANE * CORES, high * PLANE * CORES):
+        row = plan.first_row(device) - base
+        parts[
+            (device % CORES) ^ core_at,
+            (device // CORES % PLANE) ^ plane_at,
+            device // (PLANE * CORES) - low,
+        ] = flat[row : row + plan.rows].astype(BF16)
 
 
 class Sums:
@@ -309,7 +305,7 @@
         "x_in", "cot_in", "wq", "wo", "wi", "wb", "normed", "packed", "scores", "probs", "cap",
         "attended", "middle", "hats", "inverses", "normed_two", "cots", "inner", "grad_act",
         "activated", "grad_inner", "grad_normed", "branch", "out_blocks", "acc_in", "acc_back",
-        "acc_out", "flat", "keep_in", "send_in", "sems",
+        "acc_out", "flat", "parts_in", "sems",
     )
 
     def kernel(place_ref, both, w_qkv, w_out, w_in, w_back, vectors, bias_in, *refs):
@@ -329,16 +325,17 @@
         copies = Copies(r["sems"])
         waits = {}
         arriving = [[copies.start(both.at[:, 0, 0], x_in.at[0])]]
-        arriving[0] += [copies.start(w_qkv, r["wq"]), copies.start(w_out, r["wo"])]
+        arriving[0].append(copies.start(w_qkv, r["wq"]))
+        arriving.append([copies.start(both.at[:, 1, 0], x_in.at[1])])
+        arriving[1].append(copies.start(w_out, r["wo"]))
         arriving.append([copies.start(both.at[:, 0, 1], cot_in.at[0])])
-        arriving[1] += [copies.start(w_in, r["wi"]), copies.start(w_back, r["wb"])]
-        for step in range(1, steps):
-            arriving.append(
-                [
-                    copies.start(both.at[:, step, 0], x_in.at[step]),
-                    copies.start(both.at[:, step, 1], cot_in.at[step]),
-                ]
-            )
+        arriving[2] += [copies.start(w_in, r["wi"]), copies.start(w_back, r["wb"])]
+        arriving[2] += [
+            copies.start(both.at[:, step, 0], x_in.at[step]) for step in range(2, steps)
+        ]
+        arriving.append(
+            [copies.start(both.at[:, step, 1], cot_in.at[step]) for step in range(1, steps)]
+        )
         outs = []
 
         def arrive():
@@ -407,16 +404,14 @@
                 normed_two[piece] = (hat * vectors[2:3] + vectors[3:4]).astype(BF16)
 
             return (
-                [lambda p=p: project(p) for p in range(3)]
-                + [score]
-                + [lambda q=q: soften(*q) for q in quarters()]
-                + [mix, add]
-                + [lambda p=p: norm(p) for p in pieces_of(tile, PIECE)]
+                [lambda p=p: project(p) for p in range(3)],
+                [score] + [lambda q=q: soften(*q) for q in quarters()],
+                [mix, add] + [lambda p=p: norm(p) for p in pieces_of(tile, PIECE)],
             )
 
         def expand(tile, part):
             rows, cut = tile_rows(tile), slice(part * D, (part + 1) * D)
-            slot = part % 2
+            slot = part
 
             def up():
                 inner[slot] = nn(normed_two[rows], r["wi"][:, cut])
@@ -428,7 +423,7 @@
 
         def activate(tile, part, index):
             cut = slice(part * D, (part + 1) * D)
-            slot = part % 2
+            slot = part
             inside = slice(index * SLAB, (index + 1) * SLAB)
             rows = slice(tile * TILE + index * SLAB, tile * TILE + (index + 1) * SLAB)
             value = inner[slot, inside] + bias_in[0:1, cut]
@@ -509,12 +504,10 @@
             def weigh_out():
                 add_to(r["acc_out"], slice(0, D), tn(attended[rows], branch[rows]))
 
-            listed = [turn_cots, turn_normed]
-            for part in range(FF // D):
-                listed.append(lambda p=part: weigh(p))
-                listed.append(lambda p=part: weigh_in(p))
-                listed.append(lambda p=part: write(p))
-            return listed + [weigh_out]
+            parts = range(FF // D)
+            weights = [turn_cots] + [lambda p=p: weigh(p) for p in parts]
+            weights += [turn_normed] + [lambda p=p: weigh_in(p) for p in parts]
+            return weights, [lambda p=p: write(p) for p in parts] + [weigh_out]
 
         def send_packed(step):
             rows = step_rows(step)
@@ -529,37 +522,49 @@
                 )
             )
 
+        stages = [attention(tile) for tile in range(tiles)]
+        weights, closing = zip(*[release(step) for step in range(steps)])
         arrive()
-        for one in read_tokens(0) + attention(0):
+        for one in read_tokens(0):
             one()
         arrive()
-        for one in read_cots(0) + list(expand(0, 0)):
+        interleave(stages[0][0], read_tokens(1))
+        interleave(stages[1][0], stages[0][1])
+        arrive()
+        interleave(stages[2][0], stages[1][1], stages[0][2], read_cots(0))
+        for one in expand(0, 0):
             one()
         for tile in range(tiles):
-            if tile % 2 and tile + 1 < tiles:
+            if tile == 1:
                 arrive()
-                send_packed(tile // 2)
-                if tile > 3:
-                    send_step((tile - 5) // 2)
+                send_packed(0)
+            if tile == 3:
+                send_packed(1)
+            if tile > 4 and tile % 2:
+                send_step((tile - 5) // 2)
             lists = [hidden(tile)]
+            if tile + 3 < tiles:
+                lists.append(stages[tile + 3][0])
+            if tile + 2 < tiles:
+                lists.append(stages[tile + 2][1])
             if tile + 1 < tiles:
-                before = read_tokens((tile + 1) // 2) if tile % 2 else []
-                after = list(expand(tile + 1, 0))
-                if tile % 2:
-                    after = read_cots((tile + 1) // 2) + after
-                lists.append(before + attention(tile + 1) + after)
+                lists.append(stages[tile + 1][2] + list(expand(tile + 1, 0)))
+            if tile % 2 == 0 and tile // 2 + 2 < steps:
+                lists.append(read_tokens(tile // 2 + 2))
+            if tile % 2 and (tile + 1) // 2 < steps:
+                lists.append(read_cots((tile + 1) // 2))
             if tile:
                 lists.append(finish(tile - 1))
+            if tile > 1 and tile % 2 == 0:
+                lists.append(weights[tile // 2 - 1])
             if tile > 1 and tile % 2:
-                lists.append(release((tile - 3) // 2))
+                lists.append(closing[(tile - 3) // 2])
             interleave(*lists)
         last = steps - 1
         send_packed(last)
-        for step in range(max(0, (tiles - 1 - 5 + 1) // 2), last):
-            send_step(step)
-        for one in finish(tiles - 1):
-            one()
-        for one in release(last):
+        send_step(last - 1)
+        interleave(finish(tiles - 1), weights[last])
+        for one in closing[last]:
             one()
         send_step(last)
         flatten(flat, base, r["acc_back"][...].T, ROW_BACK, 2)
@@ -574,10 +579,10 @@
             )
         first[...] = flat[ROW_OUT - base : ROW_OUT - base + 8]
         send_rows(
-            plan, place_ref, flat, base, (r["keep_in"], r["send_in"]), plan.lead, plan.deep
+            plan, place_ref, flat, base, r["parts_in"], plan.lead, plan.deep
         )
-        outs.append(copies.start(r["send_in"], send))
-        outs.append(copies.start(r["keep_in"], keep))
+        outs.append(copies.start(r["parts_in"].at[1], send))
+        outs.append(copies.start(r["parts_in"].at[0], keep))
         for copy in outs:
             copy.wait()
 
@@ -606,8 +611,8 @@
         inverses=wide(LANES, F32),
         normed_two=wide(D, BF16),
         cots=wide(D, BF16),
-        inner=pair(TILE, F32),
-        grad_act=pair(TILE, F32),
+        inner=pltpu.VMEM((FF // D, TILE, D), F32),
+        grad_act=pltpu.VMEM((FF // D, TILE, D), F32),
         activated=wide(FF, BF16),
         grad_inner=wide(FF, BF16),
         grad_normed=wide(D, F32),
@@ -617,8 +622,7 @@
         acc_back=pltpu.VMEM((D, FF), F32),
         acc_out=pltpu.VMEM((D, D), F32),
         flat=pltpu.VMEM((ROWS - base + plan.rows, LANES), F32),
-        keep_in=pltpu.VMEM(parts, BF16),
-        send_in=pltpu.VMEM(parts, BF16),
+        parts_in=pltpu.VMEM((CORES,) + parts, BF16),
         sems=pltpu.SemaphoreType.DMA((6 + 5 * steps,)),
     )
     return pl.pallas_call(
@@ -648,7 +652,7 @@
     names = (
         "x_in", "packed_in", "branch_in", "wq", "wo", "hats", "inverses", "normed", "grad_att",
         "scores", "grad_probs", "probs", "grad_scores", "grad_packed", "grad_normed", "x_blocks",
-        "cap", "acc", "flat", "keep_in", "send_in", "sems",
+        "cap", "acc", "flat", "parts_in", "sems",
     )
 
     def kernel(place_ref, both, packed, branch, w_qkv, w_out, vectors, logsum, first, *refs):
@@ -797,36 +801,40 @@
                 )
             )
 
+        released = [release(step) for step in range(steps)]
         arrive()
         for one in start(0):
             one()
+        interleave(soften(0), start(1), read_tokens(0))
         for tile in range(tiles):
-            if tile % 2 and tile + 1 < tiles:
+            if tile % 2 == 0 and tile + 2 < tiles:
                 arrive()
-            lists = [soften(tile) + gather(tile)]
+            if tile > 4 and tile % 2:
+                send_step((tile - 5) // 2)
+            lists = [gather(tile)]
             if tile + 1 < tiles:
-                lists.append(start(tile + 1))
-            if tile % 2 == 0:
-                lists.append(read_tokens(tile // 2))
+                lists.append(soften(tile + 1))
+            if tile + 2 < tiles:
+                lists.append(start(tile + 2))
+            if tile % 2 and (tile + 1) // 2 < steps:
+                lists.append(read_tokens((tile + 1) // 2))
             if tile:
                 lists.append(finish(tile - 1))
             if tile > 1 and tile % 2:
-                lists.append(release((tile - 3) // 2))
+                lists.append(released[(tile - 3) // 2])
             interleave(*lists)
-        for one in finish(tiles - 1):
-            one()
-        for step in range(steps - 1):
-            send_step(step)
-        for one in release(steps - 1):
+        send_step(steps - 2)
+        interleave(finish(tiles - 1), released[steps - 1][4:])
+        for one in released[steps - 1][:4]:
             one()
         send_step(steps - 1)
         flatten(flat, 0, r["acc"][...], ROW_QKV, 6)
         flatten_vector(flat, ROW_GAIN_ONE, column_sum(sums.gain))
         flatten_vector(flat, ROW_SHIFT_ONE, column_sum(sums.shift))
         flat[ROW_OUT : ROW_OUT + 8] = first[...]
-        send_rows(plan, place_ref, flat, 0, (r["keep_in"], r["send_in"]), 0, plan.lead)
-        outs.append(copies.start(r["send_in"], send))
-        outs.append(copies.start(r["keep_in"], keep))
+        send_rows(plan, place_ref, flat, 0, r["parts_in"], 0, plan.lead)
+        outs.append(copies.start(r["parts_in"].at[1], send))
+        outs.append(copies.start(r["parts_in"].at[0], keep))
         for copy in outs:
             copy.wait()
 
@@ -856,8 +864,7 @@
         cap=pltpu.VMEM((TILE, TILE), F32),
         acc=pltpu.VMEM((D, 3 * D), F32),
         flat=pltpu.VMEM((ROW_OUT + plan.rows + 8, LANES), F32),
-        keep_in=pltpu.VMEM(parts, BF16),
-        send_in=pltpu.VMEM(parts, BF16),
+        parts_in=pltpu.VMEM((CORES,) + parts, BF16),
         sems=pltpu.SemaphoreType.DMA((4 + 4 * steps,)),
     )
     return pl.pallas_call(

time: 106 us -> 102 us (0.962)
  Pallas kernels: 30.6 us -> 28.6 us
  local copies, waits for them, and re-layouts: 8.36 us -> 6.46 us
    unnamed x28 -> x20, local copies, waits for them, and re-layouts: 3.39 us -> 1.45 us
    pallas_call x1, Pallas kernels: 15.9 us -> 14.3 us  [local(): layer(plan, steps, local_rows)]
where the time goes in v5:
time: 102 us
  starting transfers between devices  35 us (34%)
  Pallas kernels  28.6 us (28%)
  waiting for transfers between devices  26.5 us (26%)
  local copies, waits for them, and re-layouts  6.46 us (6%)
  other arithmetic  4.05 us (4%)
    ppermute x15, waiting for transfers between devices, swap_seq(): return lax.ppermute(value, 'seq', [(i, i ^ distance) for i in range(seq)])  22.4 us
    ppermute x15, starting transfers between devices, swap_seq(): return lax.ppermute(value, 'seq', [(i, i ^ distance) for i in range(seq)])  20.8 us
    pallas_call x1, Pallas kernels, local(): layer(plan, steps, local_rows)  14.3 us
    all_to_all x3, starting transfers between devices, exchange(): lax.all_to_all(blocks, 'seq', 0, 0, axis_index_groups=groups, tiled=True)  13.9 us
    pallas_call x1, Pallas kernels, local(): back(plan, steps, local_rows)  7.84 us
    pallas_call x1, Pallas kernels, local(): w_qkv, w_out, w_in, w_back, vectors, bias_in = prepare(plan)(place, *pieces)  3.85 us
    all_to_all x3, waiting for transfers between devices, exchange(): lax.all_to_all(blocks, 'seq', 0, 0, axis_index_groups=groups, tiled=True)  2.62 us
    pallas_call x1, Pallas kernels, local(): pl.pallas_call(cut_kernel(group, steps), out_shape=jax.ShapeDtypeStruct((...  2.61 us
  transfers between devices with their start and end apart: 24, of which 11 were waited for; matrix products, arithmetic and copies ran while one was open for 6% of the time, Pallas kernels for 14%

profile of v5, /device:TPU:0, one launch (start us, length us, event | category | flops | bytes accessed | tf_op | source)
XLA Modules:
  0.0 101.5 jit_solution(2313506492284880949)
XLA Ops:
  2.5 5.1 %collective-permute-start.2 = (bf16[208,128]{1,0:T(8,128)(2,1)S(1)}, bf16[208,128]{1,0:T(8,128)(2,1)S(1)}, u32[]{:S(2)}, u32[]{:S(2)}) collective-permute-start(bf16[208,128]{1,0:T(8,128)(2,1)S(1)} %bitcast.71), channel_id=1, source_target_pairs={{0,24},{2,26},{4,28},{6,30},{8,16},{10,18},{12,20},{14,22},{16,8},... | collective-permute-start | bytes 159752 | tf_op jit(solution)/shard_map/ppermute | solution.py:923
  8.3 2.6 %cut.1 = bf16[8,3,2,4,16,256]{5,4,3,2,1,0:T(8,128)(2,1)} custom-call(bf16[4,384,256]{2,1,0:T(8,128)(2,1)} %bitcast.69, bf16[4,384,256]{2,1,0:T(8,128)(2,1)} %bitcast.70), custom_call_target="tpu_custom_call" | custom-call | tf_op jit(solution)/shard_map/cut/pallas_call | solution.py:938
  10.9 1.8 %collective-permute-done.1 = bf16[208,128]{1,0:T(8,128)(2,1)S(1)} collective-permute-done((bf16[208,128]{1,0:T(8,128)(2,1)S(1)}, bf16[208,128]{1,0:T(8,128)(2,1)S(1)}, u32[]{:S(2)}, u32[]{:S(2)}) %collective-permute-start.1) | collective-permute-done | bytes 53280 | tf_op jit(solution)/shard_map/ppermute | solution.py:923
  12.7 1.6 %collective-permute-start.3 = (bf16[4,208,128]{2,1,0:T(8,128)(2,1)S(1)}, bf16[4,208,128]{2,1,0:T(8,128)(2,1)S(1)}, u32[]{:S(2)}, u32[]{:S(2)}) collective-permute-start(bf16[4,208,128]{2,1,0:T(8,128)(2,1)S(1)} %pad_maximum_fusion.1.refs_0_), channel_id=1, source_target_pairs={{0,2},{2,0},{4,6},{6,4},{8,10},{10,8},{12,14},{14,12},{16,18},{18,... | collective-permute-start | bytes 638984 | tf_op jit(solution)/shard_map/ppermute | solution.py:923
  14.3 1.5 %collective-permute-start.4 = (bf16[4,208,128]{2,1,0:T(8,128)(2,1)S(1)}, bf16[4,208,128]{2,1,0:T(8,128)(2,1)S(1)}, u32[]{:S(2)}, u32[]{:S(2)}) collective-permute-start(bf16[4,208,128]{2,1,0:T(8,128)(2,1)S(1)} %pad_maximum_fusion.1.refs_0_), channel_id=1, source_target_pairs={{0,4},{2,6},{4,0},{6,2},{8,12},{10,14},{12,8},{14,10},{16,20},{18,... | collective-permute-start | bytes 638984 | tf_op jit(solution)/shard_map/ppermute | solution.py:923
  16.3 4.3 %all-to-all-start = ((bf16[8,3,2,4,16,256]{5,4,3,2,1,0:T(8,128)(2,1)}), bf16[8,3,2,4,16,256]{5,4,3,2,1,0:T(8,128)(2,1)}, u32[]{:S(2)}, u32[]{:S(2)}) async-start(bf16[8,3,2,4,16,256]{5,4,3,2,1,0:T(8,128)(2,1)} %cut.1), calls=%async_computation | async-start | bytes 3145728 | tf_op jit(solution)/shard_map/all_to_all | solution.py:916
  21.2 5.4 %collective-permute-done.4.refs_2_ = bf16[4,208,128]{2,1,0:T(8,128)(2,1)S(1)} collective-permute-done((bf16[4,208,128]{2,1,0:T(8,128)(2,1)S(1)}, bf16[4,208,128]{2,1,0:T(8,128)(2,1)S(1)}, u32[]{:S(2)}, u32[]{:S(2)}) %collective-permute-start.4) | collective-permute-done | bytes 213024 | tf_op jit(solution)/shard_map/ppermute | solution.py:923
  26.6 6.5 %collective-permute-done.5.refs_3_ = bf16[4,208,128]{2,1,0:T(8,128)(2,1)S(1)} collective-permute-done((bf16[4,208,128]{2,1,0:T(8,128)(2,1)S(1)}, bf16[4,208,128]{2,1,0:T(8,128)(2,1)S(1)}, u32[]{:S(2)}, u32[]{:S(2)}) %collective-permute-start.5) | collective-permute-done | bytes 213024 | tf_op jit(solution)/shard_map/ppermute | solution.py:923
  35.2 3.9 %prepare.1 = (bf16[256,768]{1,0:T(8,128)(2,1)}, bf16[256,256]{1,0:T(8,128)(2,1)}, bf16[256,1024]{1,0:T(8,128)(2,1)}, bf16[1024,256]{1,0:T(8,128)(2,1)}, f32[8,256]{1,0:T(8,128)}, /*index=5*/f32[8,1024]{1,0:T(8,128)}) custom-call(s32[4]{0:T(128)} %pad_add_fusion.place_ref, bf16[4,208,128]{2,1,0:T(8,128)(2,1)} %copy-done.1, bf16[4,208,128]{2,1,0:T(8,128)(2,1)} %copy-done.3, ...), custom_call_target="tpu_custom_call" | custom-call | flops 25500000256 | bytes 4000000 | tf_op jit(solution)/shard_map/prepare/pallas_call | solution.py:950
  39.1 2.6 %all-to-all-done.both = bf16[8,3,2,4,16,256]{5,4,3,2,1,0:T(8,128)(2,1)} async-done(((bf16[8,3,2,4,16,256]{5,4,3,2,1,0:T(8,128)(2,1)}), bf16[8,3,2,4,16,256]{5,4,3,2,1,0:T(8,128)(2,1)}, u32[]{:S(2)}, u32[]{:S(2)}) %all-to-all-start) | async-done | bytes 1572896 | tf_op jit(solution)/shard_map/all_to_all | solution.py:916
  41.7 14.3 %layer.1 = (bf16[1536,768]{1,0:T(8,128)(2,1)}, f32[16,256]{1,0:T(8,128)}, bf16[32,48,256]{2,1,0:T(8,128)(2,1)}, bf16[1536,256]{1,0:T(8,128)(2,1)}, bf16[4,3,208,...) custom-call(s32[4]{0:T(128)} %pad_add_fusion.place_ref, ...), custom_call_target="tpu_custom_call" | custom-call | flops 15000000512 | bytes 10000000 | tf_op jit(solution)/shard_map/layer/pallas_call | solution.py:952
  56.1 4.5 %all-to-all-start.1 = ((bf16[8,4,48,256]{3,2,1,0:T(8,128)(2,1)}), bf16[8,4,48,256]{3,2,1,0:T(8,128)(2,1)S(1)}, u32[]{:S(2)}, u32[]{:S(2)}) async-start(bf16[8,4,48,256]{3,2,1,0:T(8,128)(2,1)} %bitcast.68), calls=%async_computation.1 | async-start | bytes 1572864 | tf_op jit(solution)/shard_map/all_to_all | solution.py:916
  60.5 1.2 %fusion.10 = (bf16[4,3,208,128]{3,2,1,0:T(8,128)(2,1)S(1)}, f32[4,3,208,128]{3,2,1,0:T(8,128)}) fusion(bf16[4,3,208,128]{3,2,1,0:T(8,128)(2,1)S(1)} %collective-permute-done.10, bf16[4,3,208,128]{3,2,1,0:T(8,128)(2,1)S(1)} %copy-done), kind=kLoop, calls=%fused_computation.28 | loop fusion | flops 1277952 | bytes 3194880 | tf_op jit(solution)/shard_map/convert_element_type | solution.py:963
  62.5 2.9 %collective-permute-start.13 = (bf16[3,208,128]{2,1,0:T(8,128)(2,1)}, bf16[3,208,128]{2,1,0:T(8,128)(2,1)S(1)}, u32[]{:S(2)}, u32[]{:S(2)}) collective-permute-start(bf16[3,208,128]{2,1,0:T(8,128)(2,1)} %get-tuple-element.54), channel_id=1, source_target_pairs={{0,6},{2,4},{4,2},{6,0},{8,14},{10,12},{12,10},{14,8},{16,22},{18,... | collective-permute-start | bytes 479240 | tf_op jit(solution)/shard_map/ppermute | solution.py:923
  66.0 7.8 %back.1 = (bf16[32,48,256]{2,1,0:T(8,128)(2,1)}, bf16[4,1,208,128]{3,2,1,0:T(8,128)(2,1)}, bf16[4,1,208,128]{3,2,1,0:T(8,128)(2,1)}) custom-call(s32[4]{0:T(128)} %pad_add_fusion.place_ref, bf16[8,3,2,4,16,256]{5,4,3,2,1,0:T(8,128)(2,1)} %all-to-all-done.both, bf16[1536,768]{1,0:T(8,128)(2,1)} %get-tuple-element.35.packed, ...), custom_call_target="tpu_custom_call" | custom-call | flops 10000000000 | bytes 8000000 | tf_op jit(solution)/shard_map/back/pallas_call | solution.py:970
  73.9 5.1 %all-to-all-start.2 = ((bf16[8,4,48,256]{3,2,1,0:T(8,128)(2,1)}), bf16[8,4,48,256]{3,2,1,0:T(8,128)(2,1)S(1)}, u32[]{:S(2)}, u32[]{:S(2)}) async-start(bf16[8,4,48,256]{3,2,1,0:T(8,128)(2,1)} %bitcast.67), calls=%async_computation.2 | async-start | bytes 1572864 | tf_op jit(solution)/shard_map/all_to_all | solution.py:916
  79.6 1.2 %fusion.2 = f32[3,208,128]{2,1,0:T(8,128)S(1)} fusion(f32[4,3,208,128]{3,2,1,0:T(8,128)} %get-tuple-element.52, bf16[3,208,128]{2,1,0:T(8,128)(2,1)S(1)} %collective-permute-done.13, bf16[3,208,128]{2,1,0:T(8,128)(2,1)} %collective-permute-done.12, bf16[3,208,128]{2,1,0:T(8,128)(2,1)} %collective-permute-done.11), kind=kLoop, calls=%fused_computation.7 | loop fusion | flops 479232 | bytes 1118208 | tf_op jit(solution)/shard_map/add | solution.py:965
  81.8 1.4 %collective-permute-done.14 = bf16[4,1,208,128]{3,2,1,0:T(8,128)(2,1)S(1)} collective-permute-done((bf16[4,1,208,128]{3,2,1,0:T(8,128)(2,1)S(1)}, bf16[4,1,208,128]{3,2,1,0:T(8,128)(2,1)S(1)}, u32[]{:S(2)}, u32[]{:S(2)}) %collective-permute-start.14) | collective-permute-done | bytes 213024 | tf_op jit(solution)/shard_map/ppermute | solution.py:926
  83.3 2.4 %collective-permute-start.17 = (bf16[1,208,128]{2,1,0:T(8,128)(2,1)S(1)}, bf16[1,208,128]{2,1,0:T(8,128)(2,1)S(1)}, u32[]{:S(2)}, u32[]{:S(2)}) collective-permute-start(bf16[1,208,128]{2,1,0:T(8,128)(2,1)S(1)} %get-tuple-element.62), channel_id=1, source_target_pairs={{0,6},{2,4},{4,2},{6,0},{8,14},{10,12},{12,10},{14,8},{16,22},{18,... | collective-permute-start | bytes 159752 | tf_op jit(solution)/shard_map/ppermute | solution.py:923
  86.9 4.7 %collective-permute-done.17 = bf16[1,208,128]{2,1,0:T(8,128)(2,1)S(1)} collective-permute-done((bf16[1,208,128]{2,1,0:T(8,128)(2,1)S(1)}, bf16[1,208,128]{2,1,0:T(8,128)(2,1)S(1)}, u32[]{:S(2)}, u32[]{:S(2)}) %collective-permute-start.17) | collective-permute-done | bytes 53280 | tf_op jit(solution)/shard_map/ppermute | solution.py:923
  92.3 2.8 %collective-permute-start.20 = (bf16[208,128]{1,0:T(8,128)(2,1)S(1)}, bf16[208,128]{1,0:T(8,128)(2,1)S(1)}, u32[]{:S(2)}, u32[]{:S(2)}) collective-permute-start(bf16[208,128]{1,0:T(8,128)(2,1)S(1)} %get-tuple-element.59), channel_id=1, source_target_pairs={{0,24},{2,26},{4,28},{6,30},{8,16},{10,18},{12,20},{14,22},{16,8},... | collective-permute-start | bytes 159752 | tf_op jit(solution)/shard_map/ppermute | solution.py:923
  95.2 1.5 %collective-permute-start.18 = (bf16[208,128]{1,0:T(8,128)(2,1)S(1)}, bf16[208,128]{1,0:T(8,128)(2,1)S(1)}, u32[]{:S(2)}, u32[]{:S(2)}) collective-permute-start(bf16[208,128]{1,0:T(8,128)(2,1)S(1)} %get-tuple-element.58), channel_id=1, source_target_pairs={{0,8},{2,10},{4,12},{6,14},{8,0},{10,2},{12,4},{14,6},{16,24},{18,... | collective-permute-start | bytes 159752 | tf_op jit(solution)/shard_map/ppermute | solution.py:923
  96.9 1.3 %copy.8 = f32[4,8,48,256]{3,2,1,0:T(8,128)} copy(f32[4,8,48,256]{3,2,0,1:T(8,128)S(1)} %convert_bitcast_fusion) | data formatting | bytes 3145728 | tf_op jit(solution)/shard_map/convert_element_type | solution.py:979
  98.8 2.0 %collective-permute-done.19 = bf16[208,128]{1,0:T(8,128)(2,1)S(1)} collective-permute-done((bf16[208,128]{1,0:T(8,128)(2,1)S(1)}, bf16[208,128]{1,0:T(8,128)(2,1)S(1)}, u32[]{:S(2)}, u32[]{:S(2)}) %collective-permute-start.19) | collective-permute-done | bytes 53280 | tf_op jit(solution)/shard_map/ppermute | solution.py:923
  (68 shorter events, 12.3 us)
Async XLA Ops:
  2.5 8.4 %collective-permute-start.2 = (bf16[208,128]{1,0:T(8,128)(2,1)S(1)}, bf16[208,128]{1,0:T(8,128)(2,1)S(1)}, u32[]{:S(2)}, u32[]{:S(2)}) collective-permute-start(bf16[208,128]{1,0:T(8,128)(2,1)S(1)} %bitcast.71), channel_id=1, source_target_pairs={{0,24},{2,26},{4,28},{6,30},{8,16},{10,18},{12,20},{14,22},{16,8},... | collective-permute-start | bytes 159752 | tf_op jit(solution)/shard_map/ppermute | solution.py:923
  7.6 5.0 %collective-permute-start.1 = (bf16[208,128]{1,0:T(8,128)(2,1)S(1)}, bf16[208,128]{1,0:T(8,128)(2,1)S(1)}, u32[]{:S(2)}, u32[]{:S(2)}) collective-permute-start(bf16[208,128]{1,0:T(8,128)(2,1)S(1)} %bitcast.72), channel_id=1, source_target_pairs={{0,16},{2,18},{4,20},{6,22},{8,24},{10,26},{12,28},{14,30},{16,0},... | collective-permute-start | bytes 159752 | tf_op jit(solution)/shard_map/ppermute | solution.py:923
  7.6 5.0 %collective-permute-start = (bf16[208,128]{1,0:T(8,128)(2,1)S(1)}, bf16[208,128]{1,0:T(8,128)(2,1)S(1)}, u32[]{:S(2)}, u32[]{:S(2)}) collective-permute-start(bf16[208,128]{1,0:T(8,128)(2,1)S(1)} %bitcast.73), channel_id=1, source_target_pairs={{0,8},{2,10},{4,12},{6,14},{8,0},{10,2},{12,4},{14,6},{16,24},{18,... | collective-permute-start | bytes 159752 | tf_op jit(solution)/shard_map/ppermute | solution.py:923
  12.7 8.3 %collective-permute-start.3 = (bf16[4,208,128]{2,1,0:T(8,128)(2,1)S(1)}, bf16[4,208,128]{2,1,0:T(8,128)(2,1)S(1)}, u32[]{:S(2)}, u32[]{:S(2)}) collective-permute-start(bf16[4,208,128]{2,1,0:T(8,128)(2,1)S(1)} %pad_maximum_fusion.1.refs_0_), channel_id=1, source_target_pairs={{0,2},{2,0},{4,6},{6,4},{8,10},{10,8},{12,14},{14,12},{16,18},{18,... | collective-permute-start | bytes 638984 | tf_op jit(solution)/shard_map/ppermute | solution.py:923
  14.3 12.3 %collective-permute-start.4 = (bf16[4,208,128]{2,1,0:T(8,128)(2,1)S(1)}, bf16[4,208,128]{2,1,0:T(8,128)(2,1)S(1)}, u32[]{:S(2)}, u32[]{:S(2)}) collective-permute-start(bf16[4,208,128]{2,1,0:T(8,128)(2,1)S(1)} %pad_maximum_fusion.1.refs_0_), channel_id=1, source_target_pairs={{0,4},{2,6},{4,0},{6,2},{8,12},{10,14},{12,8},{14,10},{16,20},{18,... | collective-permute-start | bytes 638984 | tf_op jit(solution)/shard_map/ppermute | solution.py:923
  15.8 17.3 %collective-permute-start.5 = (bf16[4,208,128]{2,1,0:T(8,128)(2,1)S(1)}, bf16[4,208,128]{2,1,0:T(8,128)(2,1)S(1)}, u32[]{:S(2)}, u32[]{:S(2)}) collective-permute-start(bf16[4,208,128]{2,1,0:T(8,128)(2,1)S(1)} %pad_maximum_fusion.1.refs_0_), channel_id=1, source_target_pairs={{0,6},{2,4},{4,2},{6,0},{8,14},{10,12},{12,10},{14,8},{16,22},{18,... | collective-permute-start | bytes 638984 | tf_op jit(solution)/shard_map/ppermute | solution.py:923
  16.3 25.4 %all-to-all-start = ((bf16[8,3,2,4,16,256]{5,4,3,2,1,0:T(8,128)(2,1)}), bf16[8,3,2,4,16,256]{5,4,3,2,1,0:T(8,128)(2,1)}, u32[]{:S(2)}, u32[]{:S(2)}) async-start(bf16[8,3,2,4,16,256]{5,4,3,2,1,0:T(8,128)(2,1)} %cut.1), calls=%async_computation | async-start | bytes 3145728 | tf_op jit(solution)/shard_map/all_to_all | solution.py:916
  20.6 13.1 %collective-permute-start.6 = (bf16[4,208,128]{2,1,0:T(8,128)(2,1)S(1)}, bf16[4,208,128]{2,1,0:T(8,128)(2,1)S(1)}, u32[]{:S(2)}, u32[]{:S(2)}) collective-permute-start(bf16[4,208,128]{2,1,0:T(8,128)(2,1)S(1)} %pad_maximum_fusion.1.refs_0_), channel_id=1, source_target_pairs={{0,1},{1,0},{2,3},{3,2},{4,5},{5,4},{6,7},{7,6},{8,9},{9,8},{10,11... | collective-permute-start | bytes 638984 | tf_op jit(solution)/shard_map/ppermute | solution.py:926
  21.0 12.8 %collective-permute-start.7 = (bf16[4,208,128]{2,1,0:T(8,128)(2,1)S(1)}, bf16[4,208,128]{2,1,0:T(8,128)(2,1)S(1)}, u32[]{:S(2)}, u32[]{:S(2)}) collective-permute-start(bf16[4,208,128]{2,1,0:T(8,128)(2,1)S(1)} %collective-permute-done.3.refs_1_), channel_id=1, source_target_pairs={{0,1},{1,0},{2,3},{3,2},{4,5},{5,4},{6,7},{7,6},{8,9},{9,8},{10,11... | collective-permute-start | bytes 638984 | tf_op jit(solution)/shard_map/ppermute | solution.py:926
  26.6 7.2 %collective-permute-start.8 = (bf16[4,208,128]{2,1,0:T(8,128)(2,1)S(1)}, bf16[4,208,128]{2,1,0:T(8,128)(2,1)S(1)}, u32[]{:S(2)}, u32[]{:S(2)}) collective-permute-start(bf16[4,208,128]{2,1,0:T(8,128)(2,1)S(1)} %collective-permute-done.4.refs_2_), channel_id=1, source_target_pairs={{0,1},{1,0},{2,3},{3,2},{4,5},{5,4},{6,7},{7,6},{8,9},{9,8},{10,11... | collective-permute-start | bytes 638984 | tf_op jit(solution)/shard_map/ppermute | solution.py:926
  33.1 2.1 %collective-permute-start.9 = (bf16[4,208,128]{2,1,0:T(8,128)(2,1)S(1)}, bf16[4,208,128]{2,1,0:T(8,128)(2,1)}, u32[]{:S(2)}, u32[]{:S(2)}) collective-permute-start(bf16[4,208,128]{2,1,0:T(8,128)(2,1)S(1)} %collective-permute-done.5.refs_3_), channel_id=1, source_target_pairs={{0,1},{1,0},{2,3},{3,2},{4,5},{5,4},{6,7},{7,6},{8,9},{9,8},{10,11... | collective-permute-start | bytes 638984 | tf_op jit(solution)/shard_map/ppermute | solution.py:926
  56.0 4.5 %collective-permute-start.10 = (bf16[4,3,208,128]{3,2,1,0:T(8,128)(2,1)}, bf16[4,3,208,128]{3,2,1,0:T(8,128)(2,1)S(1)}, u32[]{:S(2)}, u32[]{:S(2)}) collective-permute-start(bf16[4,3,208,128]{3,2,1,0:T(8,128)(2,1)} %get-tuple-element.43), channel_id=1, source_target_pairs={{0,1},{1,0},{2,3},{3,2},{4,5},{5,4},{6,7},{7,6},{8,9},{9,8},{10,11... | collective-permute-start | bytes 1916936 | tf_op jit(solution)/shard_map/ppermute | solution.py:926
  56.1 17.8 %all-to-all-start.1 = ((bf16[8,4,48,256]{3,2,1,0:T(8,128)(2,1)}), bf16[8,4,48,256]{3,2,1,0:T(8,128)(2,1)S(1)}, u32[]{:S(2)}, u32[]{:S(2)}) async-start(bf16[8,4,48,256]{3,2,1,0:T(8,128)(2,1)} %bitcast.68), calls=%async_computation.1 | async-start | bytes 1572864 | tf_op jit(solution)/shard_map/all_to_all | solution.py:916
  62.5 16.5 %collective-permute-start.13 = (bf16[3,208,128]{2,1,0:T(8,128)(2,1)}, bf16[3,208,128]{2,1,0:T(8,128)(2,1)S(1)}, u32[]{:S(2)}, u32[]{:S(2)}) collective-permute-start(bf16[3,208,128]{2,1,0:T(8,128)(2,1)} %get-tuple-element.54), channel_id=1, source_target_pairs={{0,6},{2,4},{4,2},{6,0},{8,14},{10,12},{12,10},{14,8},{16,22},{18,... | collective-permute-start | bytes 479240 | tf_op jit(solution)/shard_map/ppermute | solution.py:923
  65.5 14.2 %collective-permute-start.12 = (bf16[3,208,128]{2,1,0:T(8,128)(2,1)}, bf16[3,208,128]{2,1,0:T(8,128)(2,1)}, u32[]{:S(2)}, u32[]{:S(2)}) collective-permute-start(bf16[3,208,128]{2,1,0:T(8,128)(2,1)} %get-tuple-element.55), channel_id=1, source_target_pairs={{0,4},{2,6},{4,0},{6,2},{8,12},{10,14},{12,8},{14,10},{16,20},{18,... | collective-permute-start | bytes 479240 | tf_op jit(solution)/shard_map/ppermute | solution.py:923
  66.0 13.6 %collective-permute-start.11 = (bf16[3,208,128]{2,1,0:T(8,128)(2,1)}, bf16[3,208,128]{2,1,0:T(8,128)(2,1)}, u32[]{:S(2)}, u32[]{:S(2)}) collective-permute-start(bf16[3,208,128]{2,1,0:T(8,128)(2,1)} %get-tuple-element.53), channel_id=1, source_target_pairs={{0,2},{2,0},{4,6},{6,4},{8,10},{10,8},{12,14},{14,12},{16,18},{18,... | collective-permute-start | bytes 479240 | tf_op jit(solution)/shard_map/ppermute | solution.py:923
  73.9 18.3 %all-to-all-start.2 = ((bf16[8,4,48,256]{3,2,1,0:T(8,128)(2,1)}), bf16[8,4,48,256]{3,2,1,0:T(8,128)(2,1)S(1)}, u32[]{:S(2)}, u32[]{:S(2)}) async-start(bf16[8,4,48,256]{3,2,1,0:T(8,128)(2,1)} %bitcast.67), calls=%async_computation.2 | async-start | bytes 1572864 | tf_op jit(solution)/shard_map/all_to_all | solution.py:916
  81.7 1.5 %collective-permute-start.14 = (bf16[4,1,208,128]{3,2,1,0:T(8,128)(2,1)S(1)}, bf16[4,1,208,128]{3,2,1,0:T(8,128)(2,1)S(1)}, u32[]{:S(2)}, u32[]{:S(2)}) collective-permute-start(bf16[4,1,208,128]{3,2,1,0:T(8,128)(2,1)S(1)} %copy-done.9), channel_id=1, source_target_pairs={{0,1},{1,0},{2,3},{3,2},{4,5},{5,4},{6,7},{7,6},{8,9},{9,8},{10,11... | collective-permute-start | bytes 638984 | tf_op jit(solution)/shard_map/ppermute | solution.py:926
  83.3 8.2 %collective-permute-start.17 = (bf16[1,208,128]{2,1,0:T(8,128)(2,1)S(1)}, bf16[1,208,128]{2,1,0:T(8,128)(2,1)S(1)}, u32[]{:S(2)}, u32[]{:S(2)}) collective-permute-start(bf16[1,208,128]{2,1,0:T(8,128)(2,1)S(1)} %get-tuple-element.62), channel_id=1, source_target_pairs={{0,6},{2,4},{4,2},{6,0},{8,14},{10,12},{12,10},{14,8},{16,22},{18,... | collective-permute-start | bytes 159752 | tf_op jit(solution)/shard_map/ppermute | solution.py:923
  85.7 6.4 %collective-permute-start.16 = (bf16[1,208,128]{2,1,0:T(8,128)(2,1)S(1)}, bf16[1,208,128]{2,1,0:T(8,128)(2,1)S(1)}, u32[]{:S(2)}, u32[]{:S(2)}) collective-permute-start(bf16[1,208,128]{2,1,0:T(8,128)(2,1)S(1)} %get-tuple-element.63), channel_id=1, source_target_pairs={{0,4},{2,6},{4,0},{6,2},{8,12},{10,14},{12,8},{14,10},{16,20},{18,... | collective-permute-start | bytes 159752 | tf_op jit(solution)/shard_map/ppermute | solution.py:923
  86.3 5.8 %collective-permute-start.15 = (bf16[1,208,128]{2,1,0:T(8,128)(2,1)S(1)}, bf16[1,208,128]{2,1,0:T(8,128)(2,1)S(1)}, u32[]{:S(2)}, u32[]{:S(2)}) collective-permute-start(bf16[1,208,128]{2,1,0:T(8,128)(2,1)S(1)} %get-tuple-element.61), channel_id=1, source_target_pairs={{0,2},{2,0},{4,6},{6,4},{8,10},{10,8},{12,14},{14,12},{16,18},{18,... | collective-permute-start | bytes 159752 | tf_op jit(solution)/shard_map/ppermute | solution.py:923
  92.3 6.5 %collective-permute-start.20 = (bf16[208,128]{1,0:T(8,128)(2,1)S(1)}, bf16[208,128]{1,0:T(8,128)(2,1)S(1)}, u32[]{:S(2)}, u32[]{:S(2)}) collective-permute-start(bf16[208,128]{1,0:T(8,128)(2,1)S(1)} %get-tuple-element.59), channel_id=1, source_target_pairs={{0,24},{2,26},{4,28},{6,30},{8,16},{10,18},{12,20},{14,22},{16,8},... | collective-permute-start | bytes 159752 | tf_op jit(solution)/shard_map/ppermute | solution.py:923
  95.1 5.7 %collective-permute-start.19 = (bf16[208,128]{1,0:T(8,128)(2,1)S(1)}, bf16[208,128]{1,0:T(8,128)(2,1)S(1)}, u32[]{:S(2)}, u32[]{:S(2)}) collective-permute-start(bf16[208,128]{1,0:T(8,128)(2,1)S(1)} %get-tuple-element.60), channel_id=1, source_target_pairs={{0,16},{2,18},{4,20},{6,22},{8,24},{10,26},{12,28},{14,30},{16,0},... | collective-permute-start | bytes 159752 | tf_op jit(solution)/shard_map/ppermute | solution.py:923
  95.2 5.5 %collective-permute-start.18 = (bf16[208,128]{1,0:T(8,128)(2,1)S(1)}, bf16[208,128]{1,0:T(8,128)(2,1)S(1)}, u32[]{:S(2)}, u32[]{:S(2)}) collective-permute-start(bf16[208,128]{1,0:T(8,128)(2,1)S(1)} %get-tuple-element.58), channel_id=1, source_target_pairs={{0,8},{2,10},{4,12},{6,14},{8,0},{10,2},{12,4},{14,6},{16,24},{18,... | collective-permute-start | bytes 159752 | tf_op jit(solution)/shard_map/ppermute | solution.py:923
  (10 other events, 46.4 us)

commit v6 on v5

--- a/solution.py
+++ b/solution.py
@@ -167,7 +167,7 @@
 LOG2E = 1.4426950408889634
 SCORE_RATE = HEAD**-0.5 * LOG2E
 PIECE = 128
-SLAB = 32
+SLAB = 16
 GELU_RATE = (2.0 / jnp.pi) ** 0.5
 GELU_CUBE = GELU_RATE * 0.044715
 
@@ -925,9 +925,11 @@
     def swap_core(value):
         return lax.ppermute(value, "dp", [(0, 1), (1, 0)])
 
-    blank = jnp.zeros((plan.rows - 1) * LANES, BF16)
-    blank = jnp.concatenate([blank, jnp.broadcast_to(column_rows[0, 0].astype(BF16), (LANES,))])
-    own = lax.dynamic_update_slice(blank, flat_params, (shift,)).reshape(plan.rows, LANES)
+    wide = jnp.pad(flat_params, (LANES, plan.rows * LANES - plan.shard))
+    own = lax.dynamic_slice(wide, (LANES - shift,), (plan.rows * LANES,))
+    index = lax.iota(jnp.int32, plan.rows * LANES)
+    own = jnp.where(index >= (plan.rows - 1) * LANES, column_rows[0, 0].astype(BF16), own)
+    own = own.reshape(plan.rows, LANES)
     if plan.pairwise:
         arrived = [swap_seq(own, PLANE * k) for k in range(1, plan.deep)]
         deep = jnp.stack([own] + arrived)
@@ -953,29 +955,32 @@
         place, both, w_qkv, w_out, w_in, w_back, vectors, bias_in
     )
 
-    layer_out = to_rows(out)
+    moved_out = exchange(out.reshape(group, local_rows, owned, D))
 
     def core_sum(keep, send):
         return keep.astype(F32) + swap_core(send).astype(F32)
 
-    def plane_sum(value):
-        total = value[0]
+    def plane_swap(value):
         sent = value.astype(BF16)
-        for k in range(1, PLANE):
-            total = total + swap_seq(sent[k], k).astype(F32)
+        return [value[0]] + [swap_seq(sent[k], k) for k in range(1, PLANE)]
+
+    def added(pieces):
+        total = pieces[0]
+        for piece in pieces[1:]:
+            total = total + piece.astype(F32)
         return total
 
-    later = plane_sum(core_sum(keep, send))
+    later = added(plane_swap(core_sum(keep, send)))
 
     grad_x, lead_keep, lead_send = back(plan, steps, local_rows)(
         place, both, packed, branch, w_qkv, w_out, vectors, logsum, first
     )
-    (lead_keep, lead_send), layer_out, later = lax.optimization_barrier(
-        ((lead_keep, lead_send), layer_out, later)
-    )
-    total = jnp.concatenate([plane_sum(core_sum(lead_keep, lead_send)), later], axis=0)
+    lead_send, moved_out, later = lax.optimization_barrier((lead_send, moved_out, later))
+    lead = plane_swap(core_sum(lead_keep, lead_send))
+    total = jnp.concatenate([added(lead), later], axis=0)
     moved_x = exchange(grad_x.reshape(group, local_rows, owned, D))
-    total, moved_x = lax.optimization_barrier((total, moved_x))
+    total, moved_x, moved_out = lax.optimization_barrier((total, moved_x, moved_out))
+    layer_out = moved_out.transpose(1, 0, 2, 3).reshape(tokens.shape)
     input_grad = moved_x.transpose(1, 0, 2, 3).reshape(tokens.shape).astype(F32)
     if plan.pairwise:
         sent = total.astype(BF16)

time: 102 us -> 101 us (level)
  local copies, waits for them, and re-layouts: 6.46 us -> 5.25 us
  other arithmetic: 4.05 us -> 5.12 us
    dynamic_update_slice x1 -> x0, local copies, waits for them, and re-layouts: 1.15 us -> none  [local(): lax.dynamic_update_slice(blank, flat_params, (shift,))]
    another operation x1 -> x2, other arithmetic: 0.03 us -> 1.09 us  [local(): deep = jnp.stack([own] + arrived)]
  transfers between devices with their start and end apart: 24 -> 24, of which waited for: 11 -> 10; matrix products, arithmetic and copies ran while one was open for 6% -> 6% of each run, Pallas kernels for 14% -> 14%
where the time goes in v6:
time: 101 us
  starting transfers between devices  35 us (35%)
  Pallas kernels  28.3 us (28%)
  waiting for transfers between devices  26.1 us (26%)
  local copies, waits for them, and re-layouts  5.25 us (5%)
  other arithmetic  5.12 us (5%)
    ppermute x15, waiting for transfers between devices, swap_seq(): return lax.ppermute(value, 'seq', [(i, i ^ distance) for i in range(seq)])  22.1 us
    ppermute x15, starting transfers between devices, swap_seq(): return lax.ppermute(value, 'seq', [(i, i ^ distance) for i in range(seq)])  20.8 us
    pallas_call x1, Pallas kernels, local(): layer(plan, steps, local_rows)  14 us
    all_to_all x3, starting transfers between devices, exchange(): lax.all_to_all(blocks, 'seq', 0, 0, axis_index_groups=groups, tiled=True)  13.8 us
    pallas_call x1, Pallas kernels, local(): back(plan, steps, local_rows)  7.85 us
    pallas_call x1, Pallas kernels, local(): w_qkv, w_out, w_in, w_back, vectors, bias_in = prepare(plan)(place, *pieces)  3.85 us
    pallas_call x1, Pallas kernels, local(): pl.pallas_call(cut_kernel(group, steps), out_shape=jax.ShapeDtypeStruct((...  2.61 us
    all_to_all x3, waiting for transfers between devices, exchange(): lax.all_to_all(blocks, 'seq', 0, 0, axis_index_groups=groups, tiled=True)  2.6 us
  transfers between devices with their start and end apart: 24, of which 10 were waited for; matrix products, arithmetic and copies ran while one was open for 6% of the time, Pallas kernels for 14%

profile of v6, /device:TPU:0, one launch (start us, length us, event | category | flops | bytes accessed | tf_op | source)
XLA Modules:
  0.0 100.7 jit_solution(826121594129857469)
XLA Ops:
  2.4 5.1 %collective-permute-start.2 = (bf16[208,128]{1,0:T(8,128)(2,1)S(1)}, bf16[208,128]{1,0:T(8,128)(2,1)S(1)}, u32[]{:S(2)}, u32[]{:S(2)}) collective-permute-start(bf16[208,128]{1,0:T(8,128)(2,1)S(1)} %get-tuple-element.65), channel_id=1, source_target_pairs={{0,24},{2,26},{4,28},{6,30},{8,16},{10,18},{12,20},{14,22},{16,8},... | collective-permute-start | bytes 159752 | tf_op jit(solution)/shard_map/ppermute | solution.py:923
  8.1 2.6 %cut.1 = bf16[8,3,2,4,16,256]{5,4,3,2,1,0:T(8,128)(2,1)} custom-call(bf16[4,384,256]{2,1,0:T(8,128)(2,1)} %bitcast.71, bf16[4,384,256]{2,1,0:T(8,128)(2,1)} %bitcast.72), custom_call_target="tpu_custom_call" | custom-call | tf_op jit(solution)/shard_map/cut/pallas_call | solution.py:940
  10.7 1.8 %collective-permute-done.1 = bf16[208,128]{1,0:T(8,128)(2,1)S(1)} collective-permute-done((bf16[208,128]{1,0:T(8,128)(2,1)S(1)}, bf16[208,128]{1,0:T(8,128)(2,1)S(1)}, u32[]{:S(2)}, u32[]{:S(2)}) %collective-permute-start.1) | collective-permute-done | bytes 53280 | tf_op jit(solution)/shard_map/ppermute | solution.py:923
  12.6 1.6 %collective-permute-start.3 = (bf16[4,208,128]{2,1,0:T(8,128)(2,1)S(1)}, bf16[4,208,128]{2,1,0:T(8,128)(2,1)S(1)}, u32[]{:S(2)}, u32[]{:S(2)}) collective-permute-start(bf16[4,208,128]{2,1,0:T(8,128)(2,1)S(1)} %pad_maximum_fusion.1.refs_0_), channel_id=1, source_target_pairs={{0,2},{2,0},{4,6},{6,4},{8,10},{10,8},{12,14},{14,12},{16,18},{18,... | collective-permute-start | bytes 638984 | tf_op jit(solution)/shard_map/ppermute | solution.py:923
  14.1 1.5 %collective-permute-start.4 = (bf16[4,208,128]{2,1,0:T(8,128)(2,1)S(1)}, bf16[4,208,128]{2,1,0:T(8,128)(2,1)S(1)}, u32[]{:S(2)}, u32[]{:S(2)}) collective-permute-start(bf16[4,208,128]{2,1,0:T(8,128)(2,1)S(1)} %pad_maximum_fusion.1.refs_0_), channel_id=1, source_target_pairs={{0,4},{2,6},{4,0},{6,2},{8,12},{10,14},{12,8},{14,10},{16,20},{18,... | collective-permute-start | bytes 638984 | tf_op jit(solution)/shard_map/ppermute | solution.py:923
  16.1 4.3 %all-to-all-start = ((bf16[8,3,2,4,16,256]{5,4,3,2,1,0:T(8,128)(2,1)}), bf16[8,3,2,4,16,256]{5,4,3,2,1,0:T(8,128)(2,1)}, u32[]{:S(2)}, u32[]{:S(2)}) async-start(bf16[8,3,2,4,16,256]{5,4,3,2,1,0:T(8,128)(2,1)} %cut.1), calls=%async_computation | async-start | bytes 3145728 | tf_op jit(solution)/shard_map/all_to_all | solution.py:916
  21.0 5.4 %collective-permute-done.4.refs_2_ = bf16[4,208,128]{2,1,0:T(8,128)(2,1)S(1)} collective-permute-done((bf16[4,208,128]{2,1,0:T(8,128)(2,1)S(1)}, bf16[4,208,128]{2,1,0:T(8,128)(2,1)S(1)}, u32[]{:S(2)}, u32[]{:S(2)}) %collective-permute-start.4) | collective-permute-done | bytes 213024 | tf_op jit(solution)/shard_map/ppermute | solution.py:923
  26.4 6.5 %collective-permute-done.5.refs_3_ = bf16[4,208,128]{2,1,0:T(8,128)(2,1)S(1)} collective-permute-done((bf16[4,208,128]{2,1,0:T(8,128)(2,1)S(1)}, bf16[4,208,128]{2,1,0:T(8,128)(2,1)S(1)}, u32[]{:S(2)}, u32[]{:S(2)}) %collective-permute-start.5) | collective-permute-done | bytes 213024 | tf_op jit(solution)/shard_map/ppermute | solution.py:923
  35.1 3.8 %prepare.1 = (bf16[256,768]{1,0:T(8,128)(2,1)}, bf16[256,256]{1,0:T(8,128)(2,1)}, bf16[256,1024]{1,0:T(8,128)(2,1)}, bf16[1024,256]{1,0:T(8,128)(2,1)}, f32[8,256]{1,0:T(8,128)}, /*index=5*/f32[8,1024]{1,0:T(8,128)}) custom-call(s32[4]{0:T(128)} %pad_add_fusion.place_ref, bf16[4,208,128]{2,1,0:T(8,128)(2,1)} %copy-done.1, bf16[4,208,128]{2,1,0:T(8,128)(2,1)} %copy-done.3, ...), custom_call_target="tpu_custom_call" | custom-call | flops 25500000256 | bytes 4000000 | tf_op jit(solution)/shard_map/prepare/pallas_call | solution.py:952
  38.9 2.6 %all-to-all-done.both = bf16[8,3,2,4,16,256]{5,4,3,2,1,0:T(8,128)(2,1)} async-done(((bf16[8,3,2,4,16,256]{5,4,3,2,1,0:T(8,128)(2,1)}), bf16[8,3,2,4,16,256]{5,4,3,2,1,0:T(8,128)(2,1)}, u32[]{:S(2)}, u32[]{:S(2)}) %all-to-all-start) | async-done | bytes 1572896 | tf_op jit(solution)/shard_map/all_to_all | solution.py:916
  41.5 14.0 %layer.1 = (bf16[1536,768]{1,0:T(8,128)(2,1)}, f32[16,256]{1,0:T(8,128)}, bf16[32,48,256]{2,1,0:T(8,128)(2,1)}, bf16[1536,256]{1,0:T(8,128)(2,1)}, bf16[4,3,208,...) custom-call(s32[4]{0:T(128)} %pad_add_fusion.place_ref, ...), custom_call_target="tpu_custom_call" | custom-call | flops 15000000512 | bytes 10000000 | tf_op jit(solution)/shard_map/layer/pallas_call | solution.py:954
  55.6 4.3 %all-to-all-start.1 = ((bf16[8,4,48,256]{3,2,1,0:T(8,128)(2,1)}), bf16[8,4,48,256]{3,2,1,0:T(8,128)(2,1)S(1)}, u32[]{:S(2)}, u32[]{:S(2)}) async-start(bf16[8,4,48,256]{3,2,1,0:T(8,128)(2,1)} %bitcast.69), calls=%async_computation.1 | async-start | bytes 1572864 | tf_op jit(solution)/shard_map/all_to_all | solution.py:916
  59.9 1.2 %fusion.13 = (bf16[4,3,208,128]{3,2,1,0:T(8,128)(2,1)S(1)}, f32[4,3,208,128]{3,2,1,0:T(8,128)}) fusion(bf16[4,3,208,128]{3,2,1,0:T(8,128)(2,1)S(1)} %collective-permute-done.10, bf16[4,3,208,128]{3,2,1,0:T(8,128)(2,1)S(1)} %copy-done), kind=kLoop, calls=%fused_computation.33 | loop fusion | flops 1277952 | bytes 3194880 | tf_op jit(solution)/shard_map/convert_element_type | solution.py:964
  61.9 2.9 %collective-permute-start.13 = (bf16[3,208,128]{2,1,0:T(8,128)(2,1)}, bf16[3,208,128]{2,1,0:T(8,128)(2,1)S(1)}, u32[]{:S(2)}, u32[]{:S(2)}) collective-permute-start(bf16[3,208,128]{2,1,0:T(8,128)(2,1)} %get-tuple-element.54), channel_id=1, source_target_pairs={{0,6},{2,4},{4,2},{6,0},{8,14},{10,12},{12,10},{14,8},{16,22},{18,... | collective-permute-start | bytes 479240 | tf_op jit(solution)/shard_map/ppermute | solution.py:923
  65.4 7.9 %back.1 = (bf16[32,48,256]{2,1,0:T(8,128)(2,1)}, bf16[4,1,208,128]{3,2,1,0:T(8,128)(2,1)}, bf16[4,1,208,128]{3,2,1,0:T(8,128)(2,1)}) custom-call(s32[4]{0:T(128)} %pad_add_fusion.place_ref, bf16[8,3,2,4,16,256]{5,4,3,2,1,0:T(8,128)(2,1)} %all-to-all-done.both, bf16[1536,768]{1,0:T(8,128)(2,1)} %get-tuple-element.35.packed, ...), custom_call_target="tpu_custom_call" | custom-call | flops 10000000000 | bytes 8000000 | tf_op jit(solution)/shard_map/back/pallas_call | solution.py:975
  73.3 5.2 %all-to-all-start.2 = ((bf16[8,4,48,256]{3,2,1,0:T(8,128)(2,1)}), bf16[8,4,48,256]{3,2,1,0:T(8,128)(2,1)S(1)}, u32[]{:S(2)}, u32[]{:S(2)}) async-start(bf16[8,4,48,256]{3,2,1,0:T(8,128)(2,1)} %bitcast.68), calls=%async_computation.2 | async-start | bytes 1572864 | tf_op jit(solution)/shard_map/all_to_all | solution.py:916
  79.0 1.2 %fusion.2 = f32[3,208,128]{2,1,0:T(8,128)S(1)} fusion(f32[4,3,208,128]{3,2,1,0:T(8,128)} %get-tuple-element.52, bf16[3,208,128]{2,1,0:T(8,128)(2,1)S(1)} %collective-permute-done.13, bf16[3,208,128]{2,1,0:T(8,128)(2,1)} %collective-permute-done.12, bf16[3,208,128]{2,1,0:T(8,128)(2,1)} %collective-permute-done.11), kind=kLoop, calls=%fused_computation.7 | loop fusion | flops 479232 | bytes 1118208 | tf_op jit(solution)/shard_map/add | solution.py:970
  80.3 1.4 %collective-permute-done.14 = bf16[4,1,208,128]{3,2,1,0:T(8,128)(2,1)S(1)} collective-permute-done((bf16[4,1,208,128]{3,2,1,0:T(8,128)(2,1)S(1)}, bf16[4,1,208,128]{3,2,1,0:T(8,128)(2,1)S(1)}, u32[]{:S(2)}, u32[]{:S(2)}) %collective-permute-start.14) | collective-permute-done | bytes 213024 | tf_op jit(solution)/shard_map/ppermute | solution.py:926
  81.8 2.5 %collective-permute-start.17 = (bf16[1,208,128]{2,1,0:T(8,128)(2,1)S(1)}, bf16[1,208,128]{2,1,0:T(8,128)(2,1)S(1)}, u32[]{:S(2)}, u32[]{:S(2)}) collective-permute-start(bf16[1,208,128]{2,1,0:T(8,128)(2,1)S(1)} %get-tuple-element.62), channel_id=1, source_target_pairs={{0,6},{2,4},{4,2},{6,0},{8,14},{10,12},{12,10},{14,8},{16,22},{18,... | collective-permute-start | bytes 159752 | tf_op jit(solution)/shard_map/ppermute | solution.py:923
  85.4 5.7 %collective-permute-done.17 = bf16[1,208,128]{2,1,0:T(8,128)(2,1)S(1)} collective-permute-done((bf16[1,208,128]{2,1,0:T(8,128)(2,1)S(1)}, bf16[1,208,128]{2,1,0:T(8,128)(2,1)S(1)}, u32[]{:S(2)}, u32[]{:S(2)}) %collective-permute-start.17) | collective-permute-done | bytes 53280 | tf_op jit(solution)/shard_map/ppermute | solution.py:923
  91.8 2.5 %collective-permute-start.20 = (bf16[208,128]{1,0:T(8,128)(2,1)S(1)}, bf16[208,128]{1,0:T(8,128)(2,1)S(1)}, u32[]{:S(2)}, u32[]{:S(2)}) collective-permute-start(bf16[208,128]{1,0:T(8,128)(2,1)S(1)} %get-tuple-element.59), channel_id=1, source_target_pairs={{0,24},{2,26},{4,28},{6,30},{8,16},{10,18},{12,20},{14,22},{16,8},... | collective-permute-start | bytes 159752 | tf_op jit(solution)/shard_map/ppermute | solution.py:923
  94.4 1.9 %collective-permute-start.18 = (bf16[208,128]{1,0:T(8,128)(2,1)S(1)}, bf16[208,128]{1,0:T(8,128)(2,1)S(1)}, u32[]{:S(2)}, u32[]{:S(2)}) collective-permute-start(bf16[208,128]{1,0:T(8,128)(2,1)S(1)} %get-tuple-element.58), channel_id=1, source_target_pairs={{0,8},{2,10},{4,12},{6,14},{8,0},{10,2},{12,4},{14,6},{16,24},{18,... | collective-permute-start | bytes 159752 | tf_op jit(solution)/shard_map/ppermute | solution.py:923
  97.4 1.3 %copy.8 = f32[4,8,48,256]{3,2,1,0:T(8,128)} copy(f32[4,8,48,256]{3,2,0,1:T(8,128)S(1)} %convert_bitcast_fusion) | data formatting | bytes 3145728 | tf_op jit(solution)/shard_map/convert_element_type | solution.py:984
  98.7 1.3 %collective-permute-done.19 = bf16[208,128]{1,0:T(8,128)(2,1)S(1)} collective-permute-done((bf16[208,128]{1,0:T(8,128)(2,1)S(1)}, bf16[208,128]{1,0:T(8,128)(2,1)S(1)}, u32[]{:S(2)}, u32[]{:S(2)}) %collective-permute-start.19) | collective-permute-done | bytes 53280 | tf_op jit(solution)/shard_map/ppermute | solution.py:923
  (66 shorter events, 11.4 us)
Async XLA Ops:
  2.4 8.4 %collective-permute-start.2 = (bf16[208,128]{1,0:T(8,128)(2,1)S(1)}, bf16[208,128]{1,0:T(8,128)(2,1)S(1)}, u32[]{:S(2)}, u32[]{:S(2)}) collective-permute-start(bf16[208,128]{1,0:T(8,128)(2,1)S(1)} %get-tuple-element.65), channel_id=1, source_target_pairs={{0,24},{2,26},{4,28},{6,30},{8,16},{10,18},{12,20},{14,22},{16,8},... | collective-permute-start | bytes 159752 | tf_op jit(solution)/shard_map/ppermute | solution.py:923
  7.5 5.0 %collective-permute-start.1 = (bf16[208,128]{1,0:T(8,128)(2,1)S(1)}, bf16[208,128]{1,0:T(8,128)(2,1)S(1)}, u32[]{:S(2)}, u32[]{:S(2)}) collective-permute-start(bf16[208,128]{1,0:T(8,128)(2,1)S(1)} %get-tuple-element.65), channel_id=1, source_target_pairs={{0,16},{2,18},{4,20},{6,22},{8,24},{10,26},{12,28},{14,30},{16,0},... | collective-permute-start | bytes 159752 | tf_op jit(solution)/shard_map/ppermute | solution.py:923
  7.5 5.0 %collective-permute-start = (bf16[208,128]{1,0:T(8,128)(2,1)S(1)}, bf16[208,128]{1,0:T(8,128)(2,1)S(1)}, u32[]{:S(2)}, u32[]{:S(2)}) collective-permute-start(bf16[208,128]{1,0:T(8,128)(2,1)S(1)} %get-tuple-element.65), channel_id=1, source_target_pairs={{0,8},{2,10},{4,12},{6,14},{8,0},{10,2},{12,4},{14,6},{16,24},{18,... | collective-permute-start | bytes 159752 | tf_op jit(solution)/shard_map/ppermute | solution.py:923
  12.6 8.3 %collective-permute-start.3 = (bf16[4,208,128]{2,1,0:T(8,128)(2,1)S(1)}, bf16[4,208,128]{2,1,0:T(8,128)(2,1)S(1)}, u32[]{:S(2)}, u32[]{:S(2)}) collective-permute-start(bf16[4,208,128]{2,1,0:T(8,128)(2,1)S(1)} %pad_maximum_fusion.1.refs_0_), channel_id=1, source_target_pairs={{0,2},{2,0},{4,6},{6,4},{8,10},{10,8},{12,14},{14,12},{16,18},{18,... | collective-permute-start | bytes 638984 | tf_op jit(solution)/shard_map/ppermute | solution.py:923
  14.1 12.3 %collective-permute-start.4 = (bf16[4,208,128]{2,1,0:T(8,128)(2,1)S(1)}, bf16[4,208,128]{2,1,0:T(8,128)(2,1)S(1)}, u32[]{:S(2)}, u32[]{:S(2)}) collective-permute-start(bf16[4,208,128]{2,1,0:T(8,128)(2,1)S(1)} %pad_maximum_fusion.1.refs_0_), channel_id=1, source_target_pairs={{0,4},{2,6},{4,0},{6,2},{8,12},{10,14},{12,8},{14,10},{16,20},{18,... | collective-permute-start | bytes 638984 | tf_op jit(solution)/shard_map/ppermute | solution.py:923
  15.6 17.3 %collective-permute-start.5 = (bf16[4,208,128]{2,1,0:T(8,128)(2,1)S(1)}, bf16[4,208,128]{2,1,0:T(8,128)(2,1)S(1)}, u32[]{:S(2)}, u32[]{:S(2)}) collective-permute-start(bf16[4,208,128]{2,1,0:T(8,128)(2,1)S(1)} %pad_maximum_fusion.1.refs_0_), channel_id=1, source_target_pairs={{0,6},{2,4},{4,2},{6,0},{8,14},{10,12},{12,10},{14,8},{16,22},{18,... | collective-permute-start | bytes 638984 | tf_op jit(solution)/shard_map/ppermute | solution.py:923
  16.1 25.4 %all-to-all-start = ((bf16[8,3,2,4,16,256]{5,4,3,2,1,0:T(8,128)(2,1)}), bf16[8,3,2,4,16,256]{5,4,3,2,1,0:T(8,128)(2,1)}, u32[]{:S(2)}, u32[]{:S(2)}) async-start(bf16[8,3,2,4,16,256]{5,4,3,2,1,0:T(8,128)(2,1)} %cut.1), calls=%async_computation | async-start | bytes 3145728 | tf_op jit(solution)/shard_map/all_to_all | solution.py:916
  20.4 13.2 %collective-permute-start.6 = (bf16[4,208,128]{2,1,0:T(8,128)(2,1)S(1)}, bf16[4,208,128]{2,1,0:T(8,128)(2,1)S(1)}, u32[]{:S(2)}, u32[]{:S(2)}) collective-permute-start(bf16[4,208,128]{2,1,0:T(8,128)(2,1)S(1)} %pad_maximum_fusion.1.refs_0_), channel_id=1, source_target_pairs={{0,1},{1,0},{2,3},{3,2},{4,5},{5,4},{6,7},{7,6},{8,9},{9,8},{10,11... | collective-permute-start | bytes 638984 | tf_op jit(solution)/shard_map/ppermute | solution.py:926
  20.8 12.8 %collective-permute-start.7 = (bf16[4,208,128]{2,1,0:T(8,128)(2,1)S(1)}, bf16[4,208,128]{2,1,0:T(8,128)(2,1)S(1)}, u32[]{:S(2)}, u32[]{:S(2)}) collective-permute-start(bf16[4,208,128]{2,1,0:T(8,128)(2,1)S(1)} %collective-permute-done.3.refs_1_), channel_id=1, source_target_pairs={{0,1},{1,0},{2,3},{3,2},{4,5},{5,4},{6,7},{7,6},{8,9},{9,8},{10,11... | collective-permute-start | bytes 638984 | tf_op jit(solution)/shard_map/ppermute | solution.py:926
  26.4 7.2 %collective-permute-start.8 = (bf16[4,208,128]{2,1,0:T(8,128)(2,1)S(1)}, bf16[4,208,128]{2,1,0:T(8,128)(2,1)S(1)}, u32[]{:S(2)}, u32[]{:S(2)}) collective-permute-start(bf16[4,208,128]{2,1,0:T(8,128)(2,1)S(1)} %collective-permute-done.4.refs_2_), channel_id=1, source_target_pairs={{0,1},{1,0},{2,3},{3,2},{4,5},{5,4},{6,7},{7,6},{8,9},{9,8},{10,11... | collective-permute-start | bytes 638984 | tf_op jit(solution)/shard_map/ppermute | solution.py:926
  32.9 2.1 %collective-permute-start.9 = (bf16[4,208,128]{2,1,0:T(8,128)(2,1)S(1)}, bf16[4,208,128]{2,1,0:T(8,128)(2,1)}, u32[]{:S(2)}, u32[]{:S(2)}) collective-permute-start(bf16[4,208,128]{2,1,0:T(8,128)(2,1)S(1)} %collective-permute-done.5.refs_3_), channel_id=1, source_target_pairs={{0,1},{1,0},{2,3},{3,2},{4,5},{5,4},{6,7},{7,6},{8,9},{9,8},{10,11... | collective-permute-start | bytes 638984 | tf_op jit(solution)/shard_map/ppermute | solution.py:926
  55.5 4.4 %collective-permute-start.10 = (bf16[4,3,208,128]{3,2,1,0:T(8,128)(2,1)}, bf16[4,3,208,128]{3,2,1,0:T(8,128)(2,1)S(1)}, u32[]{:S(2)}, u32[]{:S(2)}) collective-permute-start(bf16[4,3,208,128]{3,2,1,0:T(8,128)(2,1)} %get-tuple-element.43), channel_id=1, source_target_pairs={{0,1},{1,0},{2,3},{3,2},{4,5},{5,4},{6,7},{7,6},{8,9},{9,8},{10,11... | collective-permute-start | bytes 1916936 | tf_op jit(solution)/shard_map/ppermute | solution.py:926
  55.6 17.7 %all-to-all-start.1 = ((bf16[8,4,48,256]{3,2,1,0:T(8,128)(2,1)}), bf16[8,4,48,256]{3,2,1,0:T(8,128)(2,1)S(1)}, u32[]{:S(2)}, u32[]{:S(2)}) async-start(bf16[8,4,48,256]{3,2,1,0:T(8,128)(2,1)} %bitcast.69), calls=%async_computation.1 | async-start | bytes 1572864 | tf_op jit(solution)/shard_map/all_to_all | solution.py:916
  61.9 16.6 %collective-permute-start.13 = (bf16[3,208,128]{2,1,0:T(8,128)(2,1)}, bf16[3,208,128]{2,1,0:T(8,128)(2,1)S(1)}, u32[]{:S(2)}, u32[]{:S(2)}) collective-permute-start(bf16[3,208,128]{2,1,0:T(8,128)(2,1)} %get-tuple-element.54), channel_id=1, source_target_pairs={{0,6},{2,4},{4,2},{6,0},{8,14},{10,12},{12,10},{14,8},{16,22},{18,... | collective-permute-start | bytes 479240 | tf_op jit(solution)/shard_map/ppermute | solution.py:923
  64.8 14.2 %collective-permute-start.12 = (bf16[3,208,128]{2,1,0:T(8,128)(2,1)}, bf16[3,208,128]{2,1,0:T(8,128)(2,1)}, u32[]{:S(2)}, u32[]{:S(2)}) collective-permute-start(bf16[3,208,128]{2,1,0:T(8,128)(2,1)} %get-tuple-element.55), channel_id=1, source_target_pairs={{0,4},{2,6},{4,0},{6,2},{8,12},{10,14},{12,8},{14,10},{16,20},{18,... | collective-permute-start | bytes 479240 | tf_op jit(solution)/shard_map/ppermute | solution.py:923
  65.4 13.6 %collective-permute-start.11 = (bf16[3,208,128]{2,1,0:T(8,128)(2,1)}, bf16[3,208,128]{2,1,0:T(8,128)(2,1)}, u32[]{:S(2)}, u32[]{:S(2)}) collective-permute-start(bf16[3,208,128]{2,1,0:T(8,128)(2,1)} %get-tuple-element.53), channel_id=1, source_target_pairs={{0,2},{2,0},{4,6},{6,4},{8,10},{10,8},{12,14},{14,12},{16,18},{18,... | collective-permute-start | bytes 479240 | tf_op jit(solution)/shard_map/ppermute | solution.py:923
  73.3 18.4 %all-to-all-start.2 = ((bf16[8,4,48,256]{3,2,1,0:T(8,128)(2,1)}), bf16[8,4,48,256]{3,2,1,0:T(8,128)(2,1)S(1)}, u32[]{:S(2)}, u32[]{:S(2)}) async-start(bf16[8,4,48,256]{3,2,1,0:T(8,128)(2,1)} %bitcast.68), calls=%async_computation.2 | async-start | bytes 1572864 | tf_op jit(solution)/shard_map/all_to_all | solution.py:916
  80.2 1.5 %collective-permute-start.14 = (bf16[4,1,208,128]{3,2,1,0:T(8,128)(2,1)S(1)}, bf16[4,1,208,128]{3,2,1,0:T(8,128)(2,1)S(1)}, u32[]{:S(2)}, u32[]{:S(2)}) collective-permute-start(bf16[4,1,208,128]{3,2,1,0:T(8,128)(2,1)S(1)} %copy-done.9), channel_id=1, source_target_pairs={{0,1},{1,0},{2,3},{3,2},{4,5},{5,4},{6,7},{7,6},{8,9},{9,8},{10,11... | collective-permute-start | bytes 638984 | tf_op jit(solution)/shard_map/ppermute | solution.py:926
  81.8 9.3 %collective-permute-start.17 = (bf16[1,208,128]{2,1,0:T(8,128)(2,1)S(1)}, bf16[1,208,128]{2,1,0:T(8,128)(2,1)S(1)}, u32[]{:S(2)}, u32[]{:S(2)}) collective-permute-start(bf16[1,208,128]{2,1,0:T(8,128)(2,1)S(1)} %get-tuple-element.62), channel_id=1, source_target_pairs={{0,6},{2,4},{4,2},{6,0},{8,14},{10,12},{12,10},{14,8},{16,22},{18,... | collective-permute-start | bytes 159752 | tf_op jit(solution)/shard_map/ppermute | solution.py:923
  84.3 7.3 %collective-permute-start.16 = (bf16[1,208,128]{2,1,0:T(8,128)(2,1)S(1)}, bf16[1,208,128]{2,1,0:T(8,128)(2,1)S(1)}, u32[]{:S(2)}, u32[]{:S(2)}) collective-permute-start(bf16[1,208,128]{2,1,0:T(8,128)(2,1)S(1)} %get-tuple-element.63), channel_id=1, source_target_pairs={{0,4},{2,6},{4,0},{6,2},{8,12},{10,14},{12,8},{14,10},{16,20},{18,... | collective-permute-start | bytes 159752 | tf_op jit(solution)/shard_map/ppermute | solution.py:923
  84.9 6.8 %collective-permute-start.15 = (bf16[1,208,128]{2,1,0:T(8,128)(2,1)S(1)}, bf16[1,208,128]{2,1,0:T(8,128)(2,1)S(1)}, u32[]{:S(2)}, u32[]{:S(2)}) collective-permute-start(bf16[1,208,128]{2,1,0:T(8,128)(2,1)S(1)} %get-tuple-element.61), channel_id=1, source_target_pairs={{0,2},{2,0},{4,6},{6,4},{8,10},{10,8},{12,14},{14,12},{16,18},{18,... | collective-permute-start | bytes 159752 | tf_op jit(solution)/shard_map/ppermute | solution.py:923
  91.8 6.9 %collective-permute-start.20 = (bf16[208,128]{1,0:T(8,128)(2,1)S(1)}, bf16[208,128]{1,0:T(8,128)(2,1)S(1)}, u32[]{:S(2)}, u32[]{:S(2)}) collective-permute-start(bf16[208,128]{1,0:T(8,128)(2,1)S(1)} %get-tuple-element.59), channel_id=1, source_target_pairs={{0,24},{2,26},{4,28},{6,30},{8,16},{10,18},{12,20},{14,22},{16,8},... | collective-permute-start | bytes 159752 | tf_op jit(solution)/shard_map/ppermute | solution.py:923
  94.4 5.6 %collective-permute-start.19 = (bf16[208,128]{1,0:T(8,128)(2,1)S(1)}, bf16[208,128]{1,0:T(8,128)(2,1)S(1)}, u32[]{:S(2)}, u32[]{:S(2)}) collective-permute-start(bf16[208,128]{1,0:T(8,128)(2,1)S(1)} %get-tuple-element.60), channel_id=1, source_target_pairs={{0,16},{2,18},{4,20},{6,22},{8,24},{10,26},{12,28},{14,30},{16,0},... | collective-permute-start | bytes 159752 | tf_op jit(solution)/shard_map/ppermute | solution.py:923
  94.4 5.5 %collective-permute-start.18 = (bf16[208,128]{1,0:T(8,128)(2,1)S(1)}, bf16[208,128]{1,0:T(8,128)(2,1)S(1)}, u32[]{:S(2)}, u32[]{:S(2)}) collective-permute-start(bf16[208,128]{1,0:T(8,128)(2,1)S(1)} %get-tuple-element.58), channel_id=1, source_target_pairs={{0,8},{2,10},{4,12},{6,14},{8,0},{10,2},{12,4},{14,6},{16,24},{18,... | collective-permute-start | bytes 159752 | tf_op jit(solution)/shard_map/ppermute | solution.py:923
  (10 other events, 54.7 us)

commit v7 on v6

--- a/solution.py
+++ b/solution.py
@@ -427,12 +427,12 @@
             inside = slice(index * SLAB, (index + 1) * SLAB)
             rows = slice(tile * TILE + index * SLAB, tile * TILE + (index + 1) * SLAB)
             value = inner[slot, inside] + bias_in[0:1, cut]
-            cube = value * (GELU_CUBE * (value * value))
-            angle = GELU_RATE * value + cube
-            bend = jnp.tanh(angle)
+            curve = GELU_CUBE * (value * value)
+            bend = jnp.tanh(value * (GELU_RATE + curve))
             gate = 0.5 * bend + 0.5
             activated[rows, cut] = (value * gate).astype(BF16)
-            slope = gate * ((1.0 - bend) * (angle + (cube + cube)) + 1.0)
+            rise = (gate * (1.0 - bend)) * value
+            slope = gate + rise * (GELU_RATE + 3.0 * curve)
             grad = grad_act[slot, inside] * slope
             grad_inner[rows, cut] = grad.astype(BF16)
             name = f"bias{part}"

time: 101 us -> 102 us (level)
  no operation moved by 1% of the time
where the time goes in v7:
time: 102 us; the launch traced here: 101 us
  starting transfers between devices  35.1 us (34%)
  Pallas kernels  28.5 us (28%)
  waiting for transfers between devices  26.2 us (26%)
  local copies, waits for them, and re-layouts  5.25 us (5%)
  other arithmetic  5.12 us (5%)
    ppermute x15, waiting for transfers between devices, swap_seq(): return lax.ppermute(value, 'seq', [(i, i ^ distance) for i in range(seq)])  22.2 us
    ppermute x15, starting transfers between devices, swap_seq(): return lax.ppermute(value, 'seq', [(i, i ^ distance) for i in range(seq)])  20.8 us
    pallas_call x1, Pallas kernels, local(): layer(plan, steps, local_rows)  14.2 us
    all_to_all x3, starting transfers between devices, exchange(): lax.all_to_all(blocks, 'seq', 0, 0, axis_index_groups=groups, tiled=True)  13.7 us
    pallas_call x1, Pallas kernels, local(): back(plan, steps, local_rows)  7.85 us
    pallas_call x1, Pallas kernels, local(): w_qkv, w_out, w_in, w_back, vectors, bias_in = prepare(plan)(place, *pieces)  3.85 us
    pallas_call x1, Pallas kernels, local(): pl.pallas_call(cut_kernel(group, steps), out_shape=jax.ShapeDtypeStruct((...  2.61 us
    all_to_all x3, waiting for transfers between devices, exchange(): lax.all_to_all(blocks, 'seq', 0, 0, axis_index_groups=groups, tiled=True)  2.6 us
  transfers between devices with their start and end apart: 24, of which 10 were waited for; matrix products, arithmetic and copies ran while one was open for 6% of the time, Pallas kernels for 14%

profile of v7, /device:TPU:0, one launch (start us, length us, event | category | flops | bytes accessed | tf_op | source)
XLA Modules:
  0.0 101.1 jit_solution(2463548451886058325)
XLA Ops:
  2.4 5.1 %collective-permute-start.2 = (bf16[208,128]{1,0:T(8,128)(2,1)S(1)}, bf16[208,128]{1,0:T(8,128)(2,1)S(1)}, u32[]{:S(2)}, u32[]{:S(2)}) collective-permute-start(bf16[208,128]{1,0:T(8,128)(2,1)S(1)} %get-tuple-element.65), channel_id=1, source_target_pairs={{0,24},{2,26},{4,28},{6,30},{8,16},{10,18},{12,20},{14,22},{16,8},... | collective-permute-start | bytes 159752 | tf_op jit(solution)/shard_map/ppermute | solution.py:923
  8.1 2.6 %cut.1 = bf16[8,3,2,4,16,256]{5,4,3,2,1,0:T(8,128)(2,1)} custom-call(bf16[4,384,256]{2,1,0:T(8,128)(2,1)} %bitcast.71, bf16[4,384,256]{2,1,0:T(8,128)(2,1)} %bitcast.72), custom_call_target="tpu_custom_call" | custom-call | tf_op jit(solution)/shard_map/cut/pallas_call | solution.py:940
  10.7 1.8 %collective-permute-done.1 = bf16[208,128]{1,0:T(8,128)(2,1)S(1)} collective-permute-done((bf16[208,128]{1,0:T(8,128)(2,1)S(1)}, bf16[208,128]{1,0:T(8,128)(2,1)S(1)}, u32[]{:S(2)}, u32[]{:S(2)}) %collective-permute-start.1) | collective-permute-done | bytes 53280 | tf_op jit(solution)/shard_map/ppermute | solution.py:923
  12.6 1.6 %collective-permute-start.3 = (bf16[4,208,128]{2,1,0:T(8,128)(2,1)S(1)}, bf16[4,208,128]{2,1,0:T(8,128)(2,1)S(1)}, u32[]{:S(2)}, u32[]{:S(2)}) collective-permute-start(bf16[4,208,128]{2,1,0:T(8,128)(2,1)S(1)} %pad_maximum_fusion.1.refs_0_), channel_id=1, source_target_pairs={{0,2},{2,0},{4,6},{6,4},{8,10},{10,8},{12,14},{14,12},{16,18},{18,... | collective-permute-start | bytes 638984 | tf_op jit(solution)/shard_map/ppermute | solution.py:923
  14.1 1.5 %collective-permute-start.4 = (bf16[4,208,128]{2,1,0:T(8,128)(2,1)S(1)}, bf16[4,208,128]{2,1,0:T(8,128)(2,1)S(1)}, u32[]{:S(2)}, u32[]{:S(2)}) collective-permute-start(bf16[4,208,128]{2,1,0:T(8,128)(2,1)S(1)} %pad_maximum_fusion.1.refs_0_), channel_id=1, source_target_pairs={{0,4},{2,6},{4,0},{6,2},{8,12},{10,14},{12,8},{14,10},{16,20},{18,... | collective-permute-start | bytes 638984 | tf_op jit(solution)/shard_map/ppermute | solution.py:923
  16.1 4.3 %all-to-all-start = ((bf16[8,3,2,4,16,256]{5,4,3,2,1,0:T(8,128)(2,1)}), bf16[8,3,2,4,16,256]{5,4,3,2,1,0:T(8,128)(2,1)}, u32[]{:S(2)}, u32[]{:S(2)}) async-start(bf16[8,3,2,4,16,256]{5,4,3,2,1,0:T(8,128)(2,1)} %cut.1), calls=%async_computation | async-start | bytes 3145728 | tf_op jit(solution)/shard_map/all_to_all | solution.py:916
  21.0 5.4 %collective-permute-done.4.refs_2_ = bf16[4,208,128]{2,1,0:T(8,128)(2,1)S(1)} collective-permute-done((bf16[4,208,128]{2,1,0:T(8,128)(2,1)S(1)}, bf16[4,208,128]{2,1,0:T(8,128)(2,1)S(1)}, u32[]{:S(2)}, u32[]{:S(2)}) %collective-permute-start.4) | collective-permute-done | bytes 213024 | tf_op jit(solution)/shard_map/ppermute | solution.py:923
  26.4 6.5 %collective-permute-done.5.refs_3_ = bf16[4,208,128]{2,1,0:T(8,128)(2,1)S(1)} collective-permute-done((bf16[4,208,128]{2,1,0:T(8,128)(2,1)S(1)}, bf16[4,208,128]{2,1,0:T(8,128)(2,1)S(1)}, u32[]{:S(2)}, u32[]{:S(2)}) %collective-permute-start.5) | collective-permute-done | bytes 213024 | tf_op jit(solution)/shard_map/ppermute | solution.py:923
  35.1 3.8 %prepare.1 = (bf16[256,768]{1,0:T(8,128)(2,1)}, bf16[256,256]{1,0:T(8,128)(2,1)}, bf16[256,1024]{1,0:T(8,128)(2,1)}, bf16[1024,256]{1,0:T(8,128)(2,1)}, f32[8,256]{1,0:T(8,128)}, /*index=5*/f32[8,1024]{1,0:T(8,128)}) custom-call(s32[4]{0:T(128)} %pad_add_fusion.place_ref, bf16[4,208,128]{2,1,0:T(8,128)(2,1)} %copy-done.1, bf16[4,208,128]{2,1,0:T(8,128)(2,1)} %copy-done.3, ...), custom_call_target="tpu_custom_call" | custom-call | flops 25500000256 | bytes 4000000 | tf_op jit(solution)/shard_map/prepare/pallas_call | solution.py:952
  38.9 2.6 %all-to-all-done.both = bf16[8,3,2,4,16,256]{5,4,3,2,1,0:T(8,128)(2,1)} async-done(((bf16[8,3,2,4,16,256]{5,4,3,2,1,0:T(8,128)(2,1)}), bf16[8,3,2,4,16,256]{5,4,3,2,1,0:T(8,128)(2,1)}, u32[]{:S(2)}, u32[]{:S(2)}) %all-to-all-start) | async-done | bytes 1572896 | tf_op jit(solution)/shard_map/all_to_all | solution.py:916
  41.5 14.2 %layer.1 = (bf16[1536,768]{1,0:T(8,128)(2,1)}, f32[16,256]{1,0:T(8,128)}, bf16[32,48,256]{2,1,0:T(8,128)(2,1)}, bf16[1536,256]{1,0:T(8,128)(2,1)}, bf16[4,3,208,...) custom-call(s32[4]{0:T(128)} %pad_add_fusion.place_ref, ...), custom_call_target="tpu_custom_call" | custom-call | flops 15000000512 | bytes 10000000 | tf_op jit(solution)/shard_map/layer/pallas_call | solution.py:954
  56.0 4.1 %all-to-all-start.1 = ((bf16[8,4,48,256]{3,2,1,0:T(8,128)(2,1)}), bf16[8,4,48,256]{3,2,1,0:T(8,128)(2,1)S(1)}, u32[]{:S(2)}, u32[]{:S(2)}) async-start(bf16[8,4,48,256]{3,2,1,0:T(8,128)(2,1)} %bitcast.69), calls=%async_computation.1 | async-start | bytes 1572864 | tf_op jit(solution)/shard_map/all_to_all | solution.py:916
  60.2 1.2 %fusion.13 = (bf16[4,3,208,128]{3,2,1,0:T(8,128)(2,1)S(1)}, f32[4,3,208,128]{3,2,1,0:T(8,128)}) fusion(bf16[4,3,208,128]{3,2,1,0:T(8,128)(2,1)S(1)} %collective-permute-done.10, bf16[4,3,208,128]{3,2,1,0:T(8,128)(2,1)S(1)} %copy-done), kind=kLoop, calls=%fused_computation.33 | loop fusion | flops 1277952 | bytes 3194880 | tf_op jit(solution)/shard_map/convert_element_type | solution.py:964
  62.2 2.9 %collective-permute-start.13 = (bf16[3,208,128]{2,1,0:T(8,128)(2,1)}, bf16[3,208,128]{2,1,0:T(8,128)(2,1)S(1)}, u32[]{:S(2)}, u32[]{:S(2)}) collective-permute-start(bf16[3,208,128]{2,1,0:T(8,128)(2,1)} %get-tuple-element.54), channel_id=1, source_target_pairs={{0,6},{2,4},{4,2},{6,0},{8,14},{10,12},{12,10},{14,8},{16,22},{18,... | collective-permute-start | bytes 479240 | tf_op jit(solution)/shard_map/ppermute | solution.py:923
  65.6 7.8 %back.1 = (bf16[32,48,256]{2,1,0:T(8,128)(2,1)}, bf16[4,1,208,128]{3,2,1,0:T(8,128)(2,1)}, bf16[4,1,208,128]{3,2,1,0:T(8,128)(2,1)}) custom-call(s32[4]{0:T(128)} %pad_add_fusion.place_ref, bf16[8,3,2,4,16,256]{5,4,3,2,1,0:T(8,128)(2,1)} %all-to-all-done.both, bf16[1536,768]{1,0:T(8,128)(2,1)} %get-tuple-element.35.packed, ...), custom_call_target="tpu_custom_call" | custom-call | flops 10000000000 | bytes 8000000 | tf_op jit(solution)/shard_map/back/pallas_call | solution.py:975
  73.5 5.2 %all-to-all-start.2 = ((bf16[8,4,48,256]{3,2,1,0:T(8,128)(2,1)}), bf16[8,4,48,256]{3,2,1,0:T(8,128)(2,1)S(1)}, u32[]{:S(2)}, u32[]{:S(2)}) async-start(bf16[8,4,48,256]{3,2,1,0:T(8,128)(2,1)} %bitcast.68), calls=%async_computation.2 | async-start | bytes 1572864 | tf_op jit(solution)/shard_map/all_to_all | solution.py:916
  79.5 1.2 %fusion.2 = f32[3,208,128]{2,1,0:T(8,128)S(1)} fusion(f32[4,3,208,128]{3,2,1,0:T(8,128)} %get-tuple-element.52, bf16[3,208,128]{2,1,0:T(8,128)(2,1)S(1)} %collective-permute-done.13, bf16[3,208,128]{2,1,0:T(8,128)(2,1)} %collective-permute-done.12, bf16[3,208,128]{2,1,0:T(8,128)(2,1)} %collective-permute-done.11), kind=kLoop, calls=%fused_computation.7 | loop fusion | flops 479232 | bytes 1118208 | tf_op jit(solution)/shard_map/add | solution.py:970
  80.7 1.4 %collective-permute-done.14 = bf16[4,1,208,128]{3,2,1,0:T(8,128)(2,1)S(1)} collective-permute-done((bf16[4,1,208,128]{3,2,1,0:T(8,128)(2,1)S(1)}, bf16[4,1,208,128]{3,2,1,0:T(8,128)(2,1)S(1)}, u32[]{:S(2)}, u32[]{:S(2)}) %collective-permute-start.14) | collective-permute-done | bytes 213024 | tf_op jit(solution)/shard_map/ppermute | solution.py:926
  82.3 2.3 %collective-permute-start.17 = (bf16[1,208,128]{2,1,0:T(8,128)(2,1)S(1)}, bf16[1,208,128]{2,1,0:T(8,128)(2,1)S(1)}, u32[]{:S(2)}, u32[]{:S(2)}) collective-permute-start(bf16[1,208,128]{2,1,0:T(8,128)(2,1)S(1)} %get-tuple-element.62), channel_id=1, source_target_pairs={{0,6},{2,4},{4,2},{6,0},{8,14},{10,12},{12,10},{14,8},{16,22},{18,... | collective-permute-start | bytes 159752 | tf_op jit(solution)/shard_map/ppermute | solution.py:923
  85.8 5.7 %collective-permute-done.17 = bf16[1,208,128]{2,1,0:T(8,128)(2,1)S(1)} collective-permute-done((bf16[1,208,128]{2,1,0:T(8,128)(2,1)S(1)}, bf16[1,208,128]{2,1,0:T(8,128)(2,1)S(1)}, u32[]{:S(2)}, u32[]{:S(2)}) %collective-permute-start.17) | collective-permute-done | bytes 53280 | tf_op jit(solution)/shard_map/ppermute | solution.py:923
  92.2 2.5 %collective-permute-start.20 = (bf16[208,128]{1,0:T(8,128)(2,1)S(1)}, bf16[208,128]{1,0:T(8,128)(2,1)S(1)}, u32[]{:S(2)}, u32[]{:S(2)}) collective-permute-start(bf16[208,128]{1,0:T(8,128)(2,1)S(1)} %get-tuple-element.59), channel_id=1, source_target_pairs={{0,24},{2,26},{4,28},{6,30},{8,16},{10,18},{12,20},{14,22},{16,8},... | collective-permute-start | bytes 159752 | tf_op jit(solution)/shard_map/ppermute | solution.py:923
  94.8 1.9 %collective-permute-start.18 = (bf16[208,128]{1,0:T(8,128)(2,1)S(1)}, bf16[208,128]{1,0:T(8,128)(2,1)S(1)}, u32[]{:S(2)}, u32[]{:S(2)}) collective-permute-start(bf16[208,128]{1,0:T(8,128)(2,1)S(1)} %get-tuple-element.58), channel_id=1, source_target_pairs={{0,8},{2,10},{4,12},{6,14},{8,0},{10,2},{12,4},{14,6},{16,24},{18,... | collective-permute-start | bytes 159752 | tf_op jit(solution)/shard_map/ppermute | solution.py:923
  97.8 1.3 %copy.8 = f32[4,8,48,256]{3,2,1,0:T(8,128)} copy(f32[4,8,48,256]{3,2,0,1:T(8,128)S(1)} %convert_bitcast_fusion) | data formatting | bytes 3145728 | tf_op jit(solution)/shard_map/convert_element_type | solution.py:984
  99.1 1.3 %collective-permute-done.19 = bf16[208,128]{1,0:T(8,128)(2,1)S(1)} collective-permute-done((bf16[208,128]{1,0:T(8,128)(2,1)S(1)}, bf16[208,128]{1,0:T(8,128)(2,1)S(1)}, u32[]{:S(2)}, u32[]{:S(2)}) %collective-permute-start.19) | collective-permute-done | bytes 53280 | tf_op jit(solution)/shard_map/ppermute | solution.py:923
  (66 shorter events, 11.9 us)
Async XLA Ops:
  2.4 8.4 %collective-permute-start.2 = (bf16[208,128]{1,0:T(8,128)(2,1)S(1)}, bf16[208,128]{1,0:T(8,128)(2,1)S(1)}, u32[]{:S(2)}, u32[]{:S(2)}) collective-permute-start(bf16[208,128]{1,0:T(8,128)(2,1)S(1)} %get-tuple-element.65), channel_id=1, source_target_pairs={{0,24},{2,26},{4,28},{6,30},{8,16},{10,18},{12,20},{14,22},{16,8},... | collective-permute-start | bytes 159752 | tf_op jit(solution)/shard_map/ppermute | solution.py:923
  7.5 5.0 %collective-permute-start.1 = (bf16[208,128]{1,0:T(8,128)(2,1)S(1)}, bf16[208,128]{1,0:T(8,128)(2,1)S(1)}, u32[]{:S(2)}, u32[]{:S(2)}) collective-permute-start(bf16[208,128]{1,0:T(8,128)(2,1)S(1)} %get-tuple-element.65), channel_id=1, source_target_pairs={{0,16},{2,18},{4,20},{6,22},{8,24},{10,26},{12,28},{14,30},{16,0},... | collective-permute-start | bytes 159752 | tf_op jit(solution)/shard_map/ppermute | solution.py:923
  7.5 5.0 %collective-permute-start = (bf16[208,128]{1,0:T(8,128)(2,1)S(1)}, bf16[208,128]{1,0:T(8,128)(2,1)S(1)}, u32[]{:S(2)}, u32[]{:S(2)}) collective-permute-start(bf16[208,128]{1,0:T(8,128)(2,1)S(1)} %get-tuple-element.65), channel_id=1, source_target_pairs={{0,8},{2,10},{4,12},{6,14},{8,0},{10,2},{12,4},{14,6},{16,24},{18,... | collective-permute-start | bytes 159752 | tf_op jit(solution)/shard_map/ppermute | solution.py:923
  12.6 8.3 %collective-permute-start.3 = (bf16[4,208,128]{2,1,0:T(8,128)(2,1)S(1)}, bf16[4,208,128]{2,1,0:T(8,128)(2,1)S(1)}, u32[]{:S(2)}, u32[]{:S(2)}) collective-permute-start(bf16[4,208,128]{2,1,0:T(8,128)(2,1)S(1)} %pad_maximum_fusion.1.refs_0_), channel_id=1, source_target_pairs={{0,2},{2,0},{4,6},{6,4},{8,10},{10,8},{12,14},{14,12},{16,18},{18,... | collective-permute-start | bytes 638984 | tf_op jit(solution)/shard_map/ppermute | solution.py:923
  14.1 12.3 %collective-permute-start.4 = (bf16[4,208,128]{2,1,0:T(8,128)(2,1)S(1)}, bf16[4,208,128]{2,1,0:T(8,128)(2,1)S(1)}, u32[]{:S(2)}, u32[]{:S(2)}) collective-permute-start(bf16[4,208,128]{2,1,0:T(8,128)(2,1)S(1)} %pad_maximum_fusion.1.refs_0_), channel_id=1, source_target_pairs={{0,4},{2,6},{4,0},{6,2},{8,12},{10,14},{12,8},{14,10},{16,20},{18,... | collective-permute-start | bytes 638984 | tf_op jit(solution)/shard_map/ppermute | solution.py:923
  15.6 17.3 %collective-permute-start.5 = (bf16[4,208,128]{2,1,0:T(8,128)(2,1)S(1)}, bf16[4,208,128]{2,1,0:T(8,128)(2,1)S(1)}, u32[]{:S(2)}, u32[]{:S(2)}) collective-permute-start(bf16[4,208,128]{2,1,0:T(8,128)(2,1)S(1)} %pad_maximum_fusion.1.refs_0_), channel_id=1, source_target_pairs={{0,6},{2,4},{4,2},{6,0},{8,14},{10,12},{12,10},{14,8},{16,22},{18,... | collective-permute-start | bytes 638984 | tf_op jit(solution)/shard_map/ppermute | solution.py:923
  16.1 25.4 %all-to-all-start = ((bf16[8,3,2,4,16,256]{5,4,3,2,1,0:T(8,128)(2,1)}), bf16[8,3,2,4,16,256]{5,4,3,2,1,0:T(8,128)(2,1)}, u32[]{:S(2)}, u32[]{:S(2)}) async-start(bf16[8,3,2,4,16,256]{5,4,3,2,1,0:T(8,128)(2,1)} %cut.1), calls=%async_computation | async-start | bytes 3145728 | tf_op jit(solution)/shard_map/all_to_all | solution.py:916
  20.4 13.2 %collective-permute-start.6 = (bf16[4,208,128]{2,1,0:T(8,128)(2,1)S(1)}, bf16[4,208,128]{2,1,0:T(8,128)(2,1)S(1)}, u32[]{:S(2)}, u32[]{:S(2)}) collective-permute-start(bf16[4,208,128]{2,1,0:T(8,128)(2,1)S(1)} %pad_maximum_fusion.1.refs_0_), channel_id=1, source_target_pairs={{0,1},{1,0},{2,3},{3,2},{4,5},{5,4},{6,7},{7,6},{8,9},{9,8},{10,11... | collective-permute-start | bytes 638984 | tf_op jit(solution)/shard_map/ppermute | solution.py:926
  20.8 12.8 %collective-permute-start.7 = (bf16[4,208,128]{2,1,0:T(8,128)(2,1)S(1)}, bf16[4,208,128]{2,1,0:T(8,128)(2,1)S(1)}, u32[]{:S(2)}, u32[]{:S(2)}) collective-permute-start(bf16[4,208,128]{2,1,0:T(8,128)(2,1)S(1)} %collective-permute-done.3.refs_1_), channel_id=1, source_target_pairs={{0,1},{1,0},{2,3},{3,2},{4,5},{5,4},{6,7},{7,6},{8,9},{9,8},{10,11... | collective-permute-start | bytes 638984 | tf_op jit(solution)/shard_map/ppermute | solution.py:926
  26.4 7.2 %collective-permute-start.8 = (bf16[4,208,128]{2,1,0:T(8,128)(2,1)S(1)}, bf16[4,208,128]{2,1,0:T(8,128)(2,1)S(1)}, u32[]{:S(2)}, u32[]{:S(2)}) collective-permute-start(bf16[4,208,128]{2,1,0:T(8,128)(2,1)S(1)} %collective-permute-done.4.refs_2_), channel_id=1, source_target_pairs={{0,1},{1,0},{2,3},{3,2},{4,5},{5,4},{6,7},{7,6},{8,9},{9,8},{10,11... | collective-permute-start | bytes 638984 | tf_op jit(solution)/shard_map/ppermute | solution.py:926
  32.9 2.1 %collective-permute-start.9 = (bf16[4,208,128]{2,1,0:T(8,128)(2,1)S(1)}, bf16[4,208,128]{2,1,0:T(8,128)(2,1)}, u32[]{:S(2)}, u32[]{:S(2)}) collective-permute-start(bf16[4,208,128]{2,1,0:T(8,128)(2,1)S(1)} %collective-permute-done.5.refs_3_), channel_id=1, source_target_pairs={{0,1},{1,0},{2,3},{3,2},{4,5},{5,4},{6,7},{7,6},{8,9},{9,8},{10,11... | collective-permute-start | bytes 638984 | tf_op jit(solution)/shard_map/ppermute | solution.py:926
  55.7 4.4 %collective-permute-start.10 = (bf16[4,3,208,128]{3,2,1,0:T(8,128)(2,1)}, bf16[4,3,208,128]{3,2,1,0:T(8,128)(2,1)S(1)}, u32[]{:S(2)}, u32[]{:S(2)}) collective-permute-start(bf16[4,3,208,128]{3,2,1,0:T(8,128)(2,1)} %get-tuple-element.43), channel_id=1, source_target_pairs={{0,1},{1,0},{2,3},{3,2},{4,5},{5,4},{6,7},{7,6},{8,9},{9,8},{10,11... | collective-permute-start | bytes 1916936 | tf_op jit(solution)/shard_map/ppermute | solution.py:926
  56.0 17.5 %all-to-all-start.1 = ((bf16[8,4,48,256]{3,2,1,0:T(8,128)(2,1)}), bf16[8,4,48,256]{3,2,1,0:T(8,128)(2,1)S(1)}, u32[]{:S(2)}, u32[]{:S(2)}) async-start(bf16[8,4,48,256]{3,2,1,0:T(8,128)(2,1)} %bitcast.69), calls=%async_computation.1 | async-start | bytes 1572864 | tf_op jit(solution)/shard_map/all_to_all | solution.py:916
  62.2 16.6 %collective-permute-start.13 = (bf16[3,208,128]{2,1,0:T(8,128)(2,1)}, bf16[3,208,128]{2,1,0:T(8,128)(2,1)S(1)}, u32[]{:S(2)}, u32[]{:S(2)}) collective-permute-start(bf16[3,208,128]{2,1,0:T(8,128)(2,1)} %get-tuple-element.54), channel_id=1, source_target_pairs={{0,6},{2,4},{4,2},{6,0},{8,14},{10,12},{12,10},{14,8},{16,22},{18,... | collective-permute-start | bytes 479240 | tf_op jit(solution)/shard_map/ppermute | solution.py:923
  65.1 14.4 %collective-permute-start.12 = (bf16[3,208,128]{2,1,0:T(8,128)(2,1)}, bf16[3,208,128]{2,1,0:T(8,128)(2,1)}, u32[]{:S(2)}, u32[]{:S(2)}) collective-permute-start(bf16[3,208,128]{2,1,0:T(8,128)(2,1)} %get-tuple-element.55), channel_id=1, source_target_pairs={{0,4},{2,6},{4,0},{6,2},{8,12},{10,14},{12,8},{14,10},{16,20},{18,... | collective-permute-start | bytes 479240 | tf_op jit(solution)/shard_map/ppermute | solution.py:923
  65.6 13.8 %collective-permute-start.11 = (bf16[3,208,128]{2,1,0:T(8,128)(2,1)}, bf16[3,208,128]{2,1,0:T(8,128)(2,1)}, u32[]{:S(2)}, u32[]{:S(2)}) collective-permute-start(bf16[3,208,128]{2,1,0:T(8,128)(2,1)} %get-tuple-element.53), channel_id=1, source_target_pairs={{0,2},{2,0},{4,6},{6,4},{8,10},{10,8},{12,14},{14,12},{16,18},{18,... | collective-permute-start | bytes 479240 | tf_op jit(solution)/shard_map/ppermute | solution.py:923
  73.5 18.6 %all-to-all-start.2 = ((bf16[8,4,48,256]{3,2,1,0:T(8,128)(2,1)}), bf16[8,4,48,256]{3,2,1,0:T(8,128)(2,1)S(1)}, u32[]{:S(2)}, u32[]{:S(2)}) async-start(bf16[8,4,48,256]{3,2,1,0:T(8,128)(2,1)} %bitcast.68), calls=%async_computation.2 | async-start | bytes 1572864 | tf_op jit(solution)/shard_map/all_to_all | solution.py:916
  80.6 1.5 %collective-permute-start.14 = (bf16[4,1,208,128]{3,2,1,0:T(8,128)(2,1)S(1)}, bf16[4,1,208,128]{3,2,1,0:T(8,128)(2,1)S(1)}, u32[]{:S(2)}, u32[]{:S(2)}) collective-permute-start(bf16[4,1,208,128]{3,2,1,0:T(8,128)(2,1)S(1)} %copy-done.9), channel_id=1, source_target_pairs={{0,1},{1,0},{2,3},{3,2},{4,5},{5,4},{6,7},{7,6},{8,9},{9,8},{10,11... | collective-permute-start | bytes 638984 | tf_op jit(solution)/shard_map/ppermute | solution.py:926
  82.3 9.2 %collective-permute-start.17 = (bf16[1,208,128]{2,1,0:T(8,128)(2,1)S(1)}, bf16[1,208,128]{2,1,0:T(8,128)(2,1)S(1)}, u32[]{:S(2)}, u32[]{:S(2)}) collective-permute-start(bf16[1,208,128]{2,1,0:T(8,128)(2,1)S(1)} %get-tuple-element.62), channel_id=1, source_target_pairs={{0,6},{2,4},{4,2},{6,0},{8,14},{10,12},{12,10},{14,8},{16,22},{18,... | collective-permute-start | bytes 159752 | tf_op jit(solution)/shard_map/ppermute | solution.py:923
  84.6 7.5 %collective-permute-start.16 = (bf16[1,208,128]{2,1,0:T(8,128)(2,1)S(1)}, bf16[1,208,128]{2,1,0:T(8,128)(2,1)S(1)}, u32[]{:S(2)}, u32[]{:S(2)}) collective-permute-start(bf16[1,208,128]{2,1,0:T(8,128)(2,1)S(1)} %get-tuple-element.63), channel_id=1, source_target_pairs={{0,4},{2,6},{4,0},{6,2},{8,12},{10,14},{12,8},{14,10},{16,20},{18,... | collective-permute-start | bytes 159752 | tf_op jit(solution)/shard_map/ppermute | solution.py:923
  85.1 6.9 %collective-permute-start.15 = (bf16[1,208,128]{2,1,0:T(8,128)(2,1)S(1)}, bf16[1,208,128]{2,1,0:T(8,128)(2,1)S(1)}, u32[]{:S(2)}, u32[]{:S(2)}) collective-permute-start(bf16[1,208,128]{2,1,0:T(8,128)(2,1)S(1)} %get-tuple-element.61), channel_id=1, source_target_pairs={{0,2},{2,0},{4,6},{6,4},{8,10},{10,8},{12,14},{14,12},{16,18},{18,... | collective-permute-start | bytes 159752 | tf_op jit(solution)/shard_map/ppermute | solution.py:923
  92.2 6.9 %collective-permute-start.20 = (bf16[208,128]{1,0:T(8,128)(2,1)S(1)}, bf16[208,128]{1,0:T(8,128)(2,1)S(1)}, u32[]{:S(2)}, u32[]{:S(2)}) collective-permute-start(bf16[208,128]{1,0:T(8,128)(2,1)S(1)} %get-tuple-element.59), channel_id=1, source_target_pairs={{0,24},{2,26},{4,28},{6,30},{8,16},{10,18},{12,20},{14,22},{16,8},... | collective-permute-start | bytes 159752 | tf_op jit(solution)/shard_map/ppermute | solution.py:923
  94.7 5.6 %collective-permute-start.19 = (bf16[208,128]{1,0:T(8,128)(2,1)S(1)}, bf16[208,128]{1,0:T(8,128)(2,1)S(1)}, u32[]{:S(2)}, u32[]{:S(2)}) collective-permute-start(bf16[208,128]{1,0:T(8,128)(2,1)S(1)} %get-tuple-element.60), channel_id=1, source_target_pairs={{0,16},{2,18},{4,20},{6,22},{8,24},{10,26},{12,28},{14,30},{16,0},... | collective-permute-start | bytes 159752 | tf_op jit(solution)/shard_map/ppermute | solution.py:923
  94.8 5.5 %collective-permute-start.18 = (bf16[208,128]{1,0:T(8,128)(2,1)S(1)}, bf16[208,128]{1,0:T(8,128)(2,1)S(1)}, u32[]{:S(2)}, u32[]{:S(2)}) collective-permute-start(bf16[208,128]{1,0:T(8,128)(2,1)S(1)} %get-tuple-element.58), channel_id=1, source_target_pairs={{0,8},{2,10},{4,12},{6,14},{8,0},{10,2},{12,4},{14,6},{16,24},{18,... | collective-permute-start | bytes 159752 | tf_op jit(solution)/shard_map/ppermute | solution.py:923
  (10 other events, 55.2 us)

commit v8 on v7

--- a/solution.py
+++ b/solution.py
@@ -563,11 +563,11 @@
         last = steps - 1
         send_packed(last)
         send_step(last - 1)
-        interleave(finish(tiles - 1), weights[last])
-        for one in closing[last]:
-            one()
+        half = len(weights[last]) // 2
+        interleave(finish(tiles - 1), weights[last][:half])
+        turned = [lambda: flatten(flat, base, r["acc_back"][...].T, ROW_BACK, 2)]
+        interleave(weights[last][half:], turned, closing[last])
         send_step(last)
-        flatten(flat, base, r["acc_back"][...].T, ROW_BACK, 2)
         flatten(flat, base, r["acc_in"][...], ROW_IN, 8)
         flatten(flat, base, r["acc_out"][...], ROW_OUT, 2)
         flatten_vector(flat, ROW_GAIN_TWO - base, column_sum(sums.gain))

time: 102 us -> 102 us (level)
  no operation moved by 1% of the time
where the time goes in v8:
time: 102 us; the launch traced here: 101 us
  starting transfers between devices  35.1 us (34%)
  Pallas kernels  28.5 us (28%)
  waiting for transfers between devices  26.2 us (26%)
  local copies, waits for them, and re-layouts  5.25 us (5%)
  other arithmetic  5.12 us (5%)
    ppermute x15, waiting for transfers between devices, swap_seq(): return lax.ppermute(value, 'seq', [(i, i ^ distance) for i in range(seq)])  22.2 us
    ppermute x15, starting transfers between devices, swap_seq(): return lax.ppermute(value, 'seq', [(i, i ^ distance) for i in range(seq)])  20.8 us
    pallas_call x1, Pallas kernels, local(): layer(plan, steps, local_rows)  14.2 us
    all_to_all x3, starting transfers between devices, exchange(): lax.all_to_all(blocks, 'seq', 0, 0, axis_index_groups=groups, tiled=True)  13.7 us
    pallas_call x1, Pallas kernels, local(): back(plan, steps, local_rows)  7.85 us
    pallas_call x1, Pallas kernels, local(): w_qkv, w_out, w_in, w_back, vectors, bias_in = prepare(plan)(place, *pieces)  3.85 us
    pallas_call x1, Pallas kernels, local(): pl.pallas_call(cut_kernel(group, steps), out_shape=jax.ShapeDtypeStruct((...  2.61 us
    all_to_all x3, waiting for transfers between devices, exchange(): lax.all_to_all(blocks, 'seq', 0, 0, axis_index_groups=groups, tiled=True)  2.6 us
  transfers between devices with their start and end apart: 24, of which 10 were waited for; matrix products, arithmetic and copies ran while one was open for 6% of the time, Pallas kernels for 14%

profile of v8, /device:TPU:0, one launch (start us, length us, event | category | flops | bytes accessed | tf_op | source)
XLA Modules:
  0.0 101.1 jit_solution(3558536483753557606)
XLA Ops:
  2.4 5.1 %collective-permute-start.2 = (bf16[208,128]{1,0:T(8,128)(2,1)S(1)}, bf16[208,128]{1,0:T(8,128)(2,1)S(1)}, u32[]{:S(2)}, u32[]{:S(2)}) collective-permute-start(bf16[208,128]{1,0:T(8,128)(2,1)S(1)} %get-tuple-element.65), channel_id=1, source_target_pairs={{0,24},{2,26},{4,28},{6,30},{8,16},{10,18},{12,20},{14,22},{16,8},... | collective-permute-start | bytes 159752 | tf_op jit(solution)/shard_map/ppermute | solution.py:923
  8.1 2.6 %cut.1 = bf16[8,3,2,4,16,256]{5,4,3,2,1,0:T(8,128)(2,1)} custom-call(bf16[4,384,256]{2,1,0:T(8,128)(2,1)} %bitcast.71, bf16[4,384,256]{2,1,0:T(8,128)(2,1)} %bitcast.72), custom_call_target="tpu_custom_call" | custom-call | tf_op jit(solution)/shard_map/cut/pallas_call | solution.py:940
  10.7 1.8 %collective-permute-done.1 = bf16[208,128]{1,0:T(8,128)(2,1)S(1)} collective-permute-done((bf16[208,128]{1,0:T(8,128)(2,1)S(1)}, bf16[208,128]{1,0:T(8,128)(2,1)S(1)}, u32[]{:S(2)}, u32[]{:S(2)}) %collective-permute-start.1) | collective-permute-done | bytes 53280 | tf_op jit(solution)/shard_map/ppermute | solution.py:923
  12.6 1.6 %collective-permute-start.3 = (bf16[4,208,128]{2,1,0:T(8,128)(2,1)S(1)}, bf16[4,208,128]{2,1,0:T(8,128)(2,1)S(1)}, u32[]{:S(2)}, u32[]{:S(2)}) collective-permute-start(bf16[4,208,128]{2,1,0:T(8,128)(2,1)S(1)} %pad_maximum_fusion.1.refs_0_), channel_id=1, source_target_pairs={{0,2},{2,0},{4,6},{6,4},{8,10},{10,8},{12,14},{14,12},{16,18},{18,... | collective-permute-start | bytes 638984 | tf_op jit(solution)/shard_map/ppermute | solution.py:923
  14.1 1.5 %collective-permute-start.4 = (bf16[4,208,128]{2,1,0:T(8,128)(2,1)S(1)}, bf16[4,208,128]{2,1,0:T(8,128)(2,1)S(1)}, u32[]{:S(2)}, u32[]{:S(2)}) collective-permute-start(bf16[4,208,128]{2,1,0:T(8,128)(2,1)S(1)} %pad_maximum_fusion.1.refs_0_), channel_id=1, source_target_pairs={{0,4},{2,6},{4,0},{6,2},{8,12},{10,14},{12,8},{14,10},{16,20},{18,... | collective-permute-start | bytes 638984 | tf_op jit(solution)/shard_map/ppermute | solution.py:923
  16.1 4.3 %all-to-all-start = ((bf16[8,3,2,4,16,256]{5,4,3,2,1,0:T(8,128)(2,1)}), bf16[8,3,2,4,16,256]{5,4,3,2,1,0:T(8,128)(2,1)}, u32[]{:S(2)}, u32[]{:S(2)}) async-start(bf16[8,3,2,4,16,256]{5,4,3,2,1,0:T(8,128)(2,1)} %cut.1), calls=%async_computation | async-start | bytes 3145728 | tf_op jit(solution)/shard_map/all_to_all | solution.py:916
  21.0 5.4 %collective-permute-done.4.refs_2_ = bf16[4,208,128]{2,1,0:T(8,128)(2,1)S(1)} collective-permute-done((bf16[4,208,128]{2,1,0:T(8,128)(2,1)S(1)}, bf16[4,208,128]{2,1,0:T(8,128)(2,1)S(1)}, u32[]{:S(2)}, u32[]{:S(2)}) %collective-permute-start.4) | collective-permute-done | bytes 213024 | tf_op jit(solution)/shard_map/ppermute | solution.py:923
  26.4 6.5 %collective-permute-done.5.refs_3_ = bf16[4,208,128]{2,1,0:T(8,128)(2,1)S(1)} collective-permute-done((bf16[4,208,128]{2,1,0:T(8,128)(2,1)S(1)}, bf16[4,208,128]{2,1,0:T(8,128)(2,1)S(1)}, u32[]{:S(2)}, u32[]{:S(2)}) %collective-permute-start.5) | collective-permute-done | bytes 213024 | tf_op jit(solution)/shard_map/ppermute | solution.py:923
  35.1 3.8 %prepare.1 = (bf16[256,768]{1,0:T(8,128)(2,1)}, bf16[256,256]{1,0:T(8,128)(2,1)}, bf16[256,1024]{1,0:T(8,128)(2,1)}, bf16[1024,256]{1,0:T(8,128)(2,1)}, f32[8,256]{1,0:T(8,128)}, /*index=5*/f32[8,1024]{1,0:T(8,128)}) custom-call(s32[4]{0:T(128)} %pad_add_fusion.place_ref, bf16[4,208,128]{2,1,0:T(8,128)(2,1)} %copy-done.1, bf16[4,208,128]{2,1,0:T(8,128)(2,1)} %copy-done.3, ...), custom_call_target="tpu_custom_call" | custom-call | flops 25500000256 | bytes 4000000 | tf_op jit(solution)/shard_map/prepare/pallas_call | solution.py:952
  38.9 2.6 %all-to-all-done.both = bf16[8,3,2,4,16,256]{5,4,3,2,1,0:T(8,128)(2,1)} async-done(((bf16[8,3,2,4,16,256]{5,4,3,2,1,0:T(8,128)(2,1)}), bf16[8,3,2,4,16,256]{5,4,3,2,1,0:T(8,128)(2,1)}, u32[]{:S(2)}, u32[]{:S(2)}) %all-to-all-start) | async-done | bytes 1572896 | tf_op jit(solution)/shard_map/all_to_all | solution.py:916
  41.5 14.2 %layer.1 = (bf16[1536,768]{1,0:T(8,128)(2,1)}, f32[16,256]{1,0:T(8,128)}, bf16[32,48,256]{2,1,0:T(8,128)(2,1)}, bf16[1536,256]{1,0:T(8,128)(2,1)}, bf16[4,3,208,...) custom-call(s32[4]{0:T(128)} %pad_add_fusion.place_ref, ...), custom_call_target="tpu_custom_call" | custom-call | flops 15000000512 | bytes 10000000 | tf_op jit(solution)/shard_map/layer/pallas_call | solution.py:954
  56.0 4.1 %all-to-all-start.1 = ((bf16[8,4,48,256]{3,2,1,0:T(8,128)(2,1)}), bf16[8,4,48,256]{3,2,1,0:T(8,128)(2,1)S(1)}, u32[]{:S(2)}, u32[]{:S(2)}) async-start(bf16[8,4,48,256]{3,2,1,0:T(8,128)(2,1)} %bitcast.69), calls=%async_computation.1 | async-start | bytes 1572864 | tf_op jit(solution)/shard_map/all_to_all | solution.py:916
  60.2 1.2 %fusion.13 = (bf16[4,3,208,128]{3,2,1,0:T(8,128)(2,1)S(1)}, f32[4,3,208,128]{3,2,1,0:T(8,128)}) fusion(bf16[4,3,208,128]{3,2,1,0:T(8,128)(2,1)S(1)} %collective-permute-done.10, bf16[4,3,208,128]{3,2,1,0:T(8,128)(2,1)S(1)} %copy-done), kind=kLoop, calls=%fused_computation.33 | loop fusion | flops 1277952 | bytes 3194880 | tf_op jit(solution)/shard_map/convert_element_type | solution.py:964
  62.2 2.9 %collective-permute-start.13 = (bf16[3,208,128]{2,1,0:T(8,128)(2,1)}, bf16[3,208,128]{2,1,0:T(8,128)(2,1)S(1)}, u32[]{:S(2)}, u32[]{:S(2)}) collective-permute-start(bf16[3,208,128]{2,1,0:T(8,128)(2,1)} %get-tuple-element.54), channel_id=1, source_target_pairs={{0,6},{2,4},{4,2},{6,0},{8,14},{10,12},{12,10},{14,8},{16,22},{18,... | collective-permute-start | bytes 479240 | tf_op jit(solution)/shard_map/ppermute | solution.py:923
  65.7 7.9 %back.1 = (bf16[32,48,256]{2,1,0:T(8,128)(2,1)}, bf16[4,1,208,128]{3,2,1,0:T(8,128)(2,1)}, bf16[4,1,208,128]{3,2,1,0:T(8,128)(2,1)}) custom-call(s32[4]{0:T(128)} %pad_add_fusion.place_ref, bf16[8,3,2,4,16,256]{5,4,3,2,1,0:T(8,128)(2,1)} %all-to-all-done.both, bf16[1536,768]{1,0:T(8,128)(2,1)} %get-tuple-element.35.packed, ...), custom_call_target="tpu_custom_call" | custom-call | flops 10000000000 | bytes 8000000 | tf_op jit(solution)/shard_map/back/pallas_call | solution.py:975
  73.6 5.2 %all-to-all-start.2 = ((bf16[8,4,48,256]{3,2,1,0:T(8,128)(2,1)}), bf16[8,4,48,256]{3,2,1,0:T(8,128)(2,1)S(1)}, u32[]{:S(2)}, u32[]{:S(2)}) async-start(bf16[8,4,48,256]{3,2,1,0:T(8,128)(2,1)} %bitcast.68), calls=%async_computation.2 | async-start | bytes 1572864 | tf_op jit(solution)/shard_map/all_to_all | solution.py:916
  79.5 1.2 %fusion.2 = f32[3,208,128]{2,1,0:T(8,128)S(1)} fusion(f32[4,3,208,128]{3,2,1,0:T(8,128)} %get-tuple-element.52, bf16[3,208,128]{2,1,0:T(8,128)(2,1)S(1)} %collective-permute-done.13, bf16[3,208,128]{2,1,0:T(8,128)(2,1)} %collective-permute-done.12, bf16[3,208,128]{2,1,0:T(8,128)(2,1)} %collective-permute-done.11), kind=kLoop, calls=%fused_computation.7 | loop fusion | flops 479232 | bytes 1118208 | tf_op jit(solution)/shard_map/add | solution.py:970
  80.8 1.4 %collective-permute-done.14 = bf16[4,1,208,128]{3,2,1,0:T(8,128)(2,1)S(1)} collective-permute-done((bf16[4,1,208,128]{3,2,1,0:T(8,128)(2,1)S(1)}, bf16[4,1,208,128]{3,2,1,0:T(8,128)(2,1)S(1)}, u32[]{:S(2)}, u32[]{:S(2)}) %collective-permute-start.14) | collective-permute-done | bytes 213024 | tf_op jit(solution)/shard_map/ppermute | solution.py:926
  82.3 2.3 %collective-permute-start.17 = (bf16[1,208,128]{2,1,0:T(8,128)(2,1)S(1)}, bf16[1,208,128]{2,1,0:T(8,128)(2,1)S(1)}, u32[]{:S(2)}, u32[]{:S(2)}) collective-permute-start(bf16[1,208,128]{2,1,0:T(8,128)(2,1)S(1)} %get-tuple-element.62), channel_id=1, source_target_pairs={{0,6},{2,4},{4,2},{6,0},{8,14},{10,12},{12,10},{14,8},{16,22},{18,... | collective-permute-start | bytes 159752 | tf_op jit(solution)/shard_map/ppermute | solution.py:923
  85.9 5.7 %collective-permute-done.17 = bf16[1,208,128]{2,1,0:T(8,128)(2,1)S(1)} collective-permute-done((bf16[1,208,128]{2,1,0:T(8,128)(2,1)S(1)}, bf16[1,208,128]{2,1,0:T(8,128)(2,1)S(1)}, u32[]{:S(2)}, u32[]{:S(2)}) %collective-permute-start.17) | collective-permute-done | bytes 53280 | tf_op jit(solution)/shard_map/ppermute | solution.py:923
  92.2 2.5 %collective-permute-start.20 = (bf16[208,128]{1,0:T(8,128)(2,1)S(1)}, bf16[208,128]{1,0:T(8,128)(2,1)S(1)}, u32[]{:S(2)}, u32[]{:S(2)}) collective-permute-start(bf16[208,128]{1,0:T(8,128)(2,1)S(1)} %get-tuple-element.59), channel_id=1, source_target_pairs={{0,24},{2,26},{4,28},{6,30},{8,16},{10,18},{12,20},{14,22},{16,8},... | collective-permute-start | bytes 159752 | tf_op jit(solution)/shard_map/ppermute | solution.py:923
  94.8 1.9 %collective-permute-start.18 = (bf16[208,128]{1,0:T(8,128)(2,1)S(1)}, bf16[208,128]{1,0:T(8,128)(2,1)S(1)}, u32[]{:S(2)}, u32[]{:S(2)}) collective-permute-start(bf16[208,128]{1,0:T(8,128)(2,1)S(1)} %get-tuple-element.58), channel_id=1, source_target_pairs={{0,8},{2,10},{4,12},{6,14},{8,0},{10,2},{12,4},{14,6},{16,24},{18,... | collective-permute-start | bytes 159752 | tf_op jit(solution)/shard_map/ppermute | solution.py:923
  97.8 1.3 %copy.8 = f32[4,8,48,256]{3,2,1,0:T(8,128)} copy(f32[4,8,48,256]{3,2,0,1:T(8,128)S(1)} %convert_bitcast_fusion) | data formatting | bytes 3145728 | tf_op jit(solution)/shard_map/convert_element_type | solution.py:984
  99.1 1.3 %collective-permute-done.19 = bf16[208,128]{1,0:T(8,128)(2,1)S(1)} collective-permute-done((bf16[208,128]{1,0:T(8,128)(2,1)S(1)}, bf16[208,128]{1,0:T(8,128)(2,1)S(1)}, u32[]{:S(2)}, u32[]{:S(2)}) %collective-permute-start.19) | collective-permute-done | bytes 53280 | tf_op jit(solution)/shard_map/ppermute | solution.py:923
  (66 shorter events, 11.9 us)
Async XLA Ops:
  2.4 8.4 %collective-permute-start.2 = (bf16[208,128]{1,0:T(8,128)(2,1)S(1)}, bf16[208,128]{1,0:T(8,128)(2,1)S(1)}, u32[]{:S(2)}, u32[]{:S(2)}) collective-permute-start(bf16[208,128]{1,0:T(8,128)(2,1)S(1)} %get-tuple-element.65), channel_id=1, source_target_pairs={{0,24},{2,26},{4,28},{6,30},{8,16},{10,18},{12,20},{14,22},{16,8},... | collective-permute-start | bytes 159752 | tf_op jit(solution)/shard_map/ppermute | solution.py:923
  7.5 5.0 %collective-permute-start.1 = (bf16[208,128]{1,0:T(8,128)(2,1)S(1)}, bf16[208,128]{1,0:T(8,128)(2,1)S(1)}, u32[]{:S(2)}, u32[]{:S(2)}) collective-permute-start(bf16[208,128]{1,0:T(8,128)(2,1)S(1)} %get-tuple-element.65), channel_id=1, source_target_pairs={{0,16},{2,18},{4,20},{6,22},{8,24},{10,26},{12,28},{14,30},{16,0},... | collective-permute-start | bytes 159752 | tf_op jit(solution)/shard_map/ppermute | solution.py:923
  7.5 5.0 %collective-permute-start = (bf16[208,128]{1,0:T(8,128)(2,1)S(1)}, bf16[208,128]{1,0:T(8,128)(2,1)S(1)}, u32[]{:S(2)}, u32[]{:S(2)}) collective-permute-start(bf16[208,128]{1,0:T(8,128)(2,1)S(1)} %get-tuple-element.65), channel_id=1, source_target_pairs={{0,8},{2,10},{4,12},{6,14},{8,0},{10,2},{12,4},{14,6},{16,24},{18,... | collective-permute-start | bytes 159752 | tf_op jit(solution)/shard_map/ppermute | solution.py:923
  12.6 8.3 %collective-permute-start.3 = (bf16[4,208,128]{2,1,0:T(8,128)(2,1)S(1)}, bf16[4,208,128]{2,1,0:T(8,128)(2,1)S(1)}, u32[]{:S(2)}, u32[]{:S(2)}) collective-permute-start(bf16[4,208,128]{2,1,0:T(8,128)(2,1)S(1)} %pad_maximum_fusion.1.refs_0_), channel_id=1, source_target_pairs={{0,2},{2,0},{4,6},{6,4},{8,10},{10,8},{12,14},{14,12},{16,18},{18,... | collective-permute-start | bytes 638984 | tf_op jit(solution)/shard_map/ppermute | solution.py:923
  14.1 12.3 %collective-permute-start.4 = (bf16[4,208,128]{2,1,0:T(8,128)(2,1)S(1)}, bf16[4,208,128]{2,1,0:T(8,128)(2,1)S(1)}, u32[]{:S(2)}, u32[]{:S(2)}) collective-permute-start(bf16[4,208,128]{2,1,0:T(8,128)(2,1)S(1)} %pad_maximum_fusion.1.refs_0_), channel_id=1, source_target_pairs={{0,4},{2,6},{4,0},{6,2},{8,12},{10,14},{12,8},{14,10},{16,20},{18,... | collective-permute-start | bytes 638984 | tf_op jit(solution)/shard_map/ppermute | solution.py:923
  15.6 17.3 %collective-permute-start.5 = (bf16[4,208,128]{2,1,0:T(8,128)(2,1)S(1)}, bf16[4,208,128]{2,1,0:T(8,128)(2,1)S(1)}, u32[]{:S(2)}, u32[]{:S(2)}) collective-permute-start(bf16[4,208,128]{2,1,0:T(8,128)(2,1)S(1)} %pad_maximum_fusion.1.refs_0_), channel_id=1, source_target_pairs={{0,6},{2,4},{4,2},{6,0},{8,14},{10,12},{12,10},{14,8},{16,22},{18,... | collective-permute-start | bytes 638984 | tf_op jit(solution)/shard_map/ppermute | solution.py:923
  16.1 25.4 %all-to-all-start = ((bf16[8,3,2,4,16,256]{5,4,3,2,1,0:T(8,128)(2,1)}), bf16[8,3,2,4,16,256]{5,4,3,2,1,0:T(8,128)(2,1)}, u32[]{:S(2)}, u32[]{:S(2)}) async-start(bf16[8,3,2,4,16,256]{5,4,3,2,1,0:T(8,128)(2,1)} %cut.1), calls=%async_computation | async-start | bytes 3145728 | tf_op jit(solution)/shard_map/all_to_all | solution.py:916
  20.4 13.2 %collective-permute-start.6 = (bf16[4,208,128]{2,1,0:T(8,128)(2,1)S(1)}, bf16[4,208,128]{2,1,0:T(8,128)(2,1)S(1)}, u32[]{:S(2)}, u32[]{:S(2)}) collective-permute-start(bf16[4,208,128]{2,1,0:T(8,128)(2,1)S(1)} %pad_maximum_fusion.1.refs_0_), channel_id=1, source_target_pairs={{0,1},{1,0},{2,3},{3,2},{4,5},{5,4},{6,7},{7,6},{8,9},{9,8},{10,11... | collective-permute-start | bytes 638984 | tf_op jit(solution)/shard_map/ppermute | solution.py:926
  20.8 12.8 %collective-permute-start.7 = (bf16[4,208,128]{2,1,0:T(8,128)(2,1)S(1)}, bf16[4,208,128]{2,1,0:T(8,128)(2,1)S(1)}, u32[]{:S(2)}, u32[]{:S(2)}) collective-permute-start(bf16[4,208,128]{2,1,0:T(8,128)(2,1)S(1)} %collective-permute-done.3.refs_1_), channel_id=1, source_target_pairs={{0,1},{1,0},{2,3},{3,2},{4,5},{5,4},{6,7},{7,6},{8,9},{9,8},{10,11... | collective-permute-start | bytes 638984 | tf_op jit(solution)/shard_map/ppermute | solution.py:926
  26.4 7.2 %collective-permute-start.8 = (bf16[4,208,128]{2,1,0:T(8,128)(2,1)S(1)}, bf16[4,208,128]{2,1,0:T(8,128)(2,1)S(1)}, u32[]{:S(2)}, u32[]{:S(2)}) collective-permute-start(bf16[4,208,128]{2,1,0:T(8,128)(2,1)S(1)} %collective-permute-done.4.refs_2_), channel_id=1, source_target_pairs={{0,1},{1,0},{2,3},{3,2},{4,5},{5,4},{6,7},{7,6},{8,9},{9,8},{10,11... | collective-permute-start | bytes 638984 | tf_op jit(solution)/shard_map/ppermute | solution.py:926
  32.9 2.1 %collective-permute-start.9 = (bf16[4,208,128]{2,1,0:T(8,128)(2,1)S(1)}, bf16[4,208,128]{2,1,0:T(8,128)(2,1)}, u32[]{:S(2)}, u32[]{:S(2)}) collective-permute-start(bf16[4,208,128]{2,1,0:T(8,128)(2,1)S(1)} %collective-permute-done.5.refs_3_), channel_id=1, source_target_pairs={{0,1},{1,0},{2,3},{3,2},{4,5},{5,4},{6,7},{7,6},{8,9},{9,8},{10,11... | collective-permute-start | bytes 638984 | tf_op jit(solution)/shard_map/ppermute | solution.py:926
  55.8 4.4 %collective-permute-start.10 = (bf16[4,3,208,128]{3,2,1,0:T(8,128)(2,1)}, bf16[4,3,208,128]{3,2,1,0:T(8,128)(2,1)S(1)}, u32[]{:S(2)}, u32[]{:S(2)}) collective-permute-start(bf16[4,3,208,128]{3,2,1,0:T(8,128)(2,1)} %get-tuple-element.43), channel_id=1, source_target_pairs={{0,1},{1,0},{2,3},{3,2},{4,5},{5,4},{6,7},{7,6},{8,9},{9,8},{10,11... | collective-permute-start | bytes 1916936 | tf_op jit(solution)/shard_map/ppermute | solution.py:926
  56.0 17.5 %all-to-all-start.1 = ((bf16[8,4,48,256]{3,2,1,0:T(8,128)(2,1)}), bf16[8,4,48,256]{3,2,1,0:T(8,128)(2,1)S(1)}, u32[]{:S(2)}, u32[]{:S(2)}) async-start(bf16[8,4,48,256]{3,2,1,0:T(8,128)(2,1)} %bitcast.69), calls=%async_computation.1 | async-start | bytes 1572864 | tf_op jit(solution)/shard_map/all_to_all | solution.py:916
  62.2 16.6 %collective-permute-start.13 = (bf16[3,208,128]{2,1,0:T(8,128)(2,1)}, bf16[3,208,128]{2,1,0:T(8,128)(2,1)S(1)}, u32[]{:S(2)}, u32[]{:S(2)}) collective-permute-start(bf16[3,208,128]{2,1,0:T(8,128)(2,1)} %get-tuple-element.54), channel_id=1, source_target_pairs={{0,6},{2,4},{4,2},{6,0},{8,14},{10,12},{12,10},{14,8},{16,22},{18,... | collective-permute-start | bytes 479240 | tf_op jit(solution)/shard_map/ppermute | solution.py:923
  65.1 14.4 %collective-permute-start.12 = (bf16[3,208,128]{2,1,0:T(8,128)(2,1)}, bf16[3,208,128]{2,1,0:T(8,128)(2,1)}, u32[]{:S(2)}, u32[]{:S(2)}) collective-permute-start(bf16[3,208,128]{2,1,0:T(8,128)(2,1)} %get-tuple-element.55), channel_id=1, source_target_pairs={{0,4},{2,6},{4,0},{6,2},{8,12},{10,14},{12,8},{14,10},{16,20},{18,... | collective-permute-start | bytes 479240 | tf_op jit(solution)/shard_map/ppermute | solution.py:923
  65.7 13.8 %collective-permute-start.11 = (bf16[3,208,128]{2,1,0:T(8,128)(2,1)}, bf16[3,208,128]{2,1,0:T(8,128)(2,1)}, u32[]{:S(2)}, u32[]{:S(2)}) collective-permute-start(bf16[3,208,128]{2,1,0:T(8,128)(2,1)} %get-tuple-element.53), channel_id=1, source_target_pairs={{0,2},{2,0},{4,6},{6,4},{8,10},{10,8},{12,14},{14,12},{16,18},{18,... | collective-permute-start | bytes 479240 | tf_op jit(solution)/shard_map/ppermute | solution.py:923
  73.6 18.6 %all-to-all-start.2 = ((bf16[8,4,48,256]{3,2,1,0:T(8,128)(2,1)}), bf16[8,4,48,256]{3,2,1,0:T(8,128)(2,1)S(1)}, u32[]{:S(2)}, u32[]{:S(2)}) async-start(bf16[8,4,48,256]{3,2,1,0:T(8,128)(2,1)} %bitcast.68), calls=%async_computation.2 | async-start | bytes 1572864 | tf_op jit(solution)/shard_map/all_to_all | solution.py:916
  80.7 1.5 %collective-permute-start.14 = (bf16[4,1,208,128]{3,2,1,0:T(8,128)(2,1)S(1)}, bf16[4,1,208,128]{3,2,1,0:T(8,128)(2,1)S(1)}, u32[]{:S(2)}, u32[]{:S(2)}) collective-permute-start(bf16[4,1,208,128]{3,2,1,0:T(8,128)(2,1)S(1)} %copy-done.9), channel_id=1, source_target_pairs={{0,1},{1,0},{2,3},{3,2},{4,5},{5,4},{6,7},{7,6},{8,9},{9,8},{10,11... | collective-permute-start | bytes 638984 | tf_op jit(solution)/shard_map/ppermute | solution.py:926
  82.3 9.2 %collective-permute-start.17 = (bf16[1,208,128]{2,1,0:T(8,128)(2,1)S(1)}, bf16[1,208,128]{2,1,0:T(8,128)(2,1)S(1)}, u32[]{:S(2)}, u32[]{:S(2)}) collective-permute-start(bf16[1,208,128]{2,1,0:T(8,128)(2,1)S(1)} %get-tuple-element.62), channel_id=1, source_target_pairs={{0,6},{2,4},{4,2},{6,0},{8,14},{10,12},{12,10},{14,8},{16,22},{18,... | collective-permute-start | bytes 159752 | tf_op jit(solution)/shard_map/ppermute | solution.py:923
  84.6 7.5 %collective-permute-start.16 = (bf16[1,208,128]{2,1,0:T(8,128)(2,1)S(1)}, bf16[1,208,128]{2,1,0:T(8,128)(2,1)S(1)}, u32[]{:S(2)}, u32[]{:S(2)}) collective-permute-start(bf16[1,208,128]{2,1,0:T(8,128)(2,1)S(1)} %get-tuple-element.63), channel_id=1, source_target_pairs={{0,4},{2,6},{4,0},{6,2},{8,12},{10,14},{12,8},{14,10},{16,20},{18,... | collective-permute-start | bytes 159752 | tf_op jit(solution)/shard_map/ppermute | solution.py:923
  85.2 6.9 %collective-permute-start.15 = (bf16[1,208,128]{2,1,0:T(8,128)(2,1)S(1)}, bf16[1,208,128]{2,1,0:T(8,128)(2,1)S(1)}, u32[]{:S(2)}, u32[]{:S(2)}) collective-permute-start(bf16[1,208,128]{2,1,0:T(8,128)(2,1)S(1)} %get-tuple-element.61), channel_id=1, source_target_pairs={{0,2},{2,0},{4,6},{6,4},{8,10},{10,8},{12,14},{14,12},{16,18},{18,... | collective-permute-start | bytes 159752 | tf_op jit(solution)/shard_map/ppermute | solution.py:923
  92.2 6.9 %collective-permute-start.20 = (bf16[208,128]{1,0:T(8,128)(2,1)S(1)}, bf16[208,128]{1,0:T(8,128)(2,1)S(1)}, u32[]{:S(2)}, u32[]{:S(2)}) collective-permute-start(bf16[208,128]{1,0:T(8,128)(2,1)S(1)} %get-tuple-element.59), channel_id=1, source_target_pairs={{0,24},{2,26},{4,28},{6,30},{8,16},{10,18},{12,20},{14,22},{16,8},... | collective-permute-start | bytes 159752 | tf_op jit(solution)/shard_map/ppermute | solution.py:923
  94.8 5.6 %collective-permute-start.19 = (bf16[208,128]{1,0:T(8,128)(2,1)S(1)}, bf16[208,128]{1,0:T(8,128)(2,1)S(1)}, u32[]{:S(2)}, u32[]{:S(2)}) collective-permute-start(bf16[208,128]{1,0:T(8,128)(2,1)S(1)} %get-tuple-element.60), channel_id=1, source_target_pairs={{0,16},{2,18},{4,20},{6,22},{8,24},{10,26},{12,28},{14,30},{16,0},... | collective-permute-start | bytes 159752 | tf_op jit(solution)/shard_map/ppermute | solution.py:923
  94.8 5.5 %collective-permute-start.18 = (bf16[208,128]{1,0:T(8,128)(2,1)S(1)}, bf16[208,128]{1,0:T(8,128)(2,1)S(1)}, u32[]{:S(2)}, u32[]{:S(2)}) collective-permute-start(bf16[208,128]{1,0:T(8,128)(2,1)S(1)} %get-tuple-element.58), channel_id=1, source_target_pairs={{0,8},{2,10},{4,12},{6,14},{8,0},{10,2},{12,4},{14,6},{16,24},{18,... | collective-permute-start | bytes 159752 | tf_op jit(solution)/shard_map/ppermute | solution.py:923
  (10 other events, 55.2 us)
